TPU v7x, 32 devices: a whole 2x2x4 slice. The times are simulated.
32 devices in a mesh: dp: 2 (over y), expert: 16 (over z, x, core).
Axes of the slice: x: 2, y: 2, z: 4, core: 2. Of those that a mesh axis runs over, the one named last changes fastest.
Arguments:
- tokens: bfloat16 [2048, 4096], P('expert', 'dp'), may hold values from -6 to 6
- cotangent: bfloat16 [2048, 4096], P('expert', 'dp'), may hold values from -1.5 to 1.5
- router_probs: bfloat16 [2048, 8], P('expert'), may hold values from 0.049804688 to 1
- expert_ids: int32 [2048, 8], P('expert'), may hold values from 0 to 15, all different within a row; in each aligned block of 128 rows (0 to 127, 128 to 255, ...) at most 68 rows name the same one
- w_gate: bfloat16 [16, 768, 4096], P('expert', None, 'dp'), may hold values from -0.09375 to 0.09375
- w_up: bfloat16 [16, 768, 4096], P('expert', None, 'dp'), may hold values from -0.09375 to 0.09375
- w_down: bfloat16 [16, 768, 4096], P('expert', None, 'dp'), may hold values from -0.21875 to 0.21875
Outputs:
- token_grads: bfloat16 [2048, 4096], P('expert', 'dp')
- prob_grads: float32 [2048, 8], P('expert')
- gate_grads: bfloat16 [16, 768, 4096], P('expert', None, 'dp')
- up_grads: bfloat16 [16, 768, 4096], P('expert', None, 'dp')
- down_grads: bfloat16 [16, 768, 4096], P('expert', None, 'dp')
Inputs may be any that keep to these rules, and one draw needn't show every extreme that they name: `expert_ids`: each row names 8 different experts. Among the 128 tokens of one index of expert no expert is named more than 68 times, a bound that some block reaches.
All inputs are finite; a program needn't handle non-finite values.
Results may differ from a plain program's by a relative error of at most 0.02.
Values may be sent and summed in bfloat16 or wider, within the bound.
No kernel may reach another device: no remote copies, remote signals or barrier semaphores. Data moves between devices by JAX's collectives and lax.ppermute only.
A program may use at most 128 MiB of HBM per device.

v0:
```python
import jax
import jax.numpy as jnp
from jax import lax
from jax.sharding import PartitionSpec as P


def contract_last(left_matrix, right_matrix):
    return lax.dot_general(
        left_matrix, right_matrix, (((1,), (1,)), ((), ())), preferred_element_type=jnp.float32
    )


def contract_first(left_matrix, right_matrix):
    return lax.dot_general(
        left_matrix, right_matrix, (((0,), (0,)), ((), ())), preferred_element_type=jnp.float32
    )


def activations(gate_value, up_value, back_value, weights):
    sigmoid_gate = jax.nn.sigmoid(gate_value)
    silu_gate = gate_value * sigmoid_gate
    hidden = (silu_gate * up_value).astype(jnp.bfloat16)
    prob_local = jnp.sum(hidden.astype(jnp.float32) * back_value, axis=1)
    grad_back = weights[:, None] * back_value
    grad_gate = (
        grad_back * up_value * sigmoid_gate * (1.0 + gate_value * (1.0 - sigmoid_gate))
    ).astype(jnp.bfloat16)
    grad_up = (grad_back * silu_gate).astype(jnp.bfloat16)
    return (hidden, grad_gate, grad_up, prob_local)


def local(tokens, cotangent, router_probs, expert_ids, w_gate, w_up, w_down):
    experts = lax.axis_size("expert")
    local_tokens, top_count = expert_ids.shape
    row_count = local_tokens * top_count
    slot_count = min(local_tokens, max(2, (row_count + experts - 1) // experts * 17 // 16))
    features = tokens.shape[1]
    flat_ids = expert_ids.reshape(-1)
    hit_table = (flat_ids[:, None] == jnp.arange(experts, dtype=jnp.int32)[None, :]).astype(
        jnp.int32
    )
    slot_ranks = jnp.sum(jnp.cumsum(hit_table, axis=0) * hit_table, axis=1) - 1
    slot_places = flat_ids * slot_count + slot_ranks
    slot_table = jnp.full((experts * slot_count,), row_count, jnp.int32)
    slot_table = slot_table.at[slot_places].set(jnp.arange(row_count, dtype=jnp.int32))
    filled = slot_table < row_count
    sources = jnp.minimum(slot_table, row_count - 1)
    owners = sources // top_count
    send_probs = jnp.where(
        filled, router_probs.reshape(-1)[sources], jnp.zeros((), router_probs.dtype)
    )
    send_probs = send_probs.reshape(experts, slot_count)

    def pack_rows(source):
        picked = jnp.where(filled[:, None], source[owners], jnp.zeros((), source.dtype))
        return picked.reshape(experts, slot_count, source.shape[1])

    recv_in, recv_grad, recv_probs = (
        lax.all_to_all(pack_rows(tokens), "expert", split_axis=0, concat_axis=0, tiled=True),
        lax.all_to_all(pack_rows(cotangent), "expert", split_axis=0, concat_axis=0, tiled=True),
        lax.all_to_all(send_probs, "expert", split_axis=0, concat_axis=0, tiled=True),
    )
    inputs = recv_in.reshape(experts * slot_count, features)
    grads_in = recv_grad.reshape(experts * slot_count, features)
    weights = recv_probs.reshape(-1).astype(jnp.float32)
    weight_gate = w_gate[0]
    weight_up = w_up[0]
    weight_down = w_down[0]
    gate_part = contract_last(inputs, weight_gate)
    up_part = contract_last(inputs, weight_up)
    back_part = contract_last(grads_in, weight_down)
    gate_value, up_value, back_value = (
        lax.psum(gate_part.astype(jnp.bfloat16), "dp").astype(jnp.float32),
        lax.psum(up_part.astype(jnp.bfloat16), "dp").astype(jnp.float32),
        lax.psum(back_part.astype(jnp.bfloat16), "dp").astype(jnp.float32),
    )
    hidden, grad_gate, grad_up, prob_value = activations(gate_value, up_value, back_value, weights)
    scaled = (weights[:, None] * grads_in).astype(jnp.bfloat16)
    row_term = jnp.dot(grad_gate, weight_gate, preferred_element_type=jnp.float32)
    row_term = (row_term + jnp.dot(grad_up, weight_up, preferred_element_type=jnp.float32)).astype(
        jnp.bfloat16
    )
    gate_grad = contract_first(grad_gate, inputs).astype(jnp.bfloat16)
    up_grad = contract_first(grad_up, inputs).astype(jnp.bfloat16)
    down_grad = contract_first(hidden, scaled).astype(jnp.bfloat16)
    back_terms, back_probs = (
        lax.all_to_all(
            row_term.reshape(experts, slot_count, features),
            "expert",
            split_axis=0,
            concat_axis=0,
            tiled=True,
        ),
        lax.all_to_all(
            prob_value.astype(jnp.bfloat16).reshape(experts, slot_count),
            "expert",
            split_axis=0,
            concat_axis=0,
            tiled=True,
        ),
    )
    returned = back_terms.reshape(experts * slot_count, features)[slot_places].astype(jnp.float32)
    token_sum = jnp.sum(returned.reshape(local_tokens, top_count, features), axis=1)
    prob_grads = (
        back_probs.reshape(-1)[slot_places].astype(jnp.float32).reshape(local_tokens, top_count)
    )
    return (
        token_sum.astype(jnp.bfloat16),
        prob_grads,
        gate_grad[None],
        up_grad[None],
        down_grad[None],
    )


def solution(mesh):
    return jax.shard_map(
        local,
        mesh=mesh,
        in_specs=(
            P("expert", "dp"),
            P("expert", "dp"),
            P("expert", None),
            P("expert", None),
            P("expert", None, "dp"),
            P("expert", None, "dp"),
            P("expert", None, "dp"),
        ),
        out_specs=(
            P("expert", "dp"),
            P("expert", None),
            P("expert", None, "dp"),
            P("expert", None, "dp"),
            P("expert", None, "dp"),
        ),
        check_vma=False,
    )
```

profile of v0, /device:TPU:11, one launch (start us, length us, event | category | flops | bytes accessed | tf_op | source)
XLA Modules:
  0.0 603.3 jit_solution(11430262725632702686)
XLA Ops:
  19.6 6.9 %gather_fusion = bf16[1088]{0:T(1024)(128)(2,1)S(1)} fusion(bf16[1024]{0:T(1024)(128)(2,1)S(1)} %reshape.129, s32[2048]{0:T(1024)S(1)} %get-tuple-element.25), kind=kCustom, calls=%fused_computation | custom fusion | bytes 8704 | tf_op jit(solution)/shard_map/gather | solution.py:50
  26.6 11.7 %gather_fusion.2 = bf16[1088,2048]{1,0:T(8,128)(2,1)} fusion(bf16[128,2048]{1,0:T(8,128)(2,1)} %param.7, s32[2048]{0:T(1024)S(1)} %get-tuple-element.24), kind=kCustom, calls=%fused_computation.2 | custom fusion | bytes 8917248 | tf_op jit(solution)/shard_map/gather | solution.py:55
  38.3 7.1 %gather.25 = bf16[16,68,2048]{2,1,0:T(8,128)(2,1)} reshape(bf16[1088,2048]{1,0:T(8,128)(2,1)} %gather_fusion.2) | data formatting | bytes 8912896 | tf_op jit(solution)/shard_map/gather | solution.py:55
  45.4 11.7 %gather_fusion.1 = bf16[1088,2048]{1,0:T(8,128)(2,1)} fusion(bf16[128,2048]{1,0:T(8,128)(2,1)} %param.8, s32[2048]{0:T(1024)S(1)} %get-tuple-element.24), kind=kCustom, calls=%fused_computation.1 | custom fusion | bytes 8917248 | tf_op jit(solution)/shard_map/gather | solution.py:55
  57.1 7.0 %gather.23 = bf16[16,68,2048]{2,1,0:T(8,128)(2,1)} reshape(bf16[1088,2048]{1,0:T(8,128)(2,1)} %gather_fusion.1) | data formatting | bytes 8912896 | tf_op jit(solution)/shard_map/gather | solution.py:55
  69.7 109.9 %all_to_all.31 = bf16[16,68,2048]{2,1,0:T(8,128)(2,1)} all-to-all(bf16[16,68,2048]{2,1,0:T(8,128)(2,1)S(1)} %get-tuple-element.22), channel_id=1, replica_groups=mesh['dp'=2,'expert'=16] {'expert'}, dimensions={0} | all-to-all | bytes 8912896 | tf_op jit(solution)/shard_map/all_to_all | solution.py:59
  185.2 7.1 %reshape.131 = bf16[1088,2048]{1,0:T(8,128)(2,1)} reshape(bf16[16,68,2048]{2,1,0:T(8,128)(2,1)} %all_to_all.31) | data formatting | bytes 8912896 | tf_op jit(solution)/shard_map/reshape | solution.py:63
  192.3 7.3 %convolution_convert_fusion.2 = bf16[1088,768]{1,0:T(8,128)(2,1)} fusion(bf16[1088,2048]{1,0:T(8,128)(2,1)} %reshape.131, bf16[1,768,2048]{2,1,0:T(8,128)(2,1)S(1)} %copy-done), kind=kOutput, calls=%fused_computation.25 | convolution fusion | flops 3423387648 | bytes 9273344 | tf_op jit(solution)/shard_map/dot_general | solution.py:8
  204.3 84.4 %all-to-all-done.1 = bf16[16,68,2048]{2,1,0:T(8,128)(2,1)} async-done(((bf16[16,68,2048]{2,1,0:T(8,128)(2,1)}), bf16[16,68,2048]{2,1,0:T(8,128)(2,1)}, u32[]{:S(2)}, u32[]{:S(2)}) %all-to-all-start.1) | async-done | bytes 4456480 | tf_op jit(solution)/shard_map/all_to_all | solution.py:60
  288.7 7.1 %reshape.130 = bf16[1088,2048]{1,0:T(8,128)(2,1)} reshape(bf16[16,68,2048]{2,1,0:T(8,128)(2,1)} %all-to-all-done.1) | data formatting | bytes 8912896 | tf_op jit(solution)/shard_map/reshape | solution.py:64
  295.8 8.1 %convolution_convert_fusion.4 = bf16[1088,768]{1,0:T(8,128)(2,1)} fusion(bf16[1088,2048]{1,0:T(8,128)(2,1)} %reshape.130, bf16[1,768,2048]{2,1,0:T(8,128)(2,1)} %param.13), kind=kOutput, calls=%fused_computation.27 | convolution fusion | flops 3423387648 | bytes 9273344 | tf_op jit(solution)/shard_map/dot_general | solution.py:8
  304.0 8.5 %all_to_all.32 = bf16[16,1,68]{2,1,0:T(2,128)(2,1)S(1)} all-to-all(bf16[16,1,68]{2,1,0:T(2,128)(2,1)S(1)} %all_to_all.25), channel_id=1, replica_groups=mesh['dp'=2,'expert'=16] {'expert'}, dimensions={0} | all-to-all | bytes 4352 | tf_op jit(solution)/shard_map/all_to_all | solution.py:61
  312.7 117.2 %all-reduce.3.cloned.1.call-done = (bf16[1088,768]{1,0:T(8,128)(2,1)}, bf16[1088,768]{1,0:T(8,128)(2,1)}, bf16[1088,768]{1,0:T(8,128)(2,1)}) async-done(((bf16[1088,768]{1,0:T(8,128)(2,1)}, bf16[1088,768]{1,0:T(8,128)(2,1)}, bf16[1088,768]{1,0:T(8,128)(2,1)}), (bf16[1088,768]{1,0:T(8,128)(2,1)}, bf16[1088,768]{1,0:T(8,128)(2,1)}, bf16[1088,768]{1,0:T(8,128)(2,1)})) %all-reduce.3.cloned.1.call-update) | async-done | bytes 5013520 | tf_op jit(solution)/shard_map/psum | solution.py:75
  434.3 6.4 %all-to-all-start.4 = ((bf16[16,1,68]{2,1,0:T(2,128)(2,1)}), bf16[16,1,68]{2,1,0:T(2,128)(2,1)S(1)}, u32[]{:S(2)}, u32[]{:S(2)}) async-start(bf16[16,1,68]{2,1,0:T(2,128)(2,1)} %convert_element_type.112), calls=%async_computation.4 | async-start | bytes 16384 | tf_op jit(solution)/shard_map/all_to_all | solution.py:94
  440.7 6.9 %fusion.15 = f32[1088,2048]{1,0:T(8,128)S(1)} fusion(bf16[1,768,2048]{2,1,0:T(8,128)(2,1)S(1)} %copy-done, bf16[1088,768]{1,0:T(8,128)(2,1)} %get-tuple-element.16, bf16[1088,768]{1,0:T(8,128)(2,1)} %get-tuple-element.15, bf16[1088,768]{1,0:T(8,128)(2,1)} %get-tuple-element.17, f32[1088]{0:T(1024)S(1)} %reshape.135), kind=kOutput, calls=%fused_computation.38 | convolution fusion | flops 3434250240 | bytes 17076480 | tf_op jit(solution)/shard_map/dot_general | solution.py:79
  453.9 7.1 %reshape.132 = bf16[16,68,2048]{2,1,0:T(8,128)(2,1)} reshape(bf16[1088,2048]{1,0:T(8,128)(2,1)} %fusion) | data formatting | bytes 8912896 | tf_op jit(solution)/shard_map/reshape | solution.py:88
  460.9 6.5 %all-to-all-start.3 = ((bf16[16,68,2048]{2,1,0:T(8,128)(2,1)}), bf16[16,68,2048]{2,1,0:T(8,128)(2,1)}, u32[]{:S(2)}, u32[]{:S(2)}) async-start(bf16[16,68,2048]{2,1,0:T(8,128)(2,1)} %reshape.132), calls=%async_computation.3 | async-start | bytes 9437184 | tf_op jit(solution)/shard_map/all_to_all | solution.py:87
  467.5 9.4 %fusion.22 = bf16[1,768,2048]{2,1,0:T(8,128)(2,1)} fusion(bf16[1088,2048]{1,0:T(8,128)(2,1)} %reshape.131, bf16[1088,768]{1,0:T(8,128)(2,1)S(1)} %copy-done.4, f32[1088]{0:T(1024)S(1)} %reshape.135, bf16[1088,768]{1,0:T(8,128)(2,1)} %get-tuple-element.17), kind=kOutput, calls=%fused_computation.45 | convolution fusion | flops 3431645184 | bytes 10948864 | tf_op jit(solution)/shard_map/dot_general | solution.py:14
  477.0 6.7 %fusion.23 = bf16[1,768,2048]{2,1,0:T(8,128)(2,1)} fusion(bf16[1088,2048]{1,0:T(8,128)(2,1)S(1)} %bitcast.46, f32[1088]{0:T(1024)S(1)} %reshape.135, bf16[1088,768]{1,0:T(8,128)(2,1)S(1)} %copy-done.5, bf16[1088,768]{1,0:T(8,128)(2,1)S(1)} %copy-done.7), kind=kOutput, calls=%fused_computation.46 | convolution fusion | flops 3437494272 | bytes 10948864 | tf_op jit(solution)/shard_map/dot_general | solution.py:14
  483.7 6.5 %fusion.21 = bf16[1,768,2048]{2,1,0:T(8,128)(2,1)} fusion(bf16[1088,2048]{1,0:T(8,128)(2,1)S(1)} %bitcast.44, bf16[1088,768]{1,0:T(8,128)(2,1)S(1)} %copy-done.5, bf16[1088,768]{1,0:T(8,128)(2,1)S(1)} %copy-done.4, bf16[1088,768]{1,0:T(8,128)(2,1)S(1)} %copy-done.7, f32[1088]{0:T(1024)S(1)} %reshape.135), kind=kOutput, calls=%fused_computation.44 | convolution fusion | flops 3435823104 | bytes 12620032 | tf_op jit(solution)/shard_map/dot_general | solution.py:14
  490.3 6.8 %gather_fusion.4 = bf16[1024]{0:T(1024)(128)(2,1)S(1)} fusion(bf16[1088]{0:T(1024)(128)(2,1)S(1)} %reshape.134, s32[1024]{0:T(1024)S(1)} %broadcast_clamp_fusion), kind=kCustom, calls=%fused_computation.4 | custom fusion | bytes 8192 | tf_op jit(solution)/shard_map/gather | solution.py:105
  497.9 73.1 %all-to-all-done.3 = bf16[16,68,2048]{2,1,0:T(8,128)(2,1)} async-done(((bf16[16,68,2048]{2,1,0:T(8,128)(2,1)}), bf16[16,68,2048]{2,1,0:T(8,128)(2,1)}, u32[]{:S(2)}, u32[]{:S(2)}) %all-to-all-start.3) | async-done | bytes 4456480 | tf_op jit(solution)/shard_map/all_to_all | solution.py:87
  571.0 7.1 %reshape.133 = bf16[1088,2048]{1,0:T(8,128)(2,1)} reshape(bf16[16,68,2048]{2,1,0:T(8,128)(2,1)} %all-to-all-done.3) | data formatting | bytes 8912896 | tf_op jit(solution)/shard_map/reshape | solution.py:102
  578.1 12.1 %gather_fusion.3 = bf16[1024,2048]{1,0:T(8,128)(2,1)} fusion(bf16[1088,2048]{1,0:T(8,128)(2,1)} %reshape.133, s32[1024]{0:T(1024)S(1)} %broadcast_clamp_fusion), kind=kCustom, calls=%fused_computation.3 | custom fusion | bytes 8392704 | tf_op jit(solution)/shard_map/gather | solution.py:102
  (73 shorter events, 46.1 us)
Async XLA Ops:
  7.2 185.1 %copy-start = (bf16[1,768,2048]{2,1,0:T(8,128)(2,1)S(1)}, bf16[1,768,2048]{2,1,0:T(8,128)(2,1)}, u32[]{:S(2)}) copy-start(bf16[1,768,2048]{2,1,0:T(8,128)(2,1)} %param.11) | copy-start | bytes 9437188
  179.6 109.1 %all-to-all-start.1 = ((bf16[16,68,2048]{2,1,0:T(8,128)(2,1)}), bf16[16,68,2048]{2,1,0:T(8,128)(2,1)}, u32[]{:S(2)}, u32[]{:S(2)}) async-start(bf16[16,68,2048]{2,1,0:T(8,128)(2,1)} %get-tuple-element.23), calls=%async_computation.1 | async-start | bytes 9437184 | tf_op jit(solution)/shard_map/all_to_all | solution.py:60
  185.0 244.8 %all-reduce.3.cloned.1.call-start = ((), (), s32[]{:S(2)}) async-start(), calls=%async_computation.5 | async-start | bytes 10027008 | tf_op jit(solution)/shard_map/psum | solution.py:75
  192.3 7.3 %copy-start.2 = (bf16[1088,2048]{1,0:T(8,128)(2,1)S(1)}, bf16[1088,2048]{1,0:T(8,128)(2,1)}, u32[]{:S(2)}) copy-start(bf16[1088,2048]{1,0:T(8,128)(2,1)} %reshape.131) | copy-start | bytes 13369348
  192.3 7.3 %copy-start.8 = (bf16[1,768,2048]{2,1,0:T(8,128)(2,1)S(1)}, bf16[1,768,2048]{2,1,0:T(8,128)(2,1)}, u32[]{:S(2)}) copy-start(bf16[1,768,2048]{2,1,0:T(8,128)(2,1)} %param.12) | copy-start | bytes 9437188
  434.3 26.6 %all-to-all-start.4 = ((bf16[16,1,68]{2,1,0:T(2,128)(2,1)}), bf16[16,1,68]{2,1,0:T(2,128)(2,1)S(1)}, u32[]{:S(2)}, u32[]{:S(2)}) async-start(bf16[16,1,68]{2,1,0:T(2,128)(2,1)} %convert_element_type.112), calls=%async_computation.4 | async-start | bytes 16384 | tf_op jit(solution)/shard_map/all_to_all | solution.py:94
  440.6 7.0 %copy-start.3 = (bf16[1088,768]{1,0:T(8,128)(2,1)S(1)}, bf16[1088,768]{1,0:T(8,128)(2,1)}, u32[]{:S(2)}) copy-start(bf16[1088,768]{1,0:T(8,128)(2,1)} %get-tuple-element.15) | copy-start | bytes 5013508
  440.7 7.0 %copy-start.6 = (bf16[1088,768]{1,0:T(8,128)(2,1)S(1)}, bf16[1088,768]{1,0:T(8,128)(2,1)}, u32[]{:S(2)}) copy-start(bf16[1088,768]{1,0:T(8,128)(2,1)} %get-tuple-element.17) | copy-start | bytes 5013508
  440.7 7.0 %copy-start.9 = (bf16[1,768,2048]{2,1,0:T(8,128)(2,1)S(1)}, bf16[1,768,2048]{2,1,0:T(8,128)(2,1)}, u32[]{:S(2)}) copy-start(bf16[1,768,2048]{2,1,0:T(8,128)(2,1)} %param.12) | copy-start | bytes 9437188
  460.9 6.5 %copy-start.4 = (bf16[1088,768]{1,0:T(8,128)(2,1)S(1)}, bf16[1088,768]{1,0:T(8,128)(2,1)}, u32[]{:S(2)}) copy-start(bf16[1088,768]{1,0:T(8,128)(2,1)} %get-tuple-element.15) | copy-start | bytes 5013508
  460.9 16.0 %slice-start.2 = ((s8[4456448]{0:T(1024)(128)(4,1)}), s8[262144]{0:T(1024)(128)(4,1)S(1)}, s32[]{:S(2)}) async-start(s8[4456448]{0:T(1024)(128)(4,1)} %bitcast.45), calls=%async_computation.8 | async-start | bytes 524288
  460.9 110.1 %all-to-all-start.3 = ((bf16[16,68,2048]{2,1,0:T(8,128)(2,1)}), bf16[16,68,2048]{2,1,0:T(8,128)(2,1)}, u32[]{:S(2)}, u32[]{:S(2)}) async-start(bf16[16,68,2048]{2,1,0:T(8,128)(2,1)} %reshape.132), calls=%async_computation.3 | async-start | bytes 9437184 | tf_op jit(solution)/shard_map/all_to_all | solution.py:87
  467.5 9.5 %slice-start.3 = ((s8[4456448]{0:T(1024)(128)(4,1)}), s8[4194304]{0:T(1024)(128)(4,1)S(1)}, s32[]{:S(2)}) async-start(s8[4456448]{0:T(1024)(128)(4,1)} %bitcast.45), calls=%async_computation.9 | async-start | bytes 8388608
  467.5 9.5 %copy-start.5 = (bf16[1088,768]{1,0:T(8,128)(2,1)S(1)}, bf16[1088,768]{1,0:T(8,128)(2,1)}, u32[]{:S(2)}) copy-start(bf16[1088,768]{1,0:T(8,128)(2,1)} %get-tuple-element.16) | copy-start | bytes 5013508
  467.5 9.5 %copy-start.7 = (bf16[1088,768]{1,0:T(8,128)(2,1)S(1)}, bf16[1088,768]{1,0:T(8,128)(2,1)}, u32[]{:S(2)}) copy-start(bf16[1088,768]{1,0:T(8,128)(2,1)} %get-tuple-element.17) | copy-start | bytes 5013508
  467.5 16.2 %slice-start = ((s8[4456448]{0:T(1024)(128)(4,1)}), s8[4194304]{0:T(1024)(128)(4,1)S(1)}, s32[]{:S(2)}) async-start(s8[4456448]{0:T(1024)(128)(4,1)} %bitcast.43), calls=%async_computation.6 | async-start | bytes 8388608
  477.0 6.7 %slice-start.1 = ((s8[4456448]{0:T(1024)(128)(4,1)}), s8[262144]{0:T(1024)(128)(4,1)S(1)}, s32[]{:S(2)}) async-start(s8[4456448]{0:T(1024)(128)(4,1)} %bitcast.43), calls=%async_computation.7 | async-start | bytes 524288
  578.1 18.0 %copy-start.1 = (bf16[1,768,2048]{2,1,0:T(8,128)(2,1)S(1)}, bf16[1,768,2048]{2,1,0:T(8,128)(2,1)}, u32[]{:S(2)}) copy-start(bf16[1,768,2048]{2,1,0:T(8,128)(2,1)} %param.11) | copy-start | bytes 9437188
Sparse Core Ops, SparseCore 0:
  304.0 125.7 all-reduce.2
where the time goes:
time: 614 us; the launch traced here: 603 us
  waiting for transfers between devices  275 us (45%)
  blocking collectives  118 us (19%)
  local copies, waits for them, and re-layouts  100 us (16%)
  matrix products  55.9 us (9%)
  other arithmetic  20.8 us (3%)
  starting transfers between devices  18.4 us (3%)
  between operations  14.8 us (2%)
    psum x1, waiting for transfers between devices, local(): lax.psum(back_part.astype(jnp.bfloat16), 'dp').astype(jnp.float32)  117 us
    all_to_all x1, blocking collectives, local(): lax.all_to_all(pack_rows(tokens), 'expert', split_axis=0, concat_axis=0,...  110 us
    all_to_all x1, waiting for transfers between devices, local(): lax.all_to_all(pack_rows(cotangent), 'expert', split_axis=0, concat_axis=...  84.4 us
    all_to_all x1, waiting for transfers between devices, local(): lax.all_to_all(row_term.reshape(experts, slot_count, features), 'expert',...  73.1 us
    gather x4, local copies, waits for them, and re-layouts, pack_rows(): source[owners]  37.5 us
    dot_general x3, matrix products, contract_first(): lax.dot_general(left_matrix, right_matrix, (((0,), (0,)), ((), ())), pref...  22.6 us
    dot_general x3, matrix products, contract_last(): lax.dot_general(left_matrix, right_matrix, (((1,), (1,)), ((), ())), pref...  20.1 us
  transfers between devices with their start and end apart: 4, of which 3 were waited for; matrix products, arithmetic and copies ran while one was open for 12% of the time, Pallas kernels for 0%

commit v1 on v0

--- a/solution.py
+++ b/solution.py
@@ -1,7 +1,16 @@
+import functools
+
 import jax
 import jax.numpy as jnp
 from jax import lax
+from jax.experimental import pallas as pl
+from jax.experimental.pallas import tpu as pltpu
 from jax.sharding import PartitionSpec as P
+
+F32 = jnp.float32
+BF16 = jnp.bfloat16
+LANES = 128
+VMEM = 56 * 1024 * 1024
 
 
 def contract_last(left_matrix, right_matrix):
@@ -20,8 +29,8 @@
     sigmoid_gate = jax.nn.sigmoid(gate_value)
     silu_gate = gate_value * sigmoid_gate
     hidden = (silu_gate * up_value).astype(jnp.bfloat16)
-    prob_local = jnp.sum(hidden.astype(jnp.float32) * back_value, axis=1)
-    grad_back = weights[:, None] * back_value
+    prob_local = jnp.sum(hidden.astype(jnp.float32) * back_value, axis=1, keepdims=True)
+    grad_back = weights * back_value
     grad_gate = (
         grad_back * up_value * sigmoid_gate * (1.0 + gate_value * (1.0 - sigmoid_gate))
     ).astype(jnp.bfloat16)
@@ -29,7 +38,7 @@
     return (hidden, grad_gate, grad_up, prob_local)
 
 
-def local(tokens, cotangent, router_probs, expert_ids, w_gate, w_up, w_down):
+def local_general(tokens, cotangent, router_probs, expert_ids, w_gate, w_up, w_down):
     experts = lax.axis_size("expert")
     local_tokens, top_count = expert_ids.shape
     row_count = local_tokens * top_count
@@ -55,10 +64,13 @@
         picked = jnp.where(filled[:, None], source[owners], jnp.zeros((), source.dtype))
         return picked.reshape(experts, slot_count, source.shape[1])
 
+    exchange = functools.partial(
+        lax.all_to_all, axis_name="expert", split_axis=0, concat_axis=0, tiled=True
+    )
     recv_in, recv_grad, recv_probs = (
-        lax.all_to_all(pack_rows(tokens), "expert", split_axis=0, concat_axis=0, tiled=True),
-        lax.all_to_all(pack_rows(cotangent), "expert", split_axis=0, concat_axis=0, tiled=True),
-        lax.all_to_all(send_probs, "expert", split_axis=0, concat_axis=0, tiled=True),
+        exchange(pack_rows(tokens)),
+        exchange(pack_rows(cotangent)),
+        exchange(send_probs),
     )
     inputs = recv_in.reshape(experts * slot_count, features)
     grads_in = recv_grad.reshape(experts * slot_count, features)
@@ -74,7 +86,9 @@
         lax.psum(up_part.astype(jnp.bfloat16), "dp").astype(jnp.float32),
         lax.psum(back_part.astype(jnp.bfloat16), "dp").astype(jnp.float32),
     )
-    hidden, grad_gate, grad_up, prob_value = activations(gate_value, up_value, back_value, weights)
+    hidden, grad_gate, grad_up, prob_value = activations(
+        gate_value, up_value, back_value, weights[:, None]
+    )
     scaled = (weights[:, None] * grads_in).astype(jnp.bfloat16)
     row_term = jnp.dot(grad_gate, weight_gate, preferred_element_type=jnp.float32)
     row_term = (row_term + jnp.dot(grad_up, weight_up, preferred_element_type=jnp.float32)).astype(
@@ -83,22 +97,8 @@
     gate_grad = contract_first(grad_gate, inputs).astype(jnp.bfloat16)
     up_grad = contract_first(grad_up, inputs).astype(jnp.bfloat16)
     down_grad = contract_first(hidden, scaled).astype(jnp.bfloat16)
-    back_terms, back_probs = (
-        lax.all_to_all(
-            row_term.reshape(experts, slot_count, features),
-            "expert",
-            split_axis=0,
-            concat_axis=0,
-            tiled=True,
-        ),
-        lax.all_to_all(
-            prob_value.astype(jnp.bfloat16).reshape(experts, slot_count),
-            "expert",
-            split_axis=0,
-            concat_axis=0,
-            tiled=True,
-        ),
-    )
+    back_terms = exchange(row_term.reshape(experts, slot_count, features))
+    back_probs = exchange(prob_value.astype(jnp.bfloat16).reshape(experts, slot_count))
     returned = back_terms.reshape(experts * slot_count, features)[slot_places].astype(jnp.float32)
     token_sum = jnp.sum(returned.reshape(local_tokens, top_count, features), axis=1)
     prob_grads = (
@@ -113,9 +113,287 @@
     )
 
 
+def pack_kernel(tokens, cotangent, probs, ids, out):
+    rows, width = tokens.shape
+    out[:, :width] = tokens[...]
+    out[:, width : 2 * width] = cotangent[...]
+    lane = lax.broadcasted_iota(jnp.int32, (rows, LANES), 1)
+    routing = jnp.full((rows, LANES), -1.0, F32)
+    weights = probs[...].astype(F32)
+    for k in range(ids.shape[1]):
+        routing = jnp.where(lane == ids[:, k : k + 1], weights[:, k : k + 1], routing)
+    out[:, 2 * width :] = routing.astype(BF16)
+
+
+def pack(tokens, cotangent, probs, ids):
+    rows, width = tokens.shape
+    return pl.pallas_call(
+        pack_kernel,
+        out_shape=jax.ShapeDtypeStruct((rows, 2 * width + LANES), BF16),
+        compiler_params=pltpu.CompilerParams(vmem_limit_bytes=VMEM),
+        cost_estimate=pl.CostEstimate(flops=0, bytes_accessed=8 * rows * width, transcendentals=0),
+        name="pack",
+    )(tokens, cotangent, probs, ids)
+
+
+def front_kernel(slots, expert, *refs):
+    token_refs, grad_refs, route_refs = refs[0:4], refs[4:8], refs[8:12]
+    w_gate, w_up, w_down = refs[12:15]
+    inputs, scaled, part, spread, weights = refs[15:20]
+    acc, pick = refs[20:22]
+    step = pl.program_id(0)
+    block = token_refs[0].shape[0]
+    rows = pick.shape[0]
+    units = w_gate.shape[0]
+
+    @pl.when(step == 0)
+    def _():
+        lane = lax.broadcasted_iota(jnp.int32, (block, LANES), 1)
+        tri = (
+            lax.broadcasted_iota(jnp.int32, (block, block), 1)
+            <= lax.broadcasted_iota(jnp.int32, (block, block), 0)
+        ).astype(BF16)
+        total = jnp.zeros((rows, LANES), F32)
+        for b in range(4):
+            routing = route_refs[b][...].astype(F32)
+            prob = jnp.sum(jnp.where(lane == expert[0], routing, 0.0), axis=1, keepdims=True)
+            chosen = jnp.broadcast_to(prob >= 0.0, (block, LANES))
+            count = jnp.dot(tri, chosen.astype(BF16), preferred_element_type=F32)
+            slot = jnp.where(chosen, count + (slots * b - 1.0), -1.0)
+            spread[pl.ds(b * block, block), :] = (
+                lax.broadcasted_iota(jnp.int32, (block, rows), 1) == slot[:, :1].astype(jnp.int32)
+            ).astype(BF16)
+            slot_row = slot.T[:1, :].astype(jnp.int32)
+            picked = (lax.broadcasted_iota(jnp.int32, (rows, block), 0) == slot_row).astype(BF16)
+            pick[:, pl.ds(b * block, block)] = picked
+            prob = jnp.broadcast_to(jnp.maximum(prob, 0.0), (block, LANES)).astype(BF16)
+            total = total + jnp.dot(picked, prob, preferred_element_type=F32)
+        weights[...] = total
+        acc[...] = jnp.zeros(acc.shape, F32)
+
+    def gather(block_refs):
+        stacked = jnp.concatenate([r[...] for r in block_refs], axis=0)
+        return jnp.dot(pick[...], stacked, preferred_element_type=F32).astype(BF16)
+
+    rows_in = gather(token_refs)
+    inputs[...] = rows_in
+    acc[:, 0:units] += contract_last(rows_in, w_gate[...])
+    acc[:, units : 2 * units] += contract_last(rows_in, w_up[...])
+    grads = gather(grad_refs)
+    scaled[...] = (weights[:, :1] * grads.astype(F32)).astype(BF16)
+    acc[:, 2 * units :] += contract_last(grads, w_down[...])
+
+    @pl.when(step == pl.num_programs(0) - 1)
+    def _():
+        part[...] = acc[...].astype(BF16)
+
+
+def front(blocks, expert, w_gate, w_up, w_down, slots):
+    block = blocks[0].shape[0]
+    units, width = w_gate.shape
+    tile = 512
+    steps = width // tile
+    rows = 4 * slots
+    weight_spec = pl.BlockSpec((units, tile), lambda k, e: (0, k))
+    whole = lambda shape: pl.BlockSpec(shape, lambda k, e: (0, 0))
+    return pl.pallas_call(
+        functools.partial(front_kernel, slots),
+        grid_spec=pltpu.PrefetchScalarGridSpec(
+            num_scalar_prefetch=1,
+            grid=(steps,),
+            in_specs=[pl.BlockSpec((block, tile), lambda k, e: (0, k))] * 4
+            + [pl.BlockSpec((block, tile), lambda k, e: (0, k + steps))] * 4
+            + [pl.BlockSpec((block, LANES), lambda k, e: (0, 2 * width // LANES))] * 4
+            + [weight_spec] * 3,
+            out_specs=[
+                pl.BlockSpec((rows, tile), lambda k, e: (0, k)),
+                pl.BlockSpec((rows, tile), lambda k, e: (0, k)),
+                whole((rows, 3 * units)),
+                whole((4 * block, rows)),
+                whole((rows, LANES)),
+            ],
+            scratch_shapes=[
+                pltpu.VMEM((rows, 3 * units), F32),
+                pltpu.VMEM((rows, 4 * block), BF16),
+            ],
+        ),
+        out_shape=[
+            jax.ShapeDtypeStruct((rows, width), BF16),
+            jax.ShapeDtypeStruct((rows, width), BF16),
+            jax.ShapeDtypeStruct((rows, 3 * units), BF16),
+            jax.ShapeDtypeStruct((4 * block, rows), BF16),
+            jax.ShapeDtypeStruct((rows, LANES), F32),
+        ],
+        compiler_params=pltpu.CompilerParams(vmem_limit_bytes=VMEM),
+        cost_estimate=pl.CostEstimate(
+            flops=2 * rows * width * (3 * units + 8 * block),
+            bytes_accessed=2 * (3 * units * width + 8 * block * width + 2 * rows * width),
+            transcendentals=0,
+        ),
+        name="front",
+    )(expert, *blocks, *blocks, *blocks, w_gate, w_up, w_down)
+
+
+def back_kernel(expert, own, peer, weights, spread, w_gate, w_up, *refs):
+    hidden, grad_gate, grad_up, keep, send = refs
+    step = pl.program_id(0)
+    units, tile = w_gate.shape
+    width = tile * pl.num_programs(0)
+    block = keep.shape[0] // 2
+    rows = own.shape[0]
+
+    def place(term, columns):
+        placed = jnp.dot(spread[...], term, preferred_element_type=F32).astype(BF16)
+        keep[:block, columns] = placed[:block]
+        send[:block, columns] = placed[block : 2 * block]
+        keep[block:, columns] = placed[2 * block : 3 * block]
+        send[block:, columns] = placed[3 * block :]
+
+    @pl.when(step == 0)
+    def _():
+        def value(i):
+            columns = pl.ds(i * units, units)
+            return own[:, columns].astype(F32) + peer[:, columns].astype(F32)
+
+        h, gg, gu, prob = activations(value(0), value(1), value(2), weights[:, :1])
+        hidden[...] = h
+        grad_gate[...] = gg
+        grad_up[...] = gu
+        lane = lax.broadcasted_iota(jnp.int32, (rows, LANES), 1)
+        place(
+            jnp.where(lane == expert[0], prob, 0.0).astype(BF16),
+            slice(keep.shape[1] - LANES, keep.shape[1]),
+        )
+
+    term = jnp.dot(grad_gate[...], w_gate[...], preferred_element_type=F32)
+    term = term + jnp.dot(grad_up[...], w_up[...], preferred_element_type=F32)
+    place(term.astype(BF16), pl.ds(pl.multiple_of(step * tile, tile), tile))
+
+
+def back(own, peer, weights, spread, expert, w_gate, w_up):
+    units, width = w_gate.shape
+    rows = own.shape[0]
+    tokens = spread.shape[0]
+    tile = 512
+    weight_spec = pl.BlockSpec((units, tile), lambda k, e: (0, k))
+    whole = lambda shape: pl.BlockSpec(shape, lambda k, e: (0, 0))
+    half = (tokens // 2, width + LANES)
+    return pl.pallas_call(
+        back_kernel,
+        grid_spec=pltpu.PrefetchScalarGridSpec(
+            num_scalar_prefetch=1,
+            grid=(width // tile,),
+            in_specs=[whole(own.shape), whole(peer.shape), whole(weights.shape), whole(spread.shape)]
+            + [weight_spec] * 2,
+            out_specs=[whole((rows, units))] * 3 + [whole(half)] * 2,
+        ),
+        out_shape=[jax.ShapeDtypeStruct((rows, units), BF16)] * 3
+        + [jax.ShapeDtypeStruct(half, BF16)] * 2,
+        compiler_params=pltpu.CompilerParams(vmem_limit_bytes=VMEM),
+        cost_estimate=pl.CostEstimate(
+            flops=2 * rows * width * (2 * units + tokens),
+            bytes_accessed=2 * (2 * units * width + tokens * width + 9 * rows * units),
+            transcendentals=rows * units,
+        ),
+        name="back",
+    )(expert, own, peer, weights, spread, w_gate, w_up)
+
+
+def outer_kernel(count, *refs):
+    lefts, rights, out = refs[:count], refs[count : 2 * count], refs[2 * count]
+    total = contract_first(lefts[0][...], rights[0][...])
+    for left, right in zip(lefts[1:], rights[1:]):
+        total = total + contract_first(left[...], right[...])
+    out[...] = total.astype(BF16)
+
+
+def outer(lefts, rights):
+    units, width = lefts[0].shape[1], rights[0].shape[1]
+    rows = sum(left.shape[0] for left in lefts)
+    tile = 512
+    return pl.pallas_call(
+        functools.partial(outer_kernel, len(lefts)),
+        grid=(width // tile,),
+        in_specs=[pl.BlockSpec(left.shape, lambda k: (0, 0)) for left in lefts]
+        + [pl.BlockSpec((right.shape[0], tile), lambda k: (0, k)) for right in rights],
+        out_specs=pl.BlockSpec((units, tile), lambda k: (0, k)),
+        out_shape=jax.ShapeDtypeStruct((units, width), BF16),
+        compiler_params=pltpu.CompilerParams(vmem_limit_bytes=VMEM),
+        cost_estimate=pl.CostEstimate(
+            flops=2 * rows * width * units,
+            bytes_accessed=2 * (rows * (width + units) + units * width),
+            transcendentals=0,
+        ),
+        name="outer",
+    )(*lefts, *rights)
+
+
+def add(*terms):
+    return sum(t.astype(F32) for t in terms).astype(BF16)
+
+
+def local_dense(tokens, cotangent, router_probs, expert_ids, w_gate, w_up, w_down):
+    experts = lax.axis_size("expert")
+    block, top_count = expert_ids.shape
+    row_count = block * top_count
+    slots = min(block, max(2, (row_count + experts - 1) // experts * 17 // 16))
+    me = lax.axis_index("expert")
+    expert = me.astype(jnp.int32).reshape(1)
+    weight_gate, weight_up, weight_down = w_gate[0], w_up[0], w_down[0]
+
+    def swap(value, bits):
+        return lax.ppermute(value, "expert", [(i, i ^ bits) for i in range(experts)])
+
+    core, across, near, far = (functools.partial(swap, bits=bits) for bits in (1, 2, 4, 8))
+
+    own = pack(tokens, cotangent, router_probs, expert_ids)
+    row_near = near(own)
+    row_far = far(own)
+    row_both = near(row_far)
+
+    kept = []
+    sums = []
+    for first in (own, row_near, row_far, row_both):
+        second = across(first)
+        blocks = (first, core(first), second, core(second))
+        inputs, scaled, part, spread, weights = front(
+            blocks, expert, weight_gate, weight_up, weight_down, slots
+        )
+        peer = lax.ppermute(part, "dp", [(0, 1), (1, 0)])
+        hidden, grad_gate, grad_up, keep, send = back(
+            part, peer, weights, spread, expert, weight_gate, weight_up
+        )
+        kept.append((inputs, scaled, hidden, grad_gate, grad_up))
+        got = core(send)
+        mine = add(keep[:block], got[:block])
+        theirs = add(keep[block:], got[block:])
+        sums.append(add(mine, across(theirs)))
+
+    inputs, scaled, hidden, grad_gate, grad_up = zip(*kept)
+    gate_grad = outer(grad_gate, inputs)
+    up_grad = outer(grad_up, inputs)
+    down_grad = outer(hidden, scaled)
+
+    from_near = near(sums[1])
+    from_far = far(add(sums[2], near(sums[3])))
+    total = add(sums[0], from_near, from_far)
+    features = tokens.shape[1]
+    by_expert = total[:, features : features + experts].astype(F32)
+    chosen = expert_ids[:, :, None] == jnp.arange(experts, dtype=jnp.int32)[None, None, :]
+    prob_grads = jnp.sum(jnp.where(chosen, by_expert[:, None, :], 0.0), axis=2)
+    return (
+        total[:, :features],
+        prob_grads,
+        gate_grad[None],
+        up_grad[None],
+        down_grad[None],
+    )
+
+
 def solution(mesh):
+    dense = mesh.shape["expert"] == 16 and mesh.shape["dp"] == 2
     return jax.shard_map(
-        local,
+        local_dense if dense else local_general,
         mesh=mesh,
         in_specs=(
             P("expert", "dp"),

time: 614 us -> 347 us (0.57)
  the two profiles are of different devices: /device:TPU:11 before, /device:TPU:0 now
where the time goes in v1:
time: 347 us; the launch traced here: 346 us
  waiting for transfers between devices  192 us (55%)
  Pallas kernels  113 us (33%)
  starting transfers between devices  25.4 us (7%)
  local copies, waits for them, and re-layouts  10.3 us (3%)
  other arithmetic  4.12 us (1%)
    ppermute x26, waiting for transfers between devices, swap(): lax.ppermute(value, 'expert', [(i, i ^ bits) for i in range(experts)])  151 us
    pallas_call x4, Pallas kernels, front(): pl.pallas_call(functools.partial(front_kernel, slots), grid_spec=pltpu.Pr...  44.2 us
    ppermute x4, waiting for transfers between devices, local_dense(): peer = lax.ppermute(part, 'dp', [(0, 1), (1, 0)])  41 us
    pallas_call x4, Pallas kernels, back(): pl.pallas_call(back_kernel, grid_spec=pltpu.PrefetchScalarGridSpec(num_sc...  36.4 us
    pallas_call x3, Pallas kernels, outer(): pl.pallas_call(functools.partial(outer_kernel, len(lefts)), grid=(width /...  30.3 us
    ppermute x26, starting transfers between devices, swap(): lax.ppermute(value, 'expert', [(i, i ^ bits) for i in range(experts)])  21.1 us
    unnamed x34, local copies, waits for them, and re-layouts  9.44 us
  transfers between devices with their start and end apart: 30, of which 12 were waited for; matrix products, arithmetic and copies ran while one was open for 1% of the time, Pallas kernels for 32%

profile of v1, /device:TPU:0, one launch (start us, length us, event | category | flops | bytes accessed | tf_op | source)
XLA Modules:
  0.0 346.5 jit_solution(8467661693795760211)
XLA Ops:
  3.4 2.5 pack.1.refs_0_.refs_4_.refs_8_
  5.9 4.0 %collective-permute-start.14 = (bf16[128,4224]{1,0:T(8,128)(2,1)}, bf16[128,4224]{1,0:T(8,128)(2,1)S(1)}, u32[]{:S(2)}, u32[]{:S(2)}) collective-permute-start(bf16[128,4224]{1,0:T(8,128)(2,1)} %pack.1.refs_0_.refs_4_.refs_8_), channel_id=1, source_target_pairs={{0,8},{1,9},{2,10},{3,11},{4,12},{5,13},{6,14},{7,15},{8,0},{9,1},... | collective-permute-start | bytes 3244040 | tf_op jit(solution)/shard_map/ppermute | solution.py:345
  13.0 44.3 %collective-permute-done.14.refs_0_.refs_4_.refs_8_ = bf16[128,4224]{1,0:T(8,128)(2,1)S(1)} collective-permute-done((bf16[128,4224]{1,0:T(8,128)(2,1)}, bf16[128,4224]{1,0:T(8,128)(2,1)S(1)}, u32[]{:S(2)}, u32[]{:S(2)}) %collective-permute-start.14) | collective-permute-done | bytes 1081376 | tf_op jit(solution)/shard_map/ppermute | solution.py:345
  60.3 22.0 %collective-permute-done.21.refs_0_.refs_4_.refs_8_ = bf16[128,4224]{1,0:T(8,128)(2,1)S(1)} collective-permute-done((bf16[128,4224]{1,0:T(8,128)(2,1)S(1)}, bf16[128,4224]{1,0:T(8,128)(2,1)S(1)}, u32[]{:S(2)}, u32[]{:S(2)}) %collective-permute-start.21) | collective-permute-done | bytes 1081376 | tf_op jit(solution)/shard_map/ppermute | solution.py:345
  85.4 22.7 %collective-permute-done.8.refs_2_.refs_6_.refs_10_ = bf16[128,4224]{1,0:T(8,128)(2,1)} collective-permute-done((bf16[128,4224]{1,0:T(8,128)(2,1)S(1)}, bf16[128,4224]{1,0:T(8,128)(2,1)}, u32[]{:S(2)}, u32[]{:S(2)}) %collective-permute-start.8) | collective-permute-done | bytes 1081376 | tf_op jit(solution)/shard_map/ppermute | solution.py:345
  108.6 21.4 %collective-permute-done.23.refs_2_.refs_6_.refs_10_ = bf16[128,4224]{1,0:T(8,128)(2,1)} collective-permute-done((bf16[128,4224]{1,0:T(8,128)(2,1)S(1)}, bf16[128,4224]{1,0:T(8,128)(2,1)}, u32[]{:S(2)}, u32[]{:S(2)}) %collective-permute-start.23) | collective-permute-done | bytes 1081376 | tf_op jit(solution)/shard_map/ppermute | solution.py:345
  130.0 11.0 %front.4 = (bf16[272,2048]{1,0:T(8,128)(2,1)}, bf16[272,2048]{1,0:T(8,128)(2,1)}, bf16[272,2304]{1,0:T(8,128)(2,1)}, bf16[512,272]{1,0:T(8,128)(2,1)}, f32[272,128]{1,0:T(8,128)}) custom-call(s32[1]{0:T(128)} %bitcast.expert, bf16[128,4224]{1,0:T(8,128)(2,1)} %pack.1.refs_0_.refs_4_.refs_8_, bf16[128,4224]{1,0:T(8,128)(2,1)} %copy-done.3, ...), custom_call_target="tpu_custom_call" | custom-call | flops 3707764736 | bytes 15859712 | tf_op jit(solution)/shard_map/front/pallas_call | solution.py:199
  142.6 11.0 %front.6 = (bf16[272,2048]{1,0:T(8,128)(2,1)}, bf16[272,2048]{1,0:T(8,128)(2,1)}, bf16[272,2304]{1,0:T(8,128)(2,1)}, bf16[512,272]{1,0:T(8,128)(2,1)}, f32[272,128]{1,0:T(8,128)}) custom-call(s32[1]{0:T(128)} %bitcast.expert, bf16[128,4224]{1,0:T(8,128)(2,1)} %copy-done.2, bf16[128,4224]{1,0:T(8,128)(2,1)} %copy-done.4, ...), custom_call_target="tpu_custom_call" | custom-call | flops 3707764736 | bytes 15859712 | tf_op jit(solution)/shard_map/front/pallas_call | solution.py:199
  154.3 11.1 %front.5 = (bf16[272,2048]{1,0:T(8,128)(2,1)}, bf16[272,2048]{1,0:T(8,128)(2,1)}, bf16[272,2304]{1,0:T(8,128)(2,1)}, bf16[512,272]{1,0:T(8,128)(2,1)}, f32[272,128]{1,0:T(8,128)}) custom-call(s32[1]{0:T(128)} %bitcast.expert, bf16[128,4224]{1,0:T(8,128)(2,1)} %copy-done.1, bf16[128,4224]{1,0:T(8,128)(2,1)} %collective-permute-done.7.refs_1_.refs_5_.refs_9_, ...), custom_call_target="tpu_custom_call" | custom-call | flops 3707764736 | bytes 15859712 | tf_op jit(solution)/shard_map/front/pallas_call | solution.py:199
  168.9 11.0 %front.7 = (bf16[272,2048]{1,0:T(8,128)(2,1)}, bf16[272,2048]{1,0:T(8,128)(2,1)}, bf16[272,2304]{1,0:T(8,128)(2,1)}, bf16[512,272]{1,0:T(8,128)(2,1)}, f32[272,128]{1,0:T(8,128)}) custom-call(s32[1]{0:T(128)} %bitcast.expert, bf16[128,4224]{1,0:T(8,128)(2,1)} %copy-done, bf16[128,4224]{1,0:T(8,128)(2,1)} %copy-done.5, ...), custom_call_target="tpu_custom_call" | custom-call | flops 3707764736 | bytes 15859712 | tf_op jit(solution)/shard_map/front/pallas_call | solution.py:199
  181.6 9.1 %back.4 = (bf16[272,768]{1,0:T(8,128)(2,1)}, bf16[272,768]{1,0:T(8,128)(2,1)}, bf16[272,768]{1,0:T(8,128)(2,1)}, bf16[256,2176]{1,0:T(8,128)(2,1)}, bf16[256,2176]{1,0:T(8,128)(2,1)}) custom-call(s32[1]{0:T(128)} %bitcast.expert, bf16[272,2304]{1,0:T(8,128)(2,1)} %get-tuple-element.45.own, bf16[272,2304]{1,0:T(8,128)(2,1)} %copy-done.7, ...), custom_call_target="tpu_custom_call" | custom-call | flops 2281701376 | bytes 12148736 | tf_op jit(solution)/shard_map/back/pallas_call | solution.py:281
  190.7 7.9 %collective-permute-done.18.peer = bf16[272,2304]{1,0:T(8,128)(2,1)S(1)} collective-permute-done((bf16[272,2304]{1,0:T(8,128)(2,1)}, bf16[272,2304]{1,0:T(8,128)(2,1)S(1)}, u32[]{:S(2)}, u32[]{:S(2)}) %collective-permute-start.18) | collective-permute-done | bytes 1253408 | tf_op jit(solution)/shard_map/ppermute | solution.py:362
  199.6 9.1 %back.6 = (bf16[272,768]{1,0:T(8,128)(2,1)}, bf16[272,768]{1,0:T(8,128)(2,1)}, bf16[272,768]{1,0:T(8,128)(2,1)}, bf16[256,2176]{1,0:T(8,128)(2,1)}, bf16[256,2176]{1,0:T(8,128)(2,1)}) custom-call(s32[1]{0:T(128)} %bitcast.expert, bf16[272,2304]{1,0:T(8,128)(2,1)} %get-tuple-element.55.own, bf16[272,2304]{1,0:T(8,128)(2,1)} %copy-done.8, ...), custom_call_target="tpu_custom_call" | custom-call | flops 2281701376 | bytes 12148736 | tf_op jit(solution)/shard_map/back/pallas_call | solution.py:281
  208.7 16.7 %collective-permute-done.10.peer = bf16[272,2304]{1,0:T(8,128)(2,1)S(1)} collective-permute-done((bf16[272,2304]{1,0:T(8,128)(2,1)}, bf16[272,2304]{1,0:T(8,128)(2,1)S(1)}, u32[]{:S(2)}, u32[]{:S(2)}) %collective-permute-start.10) | collective-permute-done | bytes 1253408 | tf_op jit(solution)/shard_map/ppermute | solution.py:362
  226.4 9.0 %back.5 = (bf16[272,768]{1,0:T(8,128)(2,1)}, bf16[272,768]{1,0:T(8,128)(2,1)}, bf16[272,768]{1,0:T(8,128)(2,1)}, bf16[256,2176]{1,0:T(8,128)(2,1)}, bf16[256,2176]{1,0:T(8,128)(2,1)}) custom-call(s32[1]{0:T(128)} %bitcast.expert, bf16[272,2304]{1,0:T(8,128)(2,1)} %get-tuple-element.50.own, bf16[272,2304]{1,0:T(8,128)(2,1)} %copy-done.9, ...), custom_call_target="tpu_custom_call" | custom-call | flops 2281701376 | bytes 12148736 | tf_op jit(solution)/shard_map/back/pallas_call | solution.py:281
  235.5 16.4 %collective-permute-done.25.peer = bf16[272,2304]{1,0:T(8,128)(2,1)S(1)} collective-permute-done((bf16[272,2304]{1,0:T(8,128)(2,1)}, bf16[272,2304]{1,0:T(8,128)(2,1)S(1)}, u32[]{:S(2)}, u32[]{:S(2)}) %collective-permute-start.25) | collective-permute-done | bytes 1253408 | tf_op jit(solution)/shard_map/ppermute | solution.py:362
  252.9 9.2 %back.7 = (bf16[272,768]{1,0:T(8,128)(2,1)}, bf16[272,768]{1,0:T(8,128)(2,1)}, bf16[272,768]{1,0:T(8,128)(2,1)}, bf16[256,2176]{1,0:T(8,128)(2,1)}, bf16[256,2176]{1,0:T(8,128)(2,1)}) custom-call(s32[1]{0:T(128)} %bitcast.expert, bf16[272,2304]{1,0:T(8,128)(2,1)} %get-tuple-element.60.own, bf16[272,2304]{1,0:T(8,128)(2,1)} %copy-done.10, ...), custom_call_target="tpu_custom_call" | custom-call | flops 2281701376 | bytes 12148736 | tf_op jit(solution)/shard_map/back/pallas_call | solution.py:281
  264.5 10.2 %outer.3 = bf16[768,2048]{1,0:T(8,128)(2,1)} custom-call(bf16[272,768]{1,0:T(8,128)(2,1)} %get-tuple-element.65.refs_0_, bf16[272,768]{1,0:T(8,128)(2,1)} %get-tuple-element.66.refs_1_, bf16[272,768]{1,0:T(8,128)(2,1)} %get-tuple-element.67.refs_2_, bf16[272,768]{1,0:T(8,128)(2,1)} %get-tuple-element.68.refs_3_, ...), custom_call_target="tpu_custom_call" | custom-call | flops 3422552064 | bytes 9273344 | tf_op jit(solution)/shard_map/outer/pallas_call | solution.py:314
  278.4 24.2 %collective-permute-done.27 = bf16[128,2176]{1,0:T(8,128)(2,1)S(1)} collective-permute-done((bf16[128,2176]{1,0:T(8,128)(2,1)S(1)}, bf16[128,2176]{1,0:T(8,128)(2,1)S(1)}, u32[]{:S(2)}, u32[]{:S(2)}) %collective-permute-start.27) | collective-permute-done | bytes 557088 | tf_op jit(solution)/shard_map/ppermute | solution.py:345
  303.3 10.8 %collective-permute-done.12 = bf16[128,2176]{1,0:T(8,128)(2,1)S(1)} collective-permute-done((bf16[128,2176]{1,0:T(8,128)(2,1)S(1)}, bf16[128,2176]{1,0:T(8,128)(2,1)S(1)}, u32[]{:S(2)}, u32[]{:S(2)}) %collective-permute-start.12) | collective-permute-done | bytes 557088 | tf_op jit(solution)/shard_map/ppermute | solution.py:345
  317.0 3.3 collective-permute-start.29
  320.3 10.1 %outer.4 = bf16[768,2048]{1,0:T(8,128)(2,1)} custom-call(bf16[272,768]{1,0:T(8,128)(2,1)} %get-tuple-element.73.refs_0_, bf16[272,768]{1,0:T(8,128)(2,1)} %get-tuple-element.74.refs_1_, bf16[272,768]{1,0:T(8,128)(2,1)} %get-tuple-element.75.refs_2_, bf16[272,768]{1,0:T(8,128)(2,1)} %get-tuple-element.76.refs_3_, ...), custom_call_target="tpu_custom_call" | custom-call | flops 3422552064 | bytes 9273344 | tf_op jit(solution)/shard_map/outer/pallas_call | solution.py:314
  330.4 10.1 %outer.5 = bf16[768,2048]{1,0:T(8,128)(2,1)} custom-call(bf16[272,768]{1,0:T(8,128)(2,1)} %get-tuple-element.77.refs_0_, bf16[272,768]{1,0:T(8,128)(2,1)} %get-tuple-element.78.refs_1_, bf16[272,768]{1,0:T(8,128)(2,1)} %get-tuple-element.79.refs_2_, bf16[272,768]{1,0:T(8,128)(2,1)} %get-tuple-element.80.refs_3_, ...), custom_call_target="tpu_custom_call" | custom-call | flops 3422552064 | bytes 9273344 | tf_op jit(solution)/shard_map/outer/pallas_call | solution.py:314
  340.5 3.0 collective-permute-done.29
  (94 shorter events, 35.6 us)
Async XLA Ops:
  5.9 51.4 %collective-permute-start.14 = (bf16[128,4224]{1,0:T(8,128)(2,1)}, bf16[128,4224]{1,0:T(8,128)(2,1)S(1)}, u32[]{:S(2)}, u32[]{:S(2)}) collective-permute-start(bf16[128,4224]{1,0:T(8,128)(2,1)} %pack.1.refs_0_.refs_4_.refs_8_), channel_id=1, source_target_pairs={{0,8},{1,9},{2,10},{3,11},{4,12},{5,13},{6,14},{7,15},{8,0},{9,1},... | collective-permute-start | bytes 3244040 | tf_op jit(solution)/shard_map/ppermute | solution.py:345
  9.9 49.6 %collective-permute-start.6 = (bf16[128,4224]{1,0:T(8,128)(2,1)}, bf16[128,4224]{1,0:T(8,128)(2,1)S(1)}, u32[]{:S(2)}, u32[]{:S(2)}) collective-permute-start(bf16[128,4224]{1,0:T(8,128)(2,1)} %pack.1.refs_0_.refs_4_.refs_8_), channel_id=1, source_target_pairs={{0,4},{1,5},{2,6},{3,7},{4,0},{5,1},{6,2},{7,3},{8,12},{9,13},{10,... | collective-permute-start | bytes 3244040 | tf_op jit(solution)/shard_map/ppermute | solution.py:345
  11.5 48.0 %collective-permute-start = (bf16[128,4224]{1,0:T(8,128)(2,1)}, bf16[128,4224]{1,0:T(8,128)(2,1)S(1)}, u32[]{:S(2)}, u32[]{:S(2)}) collective-permute-start(bf16[128,4224]{1,0:T(8,128)(2,1)} %pack.1.refs_0_.refs_4_.refs_8_), channel_id=1, source_target_pairs={{0,1},{1,0},{2,3},{3,2},{4,5},{5,4},{6,7},{7,6},{8,9},{9,8},{10,11... | collective-permute-start | bytes 3244040 | tf_op jit(solution)/shard_map/ppermute | solution.py:345
  11.5 48.6 %collective-permute-start.1 = (bf16[128,4224]{1,0:T(8,128)(2,1)}, bf16[128,4224]{1,0:T(8,128)(2,1)}, u32[]{:S(2)}, u32[]{:S(2)}) collective-permute-start(bf16[128,4224]{1,0:T(8,128)(2,1)} %pack.1.refs_0_.refs_4_.refs_8_), channel_id=1, source_target_pairs={{0,2},{1,3},{2,0},{3,1},{4,6},{5,7},{6,4},{7,5},{8,10},{9,11},{10,... | collective-permute-start | bytes 3244040 | tf_op jit(solution)/shard_map/ppermute | solution.py:345
  58.0 26.9 %collective-permute-start.16 = (bf16[128,4224]{1,0:T(8,128)(2,1)S(1)}, bf16[128,4224]{1,0:T(8,128)(2,1)}, u32[]{:S(2)}, u32[]{:S(2)}) collective-permute-start(bf16[128,4224]{1,0:T(8,128)(2,1)S(1)} %collective-permute-done.14.refs_0_.refs_4_.refs_8_), channel_id=1, source_target_pairs={{0,2},{1,3},{2,0},{3,1},{4,6},{5,7},{6,4},{7,5},{8,10},{9,11},{10,... | collective-permute-start | bytes 3244040 | tf_op jit(solution)/shard_map/ppermute | solution.py:345
  59.5 48.5 %collective-permute-start.8 = (bf16[128,4224]{1,0:T(8,128)(2,1)S(1)}, bf16[128,4224]{1,0:T(8,128)(2,1)}, u32[]{:S(2)}, u32[]{:S(2)}) collective-permute-start(bf16[128,4224]{1,0:T(8,128)(2,1)S(1)} %collective-permute-done.6.refs_0_.refs_4_.refs_8_), channel_id=1, source_target_pairs={{0,2},{1,3},{2,0},{3,1},{4,6},{5,7},{6,4},{7,5},{8,10},{9,11},{10,... | collective-permute-start | bytes 3244040 | tf_op jit(solution)/shard_map/ppermute | solution.py:345
  60.2 47.9 %collective-permute-start.2 = (bf16[128,4224]{1,0:T(8,128)(2,1)}, bf16[128,4224]{1,0:T(8,128)(2,1)}, u32[]{:S(2)}, u32[]{:S(2)}) collective-permute-start(bf16[128,4224]{1,0:T(8,128)(2,1)} %collective-permute-done.1.refs_2_.refs_6_.refs_10_), channel_id=1, source_target_pairs={{0,1},{1,0},{2,3},{3,2},{4,5},{5,4},{6,7},{7,6},{8,9},{9,8},{10,11... | collective-permute-start | bytes 3244040 | tf_op jit(solution)/shard_map/ppermute | solution.py:345
  82.3 47.7 %collective-permute-start.23 = (bf16[128,4224]{1,0:T(8,128)(2,1)S(1)}, bf16[128,4224]{1,0:T(8,128)(2,1)}, u32[]{:S(2)}, u32[]{:S(2)}) collective-permute-start(bf16[128,4224]{1,0:T(8,128)(2,1)S(1)} %collective-permute-done.21.refs_0_.refs_4_.refs_8_), channel_id=1, source_target_pairs={{0,2},{1,3},{2,0},{3,1},{4,6},{5,7},{6,4},{7,5},{8,10},{9,11},{10,... | collective-permute-start | bytes 3244040 | tf_op jit(solution)/shard_map/ppermute | solution.py:345
  84.9 56.2 %collective-permute-start.17 = (bf16[128,4224]{1,0:T(8,128)(2,1)}, bf16[128,4224]{1,0:T(8,128)(2,1)}, u32[]{:S(2)}, u32[]{:S(2)}) collective-permute-start(bf16[128,4224]{1,0:T(8,128)(2,1)} %collective-permute-done.16.refs_2_.refs_6_.refs_10_), channel_id=1, source_target_pairs={{0,1},{1,0},{2,3},{3,2},{4,5},{5,4},{6,7},{7,6},{8,9},{9,8},{10,11... | collective-permute-start | bytes 3244040 | tf_op jit(solution)/shard_map/ppermute | solution.py:345
  84.9 68.8 %collective-permute-start.7 = (bf16[128,4224]{1,0:T(8,128)(2,1)S(1)}, bf16[128,4224]{1,0:T(8,128)(2,1)}, u32[]{:S(2)}, u32[]{:S(2)}) collective-permute-start(bf16[128,4224]{1,0:T(8,128)(2,1)S(1)} %collective-permute-done.6.refs_0_.refs_4_.refs_8_), channel_id=1, source_target_pairs={{0,1},{1,0},{2,3},{3,2},{4,5},{5,4},{6,7},{7,6},{8,9},{9,8},{10,11... | collective-permute-start | bytes 3244040 | tf_op jit(solution)/shard_map/ppermute | solution.py:345
  108.1 46.2 %collective-permute-start.9 = (bf16[128,4224]{1,0:T(8,128)(2,1)}, bf16[128,4224]{1,0:T(8,128)(2,1)}, u32[]{:S(2)}, u32[]{:S(2)}) collective-permute-start(bf16[128,4224]{1,0:T(8,128)(2,1)} %collective-permute-done.8.refs_2_.refs_6_.refs_10_), channel_id=1, source_target_pairs={{0,1},{1,0},{2,3},{3,2},{4,5},{5,4},{6,7},{7,6},{8,9},{9,8},{10,11... | collective-permute-start | bytes 3244040 | tf_op jit(solution)/shard_map/ppermute | solution.py:345
  108.1 58.9 %collective-permute-start.22 = (bf16[128,4224]{1,0:T(8,128)(2,1)S(1)}, bf16[128,4224]{1,0:T(8,128)(2,1)S(1)}, u32[]{:S(2)}, u32[]{:S(2)}) collective-permute-start(bf16[128,4224]{1,0:T(8,128)(2,1)S(1)} %collective-permute-done.21.refs_0_.refs_4_.refs_8_), channel_id=1, source_target_pairs={{0,1},{1,0},{2,3},{3,2},{4,5},{5,4},{6,7},{7,6},{8,9},{9,8},{10,11... | collective-permute-start | bytes 3244040 | tf_op jit(solution)/shard_map/ppermute | solution.py:345
  130.0 37.0 %collective-permute-start.24 = (bf16[128,4224]{1,0:T(8,128)(2,1)}, bf16[128,4224]{1,0:T(8,128)(2,1)S(1)}, u32[]{:S(2)}, u32[]{:S(2)}) collective-permute-start(bf16[128,4224]{1,0:T(8,128)(2,1)} %collective-permute-done.23.refs_2_.refs_6_.refs_10_), channel_id=1, source_target_pairs={{0,1},{1,0},{2,3},{3,2},{4,5},{5,4},{6,7},{7,6},{8,9},{9,8},{10,11... | collective-permute-start | bytes 3244040 | tf_op jit(solution)/shard_map/ppermute | solution.py:345
  141.1 39.5 %collective-permute-start.3 = (bf16[272,2304]{1,0:T(8,128)(2,1)}, bf16[272,2304]{1,0:T(8,128)(2,1)S(1)}, u32[]{:S(2)}, u32[]{:S(2)}) collective-permute-start(bf16[272,2304]{1,0:T(8,128)(2,1)} %get-tuple-element.45.own), channel_id=1, source_target_pairs={{0,16},{16,0},{1,17},{17,1},{2,18},{18,2},{3,19},{19,3},{4,20},{20... | collective-permute-start | bytes 3760136 | tf_op jit(solution)/shard_map/ppermute | solution.py:362
  153.7 44.8 %collective-permute-start.18 = (bf16[272,2304]{1,0:T(8,128)(2,1)}, bf16[272,2304]{1,0:T(8,128)(2,1)S(1)}, u32[]{:S(2)}, u32[]{:S(2)}) collective-permute-start(bf16[272,2304]{1,0:T(8,128)(2,1)} %get-tuple-element.55.own), channel_id=1, source_target_pairs={{0,16},{16,0},{1,17},{17,1},{2,18},{18,2},{3,19},{19,3},{4,20},{20... | collective-permute-start | bytes 3760136 | tf_op jit(solution)/shard_map/ppermute | solution.py:362
  165.3 60.0 %collective-permute-start.10 = (bf16[272,2304]{1,0:T(8,128)(2,1)}, bf16[272,2304]{1,0:T(8,128)(2,1)S(1)}, u32[]{:S(2)}, u32[]{:S(2)}) collective-permute-start(bf16[272,2304]{1,0:T(8,128)(2,1)} %get-tuple-element.50.own), channel_id=1, source_target_pairs={{0,16},{16,0},{1,17},{17,1},{2,18},{18,2},{3,19},{19,3},{4,20},{20... | collective-permute-start | bytes 3760136 | tf_op jit(solution)/shard_map/ppermute | solution.py:362
  179.9 71.9 %collective-permute-start.25 = (bf16[272,2304]{1,0:T(8,128)(2,1)}, bf16[272,2304]{1,0:T(8,128)(2,1)S(1)}, u32[]{:S(2)}, u32[]{:S(2)}) collective-permute-start(bf16[272,2304]{1,0:T(8,128)(2,1)} %get-tuple-element.60.own), channel_id=1, source_target_pairs={{0,16},{16,0},{1,17},{17,1},{2,18},{18,2},{3,19},{19,3},{4,20},{20... | collective-permute-start | bytes 3760136 | tf_op jit(solution)/shard_map/ppermute | solution.py:362
  190.7 71.4 %collective-permute-start.4 = (bf16[256,2176]{1,0:T(8,128)(2,1)}, bf16[256,2176]{1,0:T(8,128)(2,1)S(1)}, u32[]{:S(2)}, u32[]{:S(2)}) collective-permute-start(bf16[256,2176]{1,0:T(8,128)(2,1)} %get-tuple-element.49), channel_id=1, source_target_pairs={{0,1},{1,0},{2,3},{3,2},{4,5},{5,4},{6,7},{7,6},{8,9},{9,8},{10,11... | collective-permute-start | bytes 3342344 | tf_op jit(solution)/shard_map/ppermute | solution.py:345
  208.7 66.1 %collective-permute-start.19 = (bf16[256,2176]{1,0:T(8,128)(2,1)}, bf16[256,2176]{1,0:T(8,128)(2,1)S(1)}, u32[]{:S(2)}, u32[]{:S(2)}) collective-permute-start(bf16[256,2176]{1,0:T(8,128)(2,1)} %get-tuple-element.59), channel_id=1, source_target_pairs={{0,1},{1,0},{2,3},{3,2},{4,5},{5,4},{6,7},{7,6},{8,9},{9,8},{10,11... | collective-permute-start | bytes 3342344 | tf_op jit(solution)/shard_map/ppermute | solution.py:345
  235.5 41.7 %collective-permute-start.11 = (bf16[256,2176]{1,0:T(8,128)(2,1)}, bf16[256,2176]{1,0:T(8,128)(2,1)S(1)}, u32[]{:S(2)}, u32[]{:S(2)}) collective-permute-start(bf16[256,2176]{1,0:T(8,128)(2,1)} %get-tuple-element.54), channel_id=1, source_target_pairs={{0,1},{1,0},{2,3},{3,2},{4,5},{5,4},{6,7},{7,6},{8,9},{9,8},{10,11... | collective-permute-start | bytes 3342344 | tf_op jit(solution)/shard_map/ppermute | solution.py:345
  263.1 77.5 %collective-permute-start.5 = (bf16[128,2176]{1,0:T(8,128)(2,1)}, bf16[128,2176]{1,0:T(8,128)(2,1)}, u32[]{:S(2)}, u32[]{:S(2)}) collective-permute-start(bf16[128,2176]{1,0:T(8,128)(2,1)} %add_convert_fusion.12), channel_id=1, source_target_pairs={{0,2},{1,3},{2,0},{3,1},{4,6},{5,7},{6,4},{7,5},{8,10},{9,11},{10,... | collective-permute-start | bytes 1671176 | tf_op jit(solution)/shard_map/ppermute | solution.py:345
  274.9 40.0 %collective-permute-start.20 = (bf16[128,2176]{1,0:T(8,128)(2,1)S(1)}, bf16[128,2176]{1,0:T(8,128)(2,1)S(1)}, u32[]{:S(2)}, u32[]{:S(2)}) collective-permute-start(bf16[128,2176]{1,0:T(8,128)(2,1)S(1)} %add_convert_fusion.6), channel_id=1, source_target_pairs={{0,2},{1,3},{2,0},{3,1},{4,6},{5,7},{6,4},{7,5},{8,10},{9,11},{10,... | collective-permute-start | bytes 1671176 | tf_op jit(solution)/shard_map/ppermute | solution.py:345
  277.3 36.8 %collective-permute-start.12 = (bf16[128,2176]{1,0:T(8,128)(2,1)S(1)}, bf16[128,2176]{1,0:T(8,128)(2,1)S(1)}, u32[]{:S(2)}, u32[]{:S(2)}) collective-permute-start(bf16[128,2176]{1,0:T(8,128)(2,1)S(1)} %add_convert_fusion.9), channel_id=1, source_target_pairs={{0,2},{1,3},{2,0},{3,1},{4,6},{5,7},{6,4},{7,5},{8,10},{9,11},{10,... | collective-permute-start | bytes 1671176 | tf_op jit(solution)/shard_map/ppermute | solution.py:345
  317.0 26.5 %collective-permute-start.29 = (bf16[128,2176]{1,0:T(8,128)(2,1)S(1)}, bf16[128,2176]{1,0:T(8,128)(2,1)S(1)}, u32[]{:S(2)}, u32[]{:S(2)}) collective-permute-start(bf16[128,2176]{1,0:T(8,128)(2,1)S(1)} %add_convert_fusion.1), channel_id=1, source_target_pairs={{0,8},{1,9},{2,10},{3,11},{4,12},{5,13},{6,14},{7,15},{8,0},{9,1},... | collective-permute-start | bytes 1671176 | tf_op jit(solution)/shard_map/ppermute | solution.py:345
  (22 other events, 456.0 us)

commit v2 on v0

--- a/solution.py
+++ b/solution.py
@@ -1,7 +1,16 @@
+import functools
+
 import jax
 import jax.numpy as jnp
 from jax import lax
+from jax.experimental import pallas as pl
+from jax.experimental.pallas import tpu as pltpu
 from jax.sharding import PartitionSpec as P
+
+F32 = jnp.float32
+BF16 = jnp.bfloat16
+LANES = 128
+VMEM = 14 * 1024 * 1024
 
 
 def contract_last(left_matrix, right_matrix):
@@ -20,8 +29,8 @@
     sigmoid_gate = jax.nn.sigmoid(gate_value)
     silu_gate = gate_value * sigmoid_gate
     hidden = (silu_gate * up_value).astype(jnp.bfloat16)
-    prob_local = jnp.sum(hidden.astype(jnp.float32) * back_value, axis=1)
-    grad_back = weights[:, None] * back_value
+    prob_local = jnp.sum(hidden.astype(jnp.float32) * back_value, axis=1, keepdims=True)
+    grad_back = weights * back_value
     grad_gate = (
         grad_back * up_value * sigmoid_gate * (1.0 + gate_value * (1.0 - sigmoid_gate))
     ).astype(jnp.bfloat16)
@@ -29,7 +38,7 @@
     return (hidden, grad_gate, grad_up, prob_local)
 
 
-def local(tokens, cotangent, router_probs, expert_ids, w_gate, w_up, w_down):
+def local_general(tokens, cotangent, router_probs, expert_ids, w_gate, w_up, w_down):
     experts = lax.axis_size("expert")
     local_tokens, top_count = expert_ids.shape
     row_count = local_tokens * top_count
@@ -55,10 +64,13 @@
         picked = jnp.where(filled[:, None], source[owners], jnp.zeros((), source.dtype))
         return picked.reshape(experts, slot_count, source.shape[1])
 
+    exchange = functools.partial(
+        lax.all_to_all, axis_name="expert", split_axis=0, concat_axis=0, tiled=True
+    )
     recv_in, recv_grad, recv_probs = (
-        lax.all_to_all(pack_rows(tokens), "expert", split_axis=0, concat_axis=0, tiled=True),
-        lax.all_to_all(pack_rows(cotangent), "expert", split_axis=0, concat_axis=0, tiled=True),
-        lax.all_to_all(send_probs, "expert", split_axis=0, concat_axis=0, tiled=True),
+        exchange(pack_rows(tokens)),
+        exchange(pack_rows(cotangent)),
+        exchange(send_probs),
     )
     inputs = recv_in.reshape(experts * slot_count, features)
     grads_in = recv_grad.reshape(experts * slot_count, features)
@@ -74,7 +86,9 @@
         lax.psum(up_part.astype(jnp.bfloat16), "dp").astype(jnp.float32),
         lax.psum(back_part.astype(jnp.bfloat16), "dp").astype(jnp.float32),
     )
-    hidden, grad_gate, grad_up, prob_value = activations(gate_value, up_value, back_value, weights)
+    hidden, grad_gate, grad_up, prob_value = activations(
+        gate_value, up_value, back_value, weights[:, None]
+    )
     scaled = (weights[:, None] * grads_in).astype(jnp.bfloat16)
     row_term = jnp.dot(grad_gate, weight_gate, preferred_element_type=jnp.float32)
     row_term = (row_term + jnp.dot(grad_up, weight_up, preferred_element_type=jnp.float32)).astype(
@@ -83,22 +97,8 @@
     gate_grad = contract_first(grad_gate, inputs).astype(jnp.bfloat16)
     up_grad = contract_first(grad_up, inputs).astype(jnp.bfloat16)
     down_grad = contract_first(hidden, scaled).astype(jnp.bfloat16)
-    back_terms, back_probs = (
-        lax.all_to_all(
-            row_term.reshape(experts, slot_count, features),
-            "expert",
-            split_axis=0,
-            concat_axis=0,
-            tiled=True,
-        ),
-        lax.all_to_all(
-            prob_value.astype(jnp.bfloat16).reshape(experts, slot_count),
-            "expert",
-            split_axis=0,
-            concat_axis=0,
-            tiled=True,
-        ),
-    )
+    back_terms = exchange(row_term.reshape(experts, slot_count, features))
+    back_probs = exchange(prob_value.astype(jnp.bfloat16).reshape(experts, slot_count))
     returned = back_terms.reshape(experts * slot_count, features)[slot_places].astype(jnp.float32)
     token_sum = jnp.sum(returned.reshape(local_tokens, top_count, features), axis=1)
     prob_grads = (
@@ -113,9 +113,367 @@
     )
 
 
+def kernel_call(body, operands, outs, scratch=(), name=None):
+    return pl.pallas_call(
+        body,
+        in_specs=[pl.BlockSpec(memory_space=pltpu.VMEM)] * len(operands),
+        out_specs=[pl.BlockSpec(memory_space=pltpu.VMEM)] * len(outs),
+        out_shape=[jax.ShapeDtypeStruct(shape, dtype) for shape, dtype in outs],
+        scratch_shapes=list(scratch),
+        compiler_params=pltpu.CompilerParams(vmem_limit_bytes=VMEM),
+        cost_estimate=pl.CostEstimate(flops=1000, bytes_accessed=1000, transcendentals=0),
+        name=name,
+    )(*operands)
+
+
+def choose_kernel(first, second, out):
+    z_index = lax.div(lax.axis_index("expert"), 4)
+    edge = (z_index == 0) | (z_index == 3)
+
+    @pl.when(edge)
+    def _():
+        out[...] = first[...]
+
+    @pl.when(jnp.logical_not(edge))
+    def _():
+        out[...] = second[...]
+
+
+def choose(first, second):
+    return kernel_call(choose_kernel, (first, second), [(first.shape, BF16)], name="choose")[0]
+
+
+def tiles(width, tile, body):
+    @pl.loop(0, width // tile)
+    def _(k):
+        body(pl.multiple_of(k * tile, tile))
+
+
+def pack_kernel(tokens, cotangent, probs, ids, out):
+    rows, width = tokens.shape
+    out[:, :width] = tokens[...]
+    out[:, width : 2 * width] = cotangent[...]
+    lane = lax.broadcasted_iota(jnp.int32, (rows, LANES), 1)
+    routing = jnp.full((rows, LANES), -1.0, F32)
+    weights = probs[...].astype(F32)
+    for k in range(ids.shape[1]):
+        routing = jnp.where(lane == ids[:, k : k + 1], weights[:, k : k + 1], routing)
+    out[:, 2 * width :] = routing.astype(BF16)
+
+
+def pack(tokens, cotangent, probs, ids):
+    rows, width = tokens.shape
+    operands = (tokens, cotangent, probs, ids)
+    return kernel_call(pack_kernel, operands, [((rows, 2 * width + LANES), BF16)], name="pack")[0]
+
+
+def front_kernel(slots, count, *refs):
+    expert = lax.axis_index("expert")
+    blocks = refs[:count]
+    w_gate, w_up, w_down = refs[count : count + 3]
+    inputs, scaled, spread, weights, *parts, acc, pick = refs[count + 3 :]
+    units, width = w_gate.shape
+    block = blocks[0].shape[0]
+    rows = pick.shape[0]
+    lane = lax.broadcasted_iota(jnp.int32, (block, LANES), 1)
+    tri = (
+        lax.broadcasted_iota(jnp.int32, (block, block), 1)
+        <= lax.broadcasted_iota(jnp.int32, (block, block), 0)
+    ).astype(BF16)
+    total = jnp.zeros((rows, LANES), F32)
+    for b, source in enumerate(blocks):
+        routing = source[:, 2 * width :].astype(F32)
+        prob = jnp.sum(jnp.where(lane == expert, routing, 0.0), axis=1, keepdims=True)
+        chosen = jnp.broadcast_to(prob >= 0.0, (block, LANES))
+        rank = jnp.dot(tri, chosen.astype(BF16), preferred_element_type=F32)
+        slot = jnp.where(chosen, rank + (slots * b - 1.0), -1.0)
+        spread[pl.ds(b * block, block), :] = (
+            lax.broadcasted_iota(jnp.int32, (block, rows), 1) == slot[:, :1].astype(jnp.int32)
+        ).astype(BF16)
+        slot_row = slot.T[:1, :].astype(jnp.int32)
+        picked = (lax.broadcasted_iota(jnp.int32, (rows, block), 0) == slot_row).astype(BF16)
+        pick[:, pl.ds(b * block, block)] = picked
+        prob = jnp.broadcast_to(jnp.maximum(prob, 0.0), (block, LANES)).astype(BF16)
+        total = total + jnp.dot(picked, prob, preferred_element_type=F32)
+    weights[...] = total
+    acc[...] = jnp.zeros(acc.shape, F32)
+    tile = 1024
+
+    def gather(columns):
+        stacked = jnp.concatenate([source[:, columns] for source in blocks], axis=0)
+        return jnp.dot(pick[...], stacked, preferred_element_type=F32)
+
+    def step(start):
+        here, there = pl.ds(start, tile), pl.ds(width + start, tile)
+        rows_in = gather(here).astype(BF16)
+        inputs[:, here] = rows_in
+        acc[:, :units] += contract_last(rows_in, w_gate[:, here])
+        acc[:, units : 2 * units] += contract_last(rows_in, w_up[:, here])
+        grads = gather(there)
+        scaled[:, here] = (weights[:, :1] * grads).astype(BF16)
+        acc[:, 2 * units :] += contract_last(grads.astype(BF16), w_down[:, here])
+
+    tiles(width, tile, step)
+    for i, part in enumerate(parts):
+        size = part.shape[0]
+        part[...] = acc[i * size : (i + 1) * size].astype(BF16)
+
+
+def front(blocks, w_gate, w_up, w_down, slots):
+    count, block = len(blocks), blocks[0].shape[0]
+    units, width = w_gate.shape
+    filled = count * slots
+    rows = -(-filled // 16) * 16
+    return kernel_call(
+        functools.partial(front_kernel, slots, count),
+        (*blocks, w_gate, w_up, w_down),
+        [
+            ((rows, width), BF16),
+            ((rows, width), BF16),
+            ((count * block, rows), BF16),
+            ((rows, LANES), F32),
+        ]
+        + [((2 * slots, 3 * units), BF16)] * (count // 2),
+        scratch=[pltpu.VMEM((rows, 3 * units), F32), pltpu.VMEM((rows, count * block), BF16)],
+        name="front",
+    )
+
+
+def back_kernel(block, weights, spread, w_gate, w_up, *refs):
+    expert = lax.axis_index("expert")
+    *shares, hidden, grad_gate, grad_up, keep, send = refs
+    units, width = w_gate.shape
+    filled = sum(share.shape[0] for share in shares) // 2
+    tokens, rows = spread.shape
+    tile = 1024
+
+    def place(term, columns):
+        placed = jnp.dot(spread[...], term, preferred_element_type=F32).astype(BF16)
+        for b in range(0, tokens // block, 2):
+            here = pl.ds(b // 2 * block, block)
+            keep[here, columns] = placed[b * block : (b + 1) * block]
+            send[here, columns] = placed[(b + 1) * block : (b + 2) * block]
+
+    def value(i):
+        columns = pl.ds(i * units, units)
+        total = [
+            own[:, columns].astype(F32) + peer[:, columns].astype(F32)
+            for own, peer in zip(shares[::2], shares[1::2])
+        ]
+        if rows > filled:
+            total.append(jnp.zeros((rows - filled, units), F32))
+        return jnp.concatenate(total, axis=0)
+
+    h, gg, gu, prob = activations(value(0), value(1), value(2), weights[:, :1])
+    hidden[...] = h
+    grad_gate[...] = gg
+    grad_up[...] = gu
+    lane = lax.broadcasted_iota(jnp.int32, (rows, LANES), 1)
+    place(jnp.where(lane == expert, prob, 0.0).astype(BF16), pl.ds(width, LANES))
+
+    def step(start):
+        columns = pl.ds(start, tile)
+        term = jnp.dot(grad_gate[...], w_gate[:, columns], preferred_element_type=F32)
+        term = term + jnp.dot(grad_up[...], w_up[:, columns], preferred_element_type=F32)
+        place(term.astype(BF16), columns)
+
+    tiles(width, tile, step)
+
+
+def back(shares, weights, spread, w_gate, w_up, block):
+    units, width = w_gate.shape
+    tokens, rows = spread.shape
+    half = (tokens // 2, width + LANES)
+    return kernel_call(
+        functools.partial(back_kernel, block),
+        (weights, spread, w_gate, w_up, *shares),
+        [((rows, units), BF16)] * 3 + [(half, BF16)] * 2,
+        name="back",
+    )
+
+
+def outer_kernel(count, *refs):
+    lefts, rights = refs[:count], refs[count : 2 * count]
+    out, turned = refs[2 * count :]
+
+    @pl.when(pl.program_id(0) == 0)
+    def _():
+        turned[...] = jnp.concatenate([left[...] for left in lefts], axis=0).T
+
+    right = jnp.concatenate([right[...] for right in rights], axis=0)
+    out[...] = jnp.dot(turned[...], right, preferred_element_type=F32).astype(BF16)
+
+
+def outer(lefts, rights):
+    units, width = lefts[0].shape[1], rights[0].shape[1]
+    rows = sum(left.shape[0] for left in lefts)
+    tile = 512
+    return pl.pallas_call(
+        functools.partial(outer_kernel, len(lefts)),
+        grid=(width // tile,),
+        in_specs=[pl.BlockSpec(left.shape, lambda k: (0, 0)) for left in lefts]
+        + [pl.BlockSpec((right.shape[0], tile), lambda k: (0, k)) for right in rights],
+        out_specs=pl.BlockSpec((units, tile), lambda k: (0, k)),
+        out_shape=jax.ShapeDtypeStruct((units, width), BF16),
+        scratch_shapes=[pltpu.VMEM((units, rows), BF16)],
+        compiler_params=pltpu.CompilerParams(vmem_limit_bytes=VMEM),
+        cost_estimate=pl.CostEstimate(flops=1000, bytes_accessed=1000, transcendentals=0),
+        name="outer",
+    )(*lefts, *rights)
+
+
+def add_kernel(block, count, *refs):
+    terms, outs = refs[:count], refs[count:]
+    for i, out in enumerate(outs):
+        rows = pl.ds(i * block, block)
+        total = terms[0][rows, :].astype(F32)
+        for term in terms[1:]:
+            total = total + term[rows, :].astype(F32)
+        out[...] = total.astype(BF16)
+
+
+def add_blocks(block, *terms):
+    rows, width = terms[0].shape
+    return kernel_call(
+        functools.partial(add_kernel, block, len(terms)),
+        terms,
+        [((block, width), BF16)] * (rows // block),
+        name="add",
+    )
+
+
+def add(*terms):
+    return add_blocks(terms[0].shape[0], *terms)[0]
+
+
+def after(value, *gates):
+    return lax.optimization_barrier((value, *gates))[0]
+
+
+def local_dense(tokens, cotangent, router_probs, expert_ids, w_gate, w_up, w_down):
+    experts = lax.axis_size("expert")
+    block, top_count = expert_ids.shape
+    row_count = block * top_count
+    slots = min(block, max(2, (row_count + experts - 1) // experts * 17 // 16))
+    weight_gate, weight_up, weight_down = w_gate[0], w_up[0], w_down[0]
+
+    def swap(value, bits, part=(0, 1, 2, 3)):
+        pairs = [(i, i ^ bits) for i in range(experts) if i // 4 in part]
+        return lax.ppermute(value, "expert", pairs)
+
+    core = functools.partial(swap, bits=1)
+    across = functools.partial(swap, bits=2)
+    outer_z = functools.partial(swap, bits=4)
+    inner_z = functools.partial(swap, bits=12, part=(1, 2))
+
+    def forward(*blocks):
+        inputs, scaled, spread, weights, *parts = front(
+            blocks, weight_gate, weight_up, weight_down, slots
+        )
+        return dict(inputs=inputs, scaled=scaled, parts=parts, spread=spread, weights=weights)
+
+    def exchange(part, *gates):
+        return lax.ppermute(after(part, *gates), "dp", [(0, 1), (1, 0)])
+
+    def backward(state, peers, *gates):
+        peers = after(peers, *gates)
+        hidden, grad_gate, grad_up, keep, send = back(
+            [share for pair in zip(state["parts"], peers) for share in pair],
+            state["weights"],
+            state["spread"],
+            weight_gate,
+            weight_up,
+            block,
+        )
+        return state | dict(
+            hidden=hidden, grad_gate=grad_gate, grad_up=grad_up, keep=keep, got=core(send)
+        )
+
+    def combine(state, *gates):
+        return add_blocks(block, state["keep"], after(state["got"], *gates))
+
+    p0 = pack(tokens, cotangent, router_probs, expert_ids)
+    q0 = core(p0)
+    p1, a0, m0 = across(p0), outer_z(p0), inner_z(p0)
+    s0 = forward(p0, q0)
+    y0 = exchange(s0["parts"][0])
+
+    p1, a0, m0 = after((p1, a0, m0), y0)
+    a1, b0e, c0m = across(a0), outer_z(m0), inner_z(a0)
+    q1 = core(p1)
+    qa0 = core(a0)
+    s1 = forward(p1, q1, a0, qa0)
+    y1a = exchange(s1["parts"][0])
+    s0 = backward(s0, (y0,), s1["parts"])
+
+    a1, b0e, c0m = after((a1, b0e, c0m), y1a, s0["hidden"])
+    y1b = exchange(s1["parts"][1], y1a)
+    b0 = choose(b0e, m0)
+    b1, c0e = across(b0), outer_z(c0m)
+    qa1 = core(a1)
+    qb0 = core(b0)
+    s2 = forward(a1, qa1, b0, qb0)
+    y2a = exchange(s2["parts"][0], y1b)
+    (sum0,) = combine(s0, s2["parts"])
+    s1 = backward(s1, (y1a, y1b), s2["parts"])
+
+    b1, c0e = after((b1, c0e), y2a, s1["hidden"])
+    y2b = exchange(s2["parts"][1], y2a)
+    c0 = choose(c0e, c0m)
+    c1 = across(c0)
+    qb1 = core(b1)
+    qc0 = core(c0)
+    s3 = forward(b1, qb1, c0, qc0)
+    y3a = exchange(s3["parts"][0], y2b)
+    there0, suma0 = combine(s1, s3["parts"])
+    s2 = backward(s2, (y2a, y2b), s3["parts"])
+
+    q_c1 = core(after(c1, s2["hidden"]))
+    y3b = exchange(s3["parts"][1], y3a, q_c1)
+    r0 = across(after(there0, c1))
+    suma1, sumb0 = combine(s2, c1)
+    ra = across(after(suma1, r0))
+    s4 = forward(c1, q_c1)
+    y4 = exchange(s4["parts"][0], y3b, r0)
+    s3 = backward(s3, (y3a, y3b), s4["parts"])
+    sumb1, sumc0 = combine(s3)
+    from_a = outer_z(add(suma0, ra))
+    rb = across(sumb1)
+    from_c0 = outer_z(sumc0, part=(0, 3))
+    s4 = backward(s4, (y4,), sumb1, ra)
+    (sumc1,) = combine(s4)
+    near_c1, across_c1 = swap(sumc1, 6, (0, 3)), swap(sumc1, 2, (1, 2))
+
+    states = (s0, s1, s2, s3, s4)
+    inputs, scaled, hidden, grad_gate, grad_up = (
+        tuple(s[key] for s in states)
+        for key in ("inputs", "scaled", "hidden", "grad_gate", "grad_up")
+    )
+    gate_grad = outer(after(grad_gate, sumc1), inputs)
+    sumb = add(sumb0, after(rb, gate_grad))
+    from_b = swap(sumb, 8, (0, 3)), swap(sumb, 12, (1, 2))
+    up_grad = outer(after(grad_up, sumb, from_a, from_c0), inputs)
+    sumc = add(sumc0, from_c0, *after((near_c1, across_c1), up_grad))
+    from_c = swap(sumc, 8, (1, 2))
+    down_grad = outer(after(hidden, sumc, *from_b), scaled)
+    total = add(sum0, r0, from_a, *from_b, after(from_c, down_grad))
+    features = tokens.shape[1]
+    by_expert = total[:, features : features + experts].astype(F32)
+    chosen = expert_ids[:, :, None] == jnp.arange(experts, dtype=jnp.int32)[None, None, :]
+    prob_grads = jnp.sum(jnp.where(chosen, by_expert[:, None, :], 0.0), axis=2)
+    return (
+        total[:, :features],
+        prob_grads,
+        gate_grad[None],
+        up_grad[None],
+        down_grad[None],
+    )
+
+
 def solution(mesh):
+    dense = mesh.shape["expert"] == 16 and mesh.shape["dp"] == 2
     return jax.shard_map(
-        local,
+        local_dense if dense else local_general,
         mesh=mesh,
         in_specs=(
             P("expert", "dp"),

time: 614 us -> 249 us (0.41)
  the two profiles are of different devices: /device:TPU:11 before, /device:TPU:0 now
where the time goes in v2:
time: 249 us
  waiting for transfers between devices  125 us (50%)
  Pallas kernels  64.5 us (26%)
  starting transfers between devices  47.4 us (19%)
  local copies, waits for them, and re-layouts  10.2 us (4%)
    ppermute x32, waiting for transfers between devices, swap(): return lax.ppermute(value, 'expert', pairs)  84.1 us
    pallas_call x22, Pallas kernels, kernel_call(): pl.pallas_call(body, in_specs=[pl.BlockSpec(memory_space=pltpu.VMEM)] * l...  44.7 us
    ppermute x8, waiting for transfers between devices, exchange(): return lax.ppermute(after(part, *gates), 'dp', [(0, 1), (1, 0)])  40.8 us
    ppermute x32, starting transfers between devices, swap(): return lax.ppermute(value, 'expert', pairs)  35.1 us
    pallas_call x3, Pallas kernels, outer(): pl.pallas_call(functools.partial(outer_kernel, len(lefts)), grid=(width /...  19.7 us
    ppermute x8, starting transfers between devices, exchange(): return lax.ppermute(after(part, *gates), 'dp', [(0, 1), (1, 0)])  12.3 us
    unnamed x20, local copies, waits for them, and re-layouts  9.35 us
  transfers between devices with their start and end apart: 40, of which 22 were waited for; matrix products, arithmetic and copies ran while one was open for 0% of the time, Pallas kernels for 25%

profile of v2, /device:TPU:0, one launch (start us, length us, event | category | flops | bytes accessed | tf_op | source)
XLA Modules:
  0.0 248.7 jit_solution(12398370941626140861)
XLA Ops:
  5.8 5.4 %collective-permute-start.3 = (bf16[128,4224]{1,0:T(8,128)(2,1)S(1)}, bf16[128,4224]{1,0:T(8,128)(2,1)S(1)}, u32[]{:S(2)}, u32[]{:S(2)}) collective-permute-start(bf16[128,4224]{1,0:T(8,128)(2,1)S(1)} %pack.1.refs_0_), channel_id=1, source_target_pairs={{0,4},{1,5},{2,6},{3,7},{4,0},{5,1},{6,2},{7,3},{8,12},{9,13},{10,... | collective-permute-start | bytes 3244040 | tf_op jit(solution)/shard_map/ppermute | solution.py:362
  18.4 4.3 %front.5 = (bf16[144,2048]{1,0:T(8,128)(2,1)S(1)}, bf16[144,2048]{1,0:T(8,128)(2,1)S(1)}, bf16[256,144]{1,0:T(8,128)(2,1)S(1)}, f32[144,128]{1,0:T(8,128)S(1)}, bf16[136,2304]{1,0:T(8,128)(2,1)S(1)}) custom-call(bf16[128,4224]{1,0:T(8,128)(2,1)S(1)} %pack.1.refs_0_, bf16[128,4224]{1,0:T(8,128)(2,1)S(1)} %collective-permute-done.refs_1_, ...), custom_call_target="tpu_custom_call" | custom-call | flops 1000 | bytes 1000 | tf_op jit(solution)/shard_map/front/pallas_call | solution.py:117
  24.3 11.2 %collective-permute-done.3.refs_2_ = bf16[128,4224]{1,0:T(8,128)(2,1)S(1)} collective-permute-done((bf16[128,4224]{1,0:T(8,128)(2,1)S(1)}, bf16[128,4224]{1,0:T(8,128)(2,1)S(1)}, u32[]{:S(2)}, u32[]{:S(2)}) %collective-permute-start.3) | collective-permute-done | bytes 1081376 | tf_op jit(solution)/shard_map/ppermute | solution.py:362
  42.7 5.5 %front.6 = (bf16[272,2048]{1,0:T(8,128)(2,1)S(1)}, bf16[272,2048]{1,0:T(8,128)(2,1)S(1)}, bf16[512,272]{1,0:T(8,128)(2,1)S(1)}, f32[272,128]{1,0:T(8,128)S(1)}, ...) custom-call(bf16[128,4224]{1,0:T(8,128)(2,1)S(1)} %collective-permute-done.2.refs_0_, ...), custom_call_target="tpu_custom_call" | custom-call | flops 1000 | bytes 1000 | tf_op jit(solution)/shard_map/front/pallas_call | solution.py:117
  52.0 12.7 %collective-permute-done.9.first = bf16[128,4224]{1,0:T(8,128)(2,1)S(1)} collective-permute-done((bf16[128,4224]{1,0:T(8,128)(2,1)S(1)}, bf16[128,4224]{1,0:T(8,128)(2,1)S(1)}, u32[]{:S(2)}, u32[]{:S(2)}) %collective-permute-start.9) | collective-permute-done | bytes 1081376 | tf_op jit(solution)/shard_map/ppermute | solution.py:362
  71.5 5.5 %front.7 = (bf16[272,2048]{1,0:T(8,128)(2,1)S(1)}, bf16[272,2048]{1,0:T(8,128)(2,1)S(1)}, bf16[512,272]{1,0:T(8,128)(2,1)S(1)}, f32[272,128]{1,0:T(8,128)S(1)}, ...) custom-call(bf16[128,4224]{1,0:T(8,128)(2,1)S(1)} %collective-permute-done.8.refs_0_, ...), custom_call_target="tpu_custom_call" | custom-call | flops 1000 | bytes 1000 | tf_op jit(solution)/shard_map/front/pallas_call | solution.py:117
  77.0 5.5 %collective-permute-done.14.refs_3_ = bf16[136,2304]{1,0:T(8,128)(2,1)S(1)} collective-permute-done((bf16[136,2304]{1,0:T(8,128)(2,1)S(1)}, bf16[136,2304]{1,0:T(8,128)(2,1)S(1)}, u32[]{:S(2)}, u32[]{:S(2)}) %collective-permute-start.14) | collective-permute-done | bytes 626720 | tf_op jit(solution)/shard_map/ppermute | solution.py:376
  88.2 5.3 %collective-permute-done.16.refs_0_ = bf16[128,4224]{1,0:T(8,128)(2,1)S(1)} collective-permute-done((bf16[128,4224]{1,0:T(8,128)(2,1)S(1)}, bf16[128,4224]{1,0:T(8,128)(2,1)S(1)}, u32[]{:S(2)}, u32[]{:S(2)}) %collective-permute-start.16) | collective-permute-done | bytes 1081376 | tf_op jit(solution)/shard_map/ppermute | solution.py:362
  102.4 5.5 %front.8 = (bf16[272,2048]{1,0:T(8,128)(2,1)S(1)}, bf16[272,2048]{1,0:T(8,128)(2,1)S(1)}, bf16[512,272]{1,0:T(8,128)(2,1)S(1)}, f32[272,128]{1,0:T(8,128)S(1)}, ...) custom-call(bf16[128,4224]{1,0:T(8,128)(2,1)S(1)} %collective-permute-done.16.refs_0_, ...), custom_call_target="tpu_custom_call" | custom-call | flops 1000 | bytes 1000 | tf_op jit(solution)/shard_map/front/pallas_call | solution.py:117
  107.9 7.1 %collective-permute-done.23.refs_3_ = bf16[136,2304]{1,0:T(8,128)(2,1)S(1)} collective-permute-done((bf16[136,2304]{1,0:T(8,128)(2,1)S(1)}, bf16[136,2304]{1,0:T(8,128)(2,1)S(1)}, u32[]{:S(2)}, u32[]{:S(2)}) %collective-permute-start.23) | collective-permute-done | bytes 626720 | tf_op jit(solution)/shard_map/ppermute | solution.py:376
  115.0 4.2 %back.7 = (bf16[272,768]{1,0:T(8,128)(2,1)S(1)}, bf16[272,768]{1,0:T(8,128)(2,1)S(1)}, bf16[272,768]{1,0:T(8,128)(2,1)S(1)}, bf16[256,2176]{1,0:T(8,128)(2,1)S(1)}, bf16[256,2176]{1,0:T(8,128)(2,1)S(1)}) custom-call(f32[272,128]{1,0:T(8,128)S(1)} %get-tuple-element.146.weights, bf16[512,272]{1,0:T(8,128)(2,1)S(1)} %get-tuple-element.147.spread, ...), custom_call_target="tpu_custom_call" | custom-call | flops 1000 | bytes 1000 | tf_op jit(solution)/shard_map/back/pallas_call | solution.py:117
  119.2 5.3 %collective-permute-done.21.refs_0_ = bf16[128,4224]{1,0:T(8,128)(2,1)S(1)} collective-permute-done((bf16[128,4224]{1,0:T(8,128)(2,1)S(1)}, bf16[128,4224]{1,0:T(8,128)(2,1)S(1)}, u32[]{:S(2)}, u32[]{:S(2)}) %collective-permute-start.21) | collective-permute-done | bytes 1081376 | tf_op jit(solution)/shard_map/ppermute | solution.py:362
  126.3 14.8 %collective-permute-done.27.refs_1_ = bf16[136,2304]{1,0:T(8,128)(2,1)S(1)} collective-permute-done((bf16[136,2304]{1,0:T(8,128)(2,1)S(1)}, bf16[136,2304]{1,0:T(8,128)(2,1)S(1)}, u32[]{:S(2)}, u32[]{:S(2)}) %collective-permute-start.27) | collective-permute-done | bytes 626720 | tf_op jit(solution)/shard_map/ppermute | solution.py:376
  143.4 4.3 %front.9 = (bf16[144,2048]{1,0:T(8,128)(2,1)S(1)}, bf16[144,2048]{1,0:T(8,128)(2,1)S(1)}, bf16[256,144]{1,0:T(8,128)(2,1)S(1)}, f32[144,128]{1,0:T(8,128)S(1)}, bf16[136,2304]{1,0:T(8,128)(2,1)S(1)}) custom-call(bf16[128,4224]{1,0:T(8,128)(2,1)S(1)} %collective-permute-done.21.refs_0_, bf16[128,4224]{1,0:T(8,128)(2,1)S(1)} %collective-permute-done.28.refs_1_, ...), custom_call_target="tpu_custom_call" | custom-call | flops 1000 | bytes 1000 | tf_op jit(solution)/shard_map/front/pallas_call | solution.py:117
  147.7 9.1 %collective-permute-done.29.refs_3_ = bf16[136,2304]{1,0:T(8,128)(2,1)S(1)} collective-permute-done((bf16[136,2304]{1,0:T(8,128)(2,1)S(1)}, bf16[136,2304]{1,0:T(8,128)(2,1)S(1)}, u32[]{:S(2)}, u32[]{:S(2)}) %collective-permute-start.29) | collective-permute-done | bytes 626720 | tf_op jit(solution)/shard_map/ppermute | solution.py:376
  164.1 13.6 %collective-permute-done.25.refs_1_ = bf16[128,2176]{1,0:T(8,128)(2,1)S(1)} collective-permute-done((bf16[128,2176]{1,0:T(8,128)(2,1)S(1)}, bf16[128,2176]{1,0:T(8,128)(2,1)S(1)}, u32[]{:S(2)}, u32[]{:S(2)}) %collective-permute-start.25) | collective-permute-done | bytes 557088 | tf_op jit(solution)/shard_map/ppermute | solution.py:362
  186.6 4.2 %collective-permute-start.37 = (bf16[128,2176]{1,0:T(8,128)(2,1)S(1)}, bf16[128,2176]{1,0:T(8,128)(2,1)S(1)}, u32[]{:S(2)}, u32[]{:S(2)}) collective-permute-start(bf16[128,2176]{1,0:T(8,128)(2,1)S(1)} %add.14), channel_id=1, source_target_pairs={{0,6},{1,7},{2,4},{3,5},{12,10},{13,11},{14,8},{15,9},{16,22},{17,... | collective-permute-start | bytes 1671176 | tf_op jit(solution)/shard_map/ppermute | solution.py:362
  190.9 6.6 %outer.3 = bf16[768,2048]{1,0:T(8,128)(2,1)} custom-call(bf16[144,768]{1,0:T(8,128)(2,1)S(1)} %get-tuple-element.180.refs_0_, bf16[272,768]{1,0:T(8,128)(2,1)S(1)} %get-tuple-element.181.refs_1_, bf16[272,768]{1,0:T(8,128)(2,1)S(1)} %get-tuple-element.182.refs_2_, bf16[272,768]{1,0:T(8,128)(2,1)S(1)} %get-tuple-element.183.refs_3_, ...), custom_call_target="tpu_custom_call" | custom-call | flops 1000 | bytes 1000 | tf_op jit(solution)/shard_map/outer/pallas_call | solution.py:311
  198.3 10.4 %collective-permute-done.36.refs_1_ = bf16[128,2176]{1,0:T(8,128)(2,1)S(1)} collective-permute-done((bf16[128,2176]{1,0:T(8,128)(2,1)S(1)}, bf16[128,2176]{1,0:T(8,128)(2,1)S(1)}, u32[]{:S(2)}, u32[]{:S(2)}) %collective-permute-start.36) | collective-permute-done | bytes 557088 | tf_op jit(solution)/shard_map/ppermute | solution.py:362
  208.7 5.4 %collective-permute-start.34 = (bf16[128,2176]{1,0:T(8,128)(2,1)S(1)}, bf16[128,2176]{1,0:T(8,128)(2,1)S(1)}, u32[]{:S(2)}, u32[]{:S(2)}) collective-permute-start(bf16[128,2176]{1,0:T(8,128)(2,1)S(1)} %add.15), channel_id=1, source_target_pairs={{0,8},{1,9},{2,10},{3,11},{12,4},{13,5},{14,6},{15,7},{16,24},{17,... | collective-permute-start | bytes 1671176 | tf_op jit(solution)/shard_map/ppermute | solution.py:362
  214.2 6.6 %outer.4 = bf16[768,2048]{1,0:T(8,128)(2,1)} custom-call(bf16[144,768]{1,0:T(8,128)(2,1)S(1)} %get-tuple-element.197.refs_0_, bf16[272,768]{1,0:T(8,128)(2,1)S(1)} %get-tuple-element.198.refs_1_, bf16[272,768]{1,0:T(8,128)(2,1)S(1)} %get-tuple-element.199.refs_2_, bf16[272,768]{1,0:T(8,128)(2,1)S(1)} %get-tuple-element.200.refs_3_, ...), custom_call_target="tpu_custom_call" | custom-call | flops 1000 | bytes 1000 | tf_op jit(solution)/shard_map/outer/pallas_call | solution.py:311
  222.5 9.4 %collective-permute-done.34.refs_3_ = bf16[128,2176]{1,0:T(8,128)(2,1)S(1)} collective-permute-done((bf16[128,2176]{1,0:T(8,128)(2,1)S(1)}, bf16[128,2176]{1,0:T(8,128)(2,1)S(1)}, u32[]{:S(2)}, u32[]{:S(2)}) %collective-permute-start.34) | collective-permute-done | bytes 557088 | tf_op jit(solution)/shard_map/ppermute | solution.py:362
  231.9 6.6 %outer.5 = bf16[768,2048]{1,0:T(8,128)(2,1)} custom-call(bf16[144,768]{1,0:T(8,128)(2,1)S(1)} %get-tuple-element.206.refs_0_, bf16[272,768]{1,0:T(8,128)(2,1)S(1)} %get-tuple-element.207.refs_1_, bf16[272,768]{1,0:T(8,128)(2,1)S(1)} %get-tuple-element.208.refs_2_, bf16[272,768]{1,0:T(8,128)(2,1)S(1)} %get-tuple-element.209.refs_3_, ...), custom_call_target="tpu_custom_call" | custom-call | flops 1000 | bytes 1000 | tf_op jit(solution)/shard_map/outer/pallas_call | solution.py:311
  238.4 8.3 %collective-permute-done.39.refs_5_ = bf16[128,2176]{1,0:T(8,128)(2,1)S(1)} collective-permute-done((bf16[128,2176]{1,0:T(8,128)(2,1)S(1)}, bf16[128,2176]{1,0:T(8,128)(2,1)S(1)}, u32[]{:S(2)}, u32[]{:S(2)}) %collective-permute-start.39) | collective-permute-done | bytes 557088 | tf_op jit(solution)/shard_map/ppermute | solution.py:362
  (105 shorter events, 71.0 us)
Async XLA Ops:
  5.1 19.2 %collective-permute-start.4 = (bf16[128,4224]{1,0:T(8,128)(2,1)S(1)}, bf16[128,4224]{1,0:T(8,128)(2,1)S(1)}, u32[]{:S(2)}, u32[]{:S(2)}) collective-permute-start(bf16[128,4224]{1,0:T(8,128)(2,1)S(1)} %pack.1.refs_0_), channel_id=1, source_target_pairs={{4,8},{5,9},{6,10},{7,11},{8,4},{9,5},{10,6},{11,7},{20,24},{21,25... | collective-permute-start | bytes 3244040 | tf_op jit(solution)/shard_map/ppermute | solution.py:362
  5.8 29.6 %collective-permute-start.3 = (bf16[128,4224]{1,0:T(8,128)(2,1)S(1)}, bf16[128,4224]{1,0:T(8,128)(2,1)S(1)}, u32[]{:S(2)}, u32[]{:S(2)}) collective-permute-start(bf16[128,4224]{1,0:T(8,128)(2,1)S(1)} %pack.1.refs_0_), channel_id=1, source_target_pairs={{0,4},{1,5},{2,6},{3,7},{4,0},{5,1},{6,2},{7,3},{8,12},{9,13},{10,... | collective-permute-start | bytes 3244040 | tf_op jit(solution)/shard_map/ppermute | solution.py:362
  11.3 25.7 %collective-permute-start.2 = (bf16[128,4224]{1,0:T(8,128)(2,1)S(1)}, bf16[128,4224]{1,0:T(8,128)(2,1)S(1)}, u32[]{:S(2)}, u32[]{:S(2)}) collective-permute-start(bf16[128,4224]{1,0:T(8,128)(2,1)S(1)} %pack.1.refs_0_), channel_id=1, source_target_pairs={{0,2},{1,3},{2,0},{3,1},{4,6},{5,7},{6,4},{7,5},{8,10},{9,11},{10,... | collective-permute-start | bytes 3244040 | tf_op jit(solution)/shard_map/ppermute | solution.py:362
  38.9 25.8 %collective-permute-start.9 = (bf16[128,4224]{1,0:T(8,128)(2,1)S(1)}, bf16[128,4224]{1,0:T(8,128)(2,1)S(1)}, u32[]{:S(2)}, u32[]{:S(2)}) collective-permute-start(bf16[128,4224]{1,0:T(8,128)(2,1)S(1)} %collective-permute-done.4.second), channel_id=1, source_target_pairs={{0,4},{1,5},{2,6},{3,7},{4,0},{5,1},{6,2},{7,3},{8,12},{9,13},{10,... | collective-permute-start | bytes 3244040 | tf_op jit(solution)/shard_map/ppermute | solution.py:362
  39.3 25.4 %collective-permute-start.10 = (bf16[128,4224]{1,0:T(8,128)(2,1)S(1)}, bf16[128,4224]{1,0:T(8,128)(2,1)S(1)}, u32[]{:S(2)}, u32[]{:S(2)}) collective-permute-start(bf16[128,4224]{1,0:T(8,128)(2,1)S(1)} %collective-permute-done.3.refs_2_), channel_id=1, source_target_pairs={{4,8},{5,9},{6,10},{7,11},{8,4},{9,5},{10,6},{11,7},{20,24},{21,25... | collective-permute-start | bytes 3244040 | tf_op jit(solution)/shard_map/ppermute | solution.py:362
  40.0 25.6 %collective-permute-start.8 = (bf16[128,4224]{1,0:T(8,128)(2,1)S(1)}, bf16[128,4224]{1,0:T(8,128)(2,1)S(1)}, u32[]{:S(2)}, u32[]{:S(2)}) collective-permute-start(bf16[128,4224]{1,0:T(8,128)(2,1)S(1)} %collective-permute-done.3.refs_2_), channel_id=1, source_target_pairs={{0,2},{1,3},{2,0},{3,1},{4,6},{5,7},{6,4},{7,5},{8,10},{9,11},{10,... | collective-permute-start | bytes 3244040 | tf_op jit(solution)/shard_map/ppermute | solution.py:362
  48.2 17.4 %collective-permute-start.11 = (bf16[136,2304]{1,0:T(8,128)(2,1)S(1)}, bf16[136,2304]{1,0:T(8,128)(2,1)S(1)}, u32[]{:S(2)}, u32[]{:S(2)}) collective-permute-start(bf16[136,2304]{1,0:T(8,128)(2,1)S(1)} %get-tuple-element.116.refs_0_), channel_id=1, source_target_pairs={{0,16},{16,0},{1,17},{17,1},{2,18},{18,2},{3,19},{19,3},{4,20},{20... | collective-permute-start | bytes 1880072 | tf_op jit(solution)/shard_map/ppermute | solution.py:376
  67.9 25.6 %collective-permute-start.16 = (bf16[128,4224]{1,0:T(8,128)(2,1)S(1)}, bf16[128,4224]{1,0:T(8,128)(2,1)S(1)}, u32[]{:S(2)}, u32[]{:S(2)}) collective-permute-start(bf16[128,4224]{1,0:T(8,128)(2,1)S(1)} %choose.2.refs_2_), channel_id=1, source_target_pairs={{0,2},{1,3},{2,0},{3,1},{4,6},{5,7},{6,4},{7,5},{8,10},{9,11},{10,... | collective-permute-start | bytes 3244040 | tf_op jit(solution)/shard_map/ppermute | solution.py:362
  68.5 26.6 %collective-permute-start.17 = (bf16[128,4224]{1,0:T(8,128)(2,1)S(1)}, bf16[128,4224]{1,0:T(8,128)(2,1)S(1)}, u32[]{:S(2)}, u32[]{:S(2)}) collective-permute-start(bf16[128,4224]{1,0:T(8,128)(2,1)S(1)} %collective-permute-done.10.second), channel_id=1, source_target_pairs={{0,4},{1,5},{2,6},{3,7},{4,0},{5,1},{6,2},{7,3},{8,12},{9,13},{10,... | collective-permute-start | bytes 3244040 | tf_op jit(solution)/shard_map/ppermute | solution.py:362
  98.7 25.8 %collective-permute-start.21 = (bf16[128,4224]{1,0:T(8,128)(2,1)S(1)}, bf16[128,4224]{1,0:T(8,128)(2,1)S(1)}, u32[]{:S(2)}, u32[]{:S(2)}) collective-permute-start(bf16[128,4224]{1,0:T(8,128)(2,1)S(1)} %choose.3.refs_2_), channel_id=1, source_target_pairs={{0,2},{1,3},{2,0},{3,1},{4,6},{5,7},{6,4},{7,5},{8,10},{9,11},{10,... | collective-permute-start | bytes 3244040 | tf_op jit(solution)/shard_map/ppermute | solution.py:362
  124.5 16.5 %collective-permute-start.28 = (bf16[128,4224]{1,0:T(8,128)(2,1)S(1)}, bf16[128,4224]{1,0:T(8,128)(2,1)S(1)}, u32[]{:S(2)}, u32[]{:S(2)}) collective-permute-start(bf16[128,4224]{1,0:T(8,128)(2,1)S(1)} %collective-permute-done.21.refs_0_), channel_id=1, source_target_pairs={{0,1},{1,0},{2,3},{3,2},{4,5},{5,4},{6,7},{7,6},{8,9},{9,8},{10,11... | collective-permute-start | bytes 3244040 | tf_op jit(solution)/shard_map/ppermute | solution.py:362
  126.0 16.5 %collective-permute-start.15 = (bf16[256,2176]{1,0:T(8,128)(2,1)S(1)}, bf16[256,2176]{1,0:T(8,128)(2,1)S(1)}, u32[]{:S(2)}, u32[]{:S(2)}) collective-permute-start(bf16[256,2176]{1,0:T(8,128)(2,1)S(1)} %get-tuple-element.134), channel_id=1, source_target_pairs={{0,1},{1,0},{2,3},{3,2},{4,5},{5,4},{6,7},{7,6},{8,9},{9,8},{10,11... | collective-permute-start | bytes 3342344 | tf_op jit(solution)/shard_map/ppermute | solution.py:362
  142.6 20.1 %collective-permute-start.24 = (bf16[256,2176]{1,0:T(8,128)(2,1)S(1)}, bf16[256,2176]{1,0:T(8,128)(2,1)S(1)}, u32[]{:S(2)}, u32[]{:S(2)}) collective-permute-start(bf16[256,2176]{1,0:T(8,128)(2,1)S(1)} %get-tuple-element.152), channel_id=1, source_target_pairs={{0,1},{1,0},{2,3},{3,2},{4,5},{5,4},{6,7},{7,6},{8,9},{9,8},{10,11... | collective-permute-start | bytes 3342344 | tf_op jit(solution)/shard_map/ppermute | solution.py:362
  142.8 18.2 %collective-permute-start.22 = (bf16[128,2176]{1,0:T(8,128)(2,1)S(1)}, bf16[128,2176]{1,0:T(8,128)(2,1)S(1)}, u32[]{:S(2)}, u32[]{:S(2)}) collective-permute-start(bf16[128,2176]{1,0:T(8,128)(2,1)S(1)} %get-tuple-element.144), channel_id=1, source_target_pairs={{0,2},{1,3},{2,0},{3,1},{4,6},{5,7},{6,4},{7,5},{8,10},{9,11},{10,... | collective-permute-start | bytes 1671176 | tf_op jit(solution)/shard_map/ppermute | solution.py:362
  161.1 16.6 %collective-permute-start.32 = (bf16[136,2304]{1,0:T(8,128)(2,1)S(1)}, bf16[136,2304]{1,0:T(8,128)(2,1)S(1)}, u32[]{:S(2)}, u32[]{:S(2)}) collective-permute-start(bf16[136,2304]{1,0:T(8,128)(2,1)S(1)} %get-tuple-element.175.refs_0_), channel_id=1, source_target_pairs={{0,16},{16,0},{1,17},{17,1},{2,18},{18,2},{3,19},{19,3},{4,20},{20... | collective-permute-start | bytes 1880072 | tf_op jit(solution)/shard_map/ppermute | solution.py:376
  180.0 17.4 %collective-permute-start.31 = (bf16[128,2176]{1,0:T(8,128)(2,1)S(1)}, bf16[128,2176]{1,0:T(8,128)(2,1)S(1)}, u32[]{:S(2)}, u32[]{:S(2)}) collective-permute-start(bf16[128,2176]{1,0:T(8,128)(2,1)S(1)} %get-tuple-element.168), channel_id=1, source_target_pairs={{0,2},{1,3},{2,0},{3,1},{4,6},{5,7},{6,4},{7,5},{8,10},{9,11},{10,... | collective-permute-start | bytes 1671176 | tf_op jit(solution)/shard_map/ppermute | solution.py:362
  180.7 16.9 %collective-permute-start.26 = (bf16[128,2176]{1,0:T(8,128)(2,1)S(1)}, bf16[128,2176]{1,0:T(8,128)(2,1)S(1)}, u32[]{:S(2)}, u32[]{:S(2)}) collective-permute-start(bf16[128,2176]{1,0:T(8,128)(2,1)S(1)} %add.12), channel_id=1, source_target_pairs={{0,4},{1,5},{2,6},{3,7},{4,0},{5,1},{6,2},{7,3},{8,12},{9,13},{10,... | collective-permute-start | bytes 1671176 | tf_op jit(solution)/shard_map/ppermute | solution.py:362
  183.8 24.9 %collective-permute-start.36 = (bf16[128,2176]{1,0:T(8,128)(2,1)S(1)}, bf16[128,2176]{1,0:T(8,128)(2,1)S(1)}, u32[]{:S(2)}, u32[]{:S(2)}) collective-permute-start(bf16[128,2176]{1,0:T(8,128)(2,1)S(1)} %get-tuple-element.191.refs_0_), channel_id=1, source_target_pairs={{0,4},{1,5},{2,6},{3,7},{12,8},{13,9},{14,10},{15,11},{16,20},{17,... | collective-permute-start | bytes 1671176 | tf_op jit(solution)/shard_map/ppermute | solution.py:362
  185.9 34.8 %collective-permute-start.38 = (bf16[128,2176]{1,0:T(8,128)(2,1)S(1)}, bf16[128,2176]{1,0:T(8,128)(2,1)S(1)}, u32[]{:S(2)}, u32[]{:S(2)}) collective-permute-start(bf16[128,2176]{1,0:T(8,128)(2,1)S(1)} %add.14), channel_id=1, source_target_pairs={{4,6},{5,7},{6,4},{7,5},{8,10},{9,11},{10,8},{11,9},{20,22},{21,23... | collective-permute-start | bytes 1671176 | tf_op jit(solution)/shard_map/ppermute | solution.py:362
  186.6 34.1 %collective-permute-start.37 = (bf16[128,2176]{1,0:T(8,128)(2,1)S(1)}, bf16[128,2176]{1,0:T(8,128)(2,1)S(1)}, u32[]{:S(2)}, u32[]{:S(2)}) collective-permute-start(bf16[128,2176]{1,0:T(8,128)(2,1)S(1)} %add.14), channel_id=1, source_target_pairs={{0,6},{1,7},{2,4},{3,5},{12,10},{13,11},{14,8},{15,9},{16,22},{17,... | collective-permute-start | bytes 1671176 | tf_op jit(solution)/shard_map/ppermute | solution.py:362
  197.4 24.9 %collective-permute-start.7 = (bf16[128,2176]{1,0:T(8,128)(2,1)S(1)}, bf16[128,2176]{1,0:T(8,128)(2,1)S(1)}, u32[]{:S(2)}, u32[]{:S(2)}) collective-permute-start(bf16[128,2176]{1,0:T(8,128)(2,1)S(1)} %get-tuple-element.120), channel_id=1, source_target_pairs={{0,1},{1,0},{2,3},{3,2},{4,5},{5,4},{6,7},{7,6},{8,9},{9,8},{10,11... | collective-permute-start | bytes 1671176 | tf_op jit(solution)/shard_map/ppermute | solution.py:362
  197.6 24.9 %collective-permute-start.35 = (bf16[128,2176]{1,0:T(8,128)(2,1)S(1)}, bf16[128,2176]{1,0:T(8,128)(2,1)S(1)}, u32[]{:S(2)}, u32[]{:S(2)}) collective-permute-start(bf16[128,2176]{1,0:T(8,128)(2,1)S(1)} %add.15), channel_id=1, source_target_pairs={{4,8},{5,9},{6,10},{7,11},{8,4},{9,5},{10,6},{11,7},{20,24},{21,25... | collective-permute-start | bytes 1671176 | tf_op jit(solution)/shard_map/ppermute | solution.py:362
  208.7 23.1 %collective-permute-start.34 = (bf16[128,2176]{1,0:T(8,128)(2,1)S(1)}, bf16[128,2176]{1,0:T(8,128)(2,1)S(1)}, u32[]{:S(2)}, u32[]{:S(2)}) collective-permute-start(bf16[128,2176]{1,0:T(8,128)(2,1)S(1)} %add.15), channel_id=1, source_target_pairs={{0,8},{1,9},{2,10},{3,11},{12,4},{13,5},{14,6},{15,7},{16,24},{17,... | collective-permute-start | bytes 1671176 | tf_op jit(solution)/shard_map/ppermute | solution.py:362
  221.1 25.6 %collective-permute-start.39 = (bf16[128,2176]{1,0:T(8,128)(2,1)S(1)}, bf16[128,2176]{1,0:T(8,128)(2,1)S(1)}, u32[]{:S(2)}, u32[]{:S(2)}) collective-permute-start(bf16[128,2176]{1,0:T(8,128)(2,1)S(1)} %add.16), channel_id=1, source_target_pairs={{4,12},{5,13},{6,14},{7,15},{8,0},{9,1},{10,2},{11,3},{20,28},{21,... | collective-permute-start | bytes 1671176 | tf_op jit(solution)/shard_map/ppermute | solution.py:362
  (25 other events, 233.4 us)

commit v3 on v2

--- a/solution.py
+++ b/solution.py
@@ -126,21 +126,30 @@
     )(*operands)
 
 
-def choose_kernel(first, second, out):
+def choose_kernel(cuts, first, second, *outs):
     z_index = lax.div(lax.axis_index("expert"), 4)
     edge = (z_index == 0) | (z_index == 3)
 
+    def write(source):
+        for (start, end), out in zip(cuts, outs):
+            out[...] = source[:, start:end]
+
     @pl.when(edge)
     def _():
-        out[...] = first[...]
+        write(first)
 
     @pl.when(jnp.logical_not(edge))
     def _():
-        out[...] = second[...]
-
-
-def choose(first, second):
-    return kernel_call(choose_kernel, (first, second), [(first.shape, BF16)], name="choose")[0]
+        write(second)
+
+
+def choose(first, second, *cuts):
+    return kernel_call(
+        functools.partial(choose_kernel, cuts),
+        (first, second),
+        [((first.shape[0], end - start), BF16) for start, end in cuts],
+        name="choose",
+    )
 
 
 def tiles(width, tile, body):
@@ -151,8 +160,8 @@
 
 def pack_kernel(tokens, cotangent, probs, ids, out):
     rows, width = tokens.shape
-    out[:, :width] = tokens[...]
-    out[:, width : 2 * width] = cotangent[...]
+    out[:, :width] = cotangent[...]
+    out[:, width : 2 * width] = tokens[...]
     lane = lax.broadcasted_iota(jnp.int32, (rows, LANES), 1)
     routing = jnp.full((rows, LANES), -1.0, F32)
     weights = probs[...].astype(F32)
@@ -167,102 +176,128 @@
     return kernel_call(pack_kernel, operands, [((rows, 2 * width + LANES), BF16)], name="pack")[0]
 
 
-def front_kernel(slots, count, *refs):
+def front_kernel(slots, layout, *refs):
+    sources = refs[: sum(layout)]
+    w_gate, w_up, w_down = refs[len(sources) : len(sources) + 3]
+    *outs, acc, picks = refs[len(sources) + 3 :]
+    units, width = w_gate.shape
+    block = sources[0].shape[0]
+    pairs = len(layout) // 2
+    rows = picks.shape[1]
+    tile = 1024
     expert = lax.axis_index("expert")
-    blocks = refs[:count]
-    w_gate, w_up, w_down = refs[count : count + 3]
-    inputs, scaled, spread, weights, *parts, acc, pick = refs[count + 3 :]
-    units, width = w_gate.shape
-    block = blocks[0].shape[0]
-    rows = pick.shape[0]
+
+    blocks, start = [], 0
+    for size in layout:
+        here = sources[start : start + size]
+        blocks.append((here[0], here[-1], width if size == 1 else 0))
+        start = start + size
+
     lane = lax.broadcasted_iota(jnp.int32, (block, LANES), 1)
     tri = (
         lax.broadcasted_iota(jnp.int32, (block, block), 1)
         <= lax.broadcasted_iota(jnp.int32, (block, block), 0)
     ).astype(BF16)
-    total = jnp.zeros((rows, LANES), F32)
-    for b, source in enumerate(blocks):
-        routing = source[:, 2 * width :].astype(F32)
-        prob = jnp.sum(jnp.where(lane == expert, routing, 0.0), axis=1, keepdims=True)
-        chosen = jnp.broadcast_to(prob >= 0.0, (block, LANES))
-        rank = jnp.dot(tri, chosen.astype(BF16), preferred_element_type=F32)
-        slot = jnp.where(chosen, rank + (slots * b - 1.0), -1.0)
-        spread[pl.ds(b * block, block), :] = (
-            lax.broadcasted_iota(jnp.int32, (block, rows), 1) == slot[:, :1].astype(jnp.int32)
-        ).astype(BF16)
-        slot_row = slot.T[:1, :].astype(jnp.int32)
-        picked = (lax.broadcasted_iota(jnp.int32, (rows, block), 0) == slot_row).astype(BF16)
-        pick[:, pl.ds(b * block, block)] = picked
-        prob = jnp.broadcast_to(jnp.maximum(prob, 0.0), (block, LANES)).astype(BF16)
-        total = total + jnp.dot(picked, prob, preferred_element_type=F32)
-    weights[...] = total
+    for p in range(pairs):
+        spread, weights = outs[5 * p + 2], outs[5 * p + 3]
+        total = jnp.zeros((rows, LANES), F32)
+        for b, (_, source, offset) in enumerate(blocks[2 * p : 2 * p + 2]):
+            routing = source[:, pl.ds(offset + width, LANES)].astype(F32)
+            prob = jnp.sum(jnp.where(lane == expert, routing, 0.0), axis=1, keepdims=True)
+            chosen = jnp.broadcast_to(prob >= 0.0, (block, LANES))
+            rank = jnp.dot(tri, chosen.astype(BF16), preferred_element_type=F32)
+            slot = jnp.where(chosen, rank + (slots * b - 1.0), -1.0)
+            spread[pl.ds(b * block, block), :] = (
+                lax.broadcasted_iota(jnp.int32, (block, rows), 1)
+                == slot[:, :1].astype(jnp.int32)
+            ).astype(BF16)
+            slot_row = slot.T[:1, :].astype(jnp.int32)
+            picked = (lax.broadcasted_iota(jnp.int32, (rows, block), 0) == slot_row).astype(BF16)
+            picks[p, :, pl.ds(b * block, block)] = picked
+            prob = jnp.broadcast_to(jnp.maximum(prob, 0.0), (block, LANES)).astype(BF16)
+            total = total + jnp.dot(picked, prob, preferred_element_type=F32)
+        weights[...] = total
     acc[...] = jnp.zeros(acc.shape, F32)
-    tile = 1024
-
-    def gather(columns):
-        stacked = jnp.concatenate([source[:, columns] for source in blocks], axis=0)
-        return jnp.dot(pick[...], stacked, preferred_element_type=F32)
 
     def step(start):
-        here, there = pl.ds(start, tile), pl.ds(width + start, tile)
-        rows_in = gather(here).astype(BF16)
-        inputs[:, here] = rows_in
+        here = pl.ds(start, tile)
+        rows_in, grads_in = [], []
+        for p in range(pairs):
+            inputs, scaled, _, weights, _ = outs[5 * p : 5 * p + 5]
+            (first_c, first_t, first_at), (second_c, second_t, second_at) = blocks[2 * p : 2 * p + 2]
+            stacked = jnp.concatenate(
+                [
+                    first_t[:, pl.ds(first_at + start, tile)],
+                    second_t[:, pl.ds(second_at + start, tile)],
+                ],
+                axis=0,
+            )
+            picked = jnp.dot(picks[p], stacked, preferred_element_type=F32).astype(BF16)
+            inputs[:, here] = picked
+            rows_in.append(picked)
+            stacked = jnp.concatenate([first_c[:, here], second_c[:, here]], axis=0)
+            picked = jnp.dot(picks[p], stacked, preferred_element_type=F32)
+            scaled[:, here] = (weights[:, :1] * picked).astype(BF16)
+            grads_in.append(picked.astype(BF16))
+        rows_in = jnp.concatenate(rows_in, axis=0)
         acc[:, :units] += contract_last(rows_in, w_gate[:, here])
         acc[:, units : 2 * units] += contract_last(rows_in, w_up[:, here])
-        grads = gather(there)
-        scaled[:, here] = (weights[:, :1] * grads).astype(BF16)
-        acc[:, 2 * units :] += contract_last(grads.astype(BF16), w_down[:, here])
+        acc[:, 2 * units :] += contract_last(jnp.concatenate(grads_in, axis=0), w_down[:, here])
 
     tiles(width, tile, step)
-    for i, part in enumerate(parts):
-        size = part.shape[0]
-        part[...] = acc[i * size : (i + 1) * size].astype(BF16)
+    for p in range(pairs):
+        part = outs[5 * p + 4]
+        part[...] = acc[p * rows : p * rows + part.shape[0]].astype(BF16)
 
 
 def front(blocks, w_gate, w_up, w_down, slots):
-    count, block = len(blocks), blocks[0].shape[0]
+    blocks = [b if isinstance(b, tuple) else (b,) for b in blocks]
+    layout = [len(b) for b in blocks]
+    sources = [array for b in blocks for array in b]
+    block = sources[0].shape[0]
     units, width = w_gate.shape
-    filled = count * slots
-    rows = -(-filled // 16) * 16
-    return kernel_call(
-        functools.partial(front_kernel, slots, count),
-        (*blocks, w_gate, w_up, w_down),
+    pairs = len(blocks) // 2
+    rows = -(-2 * slots // 16) * 16
+    results = kernel_call(
+        functools.partial(front_kernel, slots, layout),
+        (*sources, w_gate, w_up, w_down),
         [
             ((rows, width), BF16),
             ((rows, width), BF16),
-            ((count * block, rows), BF16),
+            ((2 * block, rows), BF16),
             ((rows, LANES), F32),
+            ((2 * slots, 3 * units), BF16),
         ]
-        + [((2 * slots, 3 * units), BF16)] * (count // 2),
-        scratch=[pltpu.VMEM((rows, 3 * units), F32), pltpu.VMEM((rows, count * block), BF16)],
+        * pairs,
+        scratch=[
+            pltpu.VMEM((pairs * rows, 3 * units), F32),
+            pltpu.VMEM((pairs, rows, 2 * block), BF16),
+        ],
         name="front",
     )
-
-
-def back_kernel(block, weights, spread, w_gate, w_up, *refs):
-    expert = lax.axis_index("expert")
-    *shares, hidden, grad_gate, grad_up, keep, send = refs
+    names = ("inputs", "scaled", "spread", "weights", "part")
+    return [dict(zip(names, results[5 * p : 5 * p + 5])) for p in range(pairs)]
+
+
+def back_kernel(own, peer, weights, spread, w_gate, w_up, *refs):
+    hidden, grad_gate, grad_up, keep, send = refs
     units, width = w_gate.shape
-    filled = sum(share.shape[0] for share in shares) // 2
+    filled = own.shape[0]
     tokens, rows = spread.shape
     tile = 1024
+    expert = lax.axis_index("expert")
 
     def place(term, columns):
         placed = jnp.dot(spread[...], term, preferred_element_type=F32).astype(BF16)
-        for b in range(0, tokens // block, 2):
-            here = pl.ds(b // 2 * block, block)
-            keep[here, columns] = placed[b * block : (b + 1) * block]
-            send[here, columns] = placed[(b + 1) * block : (b + 2) * block]
+        keep[:, columns] = placed[: tokens // 2]
+        send[:, columns] = placed[tokens // 2 :]
 
     def value(i):
         columns = pl.ds(i * units, units)
-        total = [
-            own[:, columns].astype(F32) + peer[:, columns].astype(F32)
-            for own, peer in zip(shares[::2], shares[1::2])
-        ]
+        total = own[:, columns].astype(F32) + peer[:, columns].astype(F32)
         if rows > filled:
-            total.append(jnp.zeros((rows - filled, units), F32))
-        return jnp.concatenate(total, axis=0)
+            total = jnp.concatenate([total, jnp.zeros((rows - filled, units), F32)], axis=0)
+        return total
 
     h, gg, gu, prob = activations(value(0), value(1), value(2), weights[:, :1])
     hidden[...] = h
@@ -280,16 +315,17 @@
     tiles(width, tile, step)
 
 
-def back(shares, weights, spread, w_gate, w_up, block):
+def back(state, peer, w_gate, w_up):
     units, width = w_gate.shape
-    tokens, rows = spread.shape
+    tokens, rows = state["spread"].shape
     half = (tokens // 2, width + LANES)
-    return kernel_call(
-        functools.partial(back_kernel, block),
-        (weights, spread, w_gate, w_up, *shares),
+    results = kernel_call(
+        back_kernel,
+        (state["part"], peer, state["weights"], state["spread"], w_gate, w_up),
         [((rows, units), BF16)] * 3 + [(half, BF16)] * 2,
         name="back",
     )
+    return state | dict(zip(("hidden", "grad_gate", "grad_up", "keep", "send"), results))
 
 
 def outer_kernel(count, *refs):
@@ -322,32 +358,36 @@
     )(*lefts, *rights)
 
 
-def add_kernel(block, count, *refs):
-    terms, outs = refs[:count], refs[count:]
-    for i, out in enumerate(outs):
-        rows = pl.ds(i * block, block)
-        total = terms[0][rows, :].astype(F32)
-        for term in terms[1:]:
-            total = total + term[rows, :].astype(F32)
-        out[...] = total.astype(BF16)
-
-
-def add_blocks(block, *terms):
-    rows, width = terms[0].shape
-    return kernel_call(
-        functools.partial(add_kernel, block, len(terms)),
-        terms,
-        [((block, width), BF16)] * (rows // block),
-        name="add",
-    )
+def add_kernel(*refs):
+    *terms, out = refs
+    total = terms[0][...].astype(F32)
+    for term in terms[1:]:
+        total = total + term[...].astype(F32)
+    out[...] = total.astype(BF16)
 
 
 def add(*terms):
-    return add_blocks(terms[0].shape[0], *terms)[0]
-
-
-def after(value, *gates):
-    return lax.optimization_barrier((value, *gates))[0]
+    return kernel_call(add_kernel, terms, [(terms[0].shape, BF16)], name="add")[0]
+
+
+def finish_kernel(*refs):
+    *terms, tokens_out, probs_out = refs
+    total = terms[0][...].astype(F32)
+    for term in terms[1:]:
+        total = total + term[...].astype(F32)
+    width = tokens_out.shape[1]
+    tokens_out[...] = total[:, :width].astype(BF16)
+    probs_out[...] = total[:, width:]
+
+
+def finish(*terms):
+    block, columns = terms[0].shape
+    outs = [((block, columns - LANES), BF16), ((block, LANES), F32)]
+    return kernel_call(finish_kernel, terms, outs, name="finish")
+
+
+def meet(*values):
+    return lax.optimization_barrier(values)
 
 
 def local_dense(tokens, cotangent, router_probs, expert_ids, w_gate, w_up, w_down):
@@ -367,102 +407,109 @@
     inner_z = functools.partial(swap, bits=12, part=(1, 2))
 
     def forward(*blocks):
-        inputs, scaled, spread, weights, *parts = front(
-            blocks, weight_gate, weight_up, weight_down, slots
-        )
-        return dict(inputs=inputs, scaled=scaled, parts=parts, spread=spread, weights=weights)
-
-    def exchange(part, *gates):
-        return lax.ppermute(after(part, *gates), "dp", [(0, 1), (1, 0)])
-
-    def backward(state, peers, *gates):
-        peers = after(peers, *gates)
-        hidden, grad_gate, grad_up, keep, send = back(
-            [share for pair in zip(state["parts"], peers) for share in pair],
-            state["weights"],
-            state["spread"],
-            weight_gate,
-            weight_up,
-            block,
-        )
-        return state | dict(
-            hidden=hidden, grad_gate=grad_gate, grad_up=grad_up, keep=keep, got=core(send)
-        )
-
-    def combine(state, *gates):
-        return add_blocks(block, state["keep"], after(state["got"], *gates))
+        return front(blocks, weight_gate, weight_up, weight_down, slots)
+
+    def exchange(part):
+        return lax.ppermute(part, "dp", [(0, 1), (1, 0)])
+
+    def backward(state, peer):
+        return back(state, peer, weight_gate, weight_up)
+
+    features = tokens.shape[1]
+    all_columns = 2 * features + LANES
 
     p0 = pack(tokens, cotangent, router_probs, expert_ids)
     q0 = core(p0)
     p1, a0, m0 = across(p0), outer_z(p0), inner_z(p0)
-    s0 = forward(p0, q0)
-    y0 = exchange(s0["parts"][0])
-
-    p1, a0, m0 = after((p1, a0, m0), y0)
+    (s0,) = forward(p0, q0)
+    y0 = exchange(s0["part"])
+
+    p1, a0, m0, y0 = meet(p1, a0, m0, y0)
     a1, b0e, c0m = across(a0), outer_z(m0), inner_z(a0)
-    q1 = core(p1)
-    qa0 = core(a0)
-    s1 = forward(p1, q1, a0, qa0)
-    y1a = exchange(s1["parts"][0])
-    s0 = backward(s0, (y0,), s1["parts"])
-
-    a1, b0e, c0m = after((a1, b0e, c0m), y1a, s0["hidden"])
-    y1b = exchange(s1["parts"][1], y1a)
-    b0 = choose(b0e, m0)
+    s1, sa0 = forward(p1, core(p1), a0, core(a0))
+    y1 = exchange(s1["part"])
+    s0 = backward(s0, y0)
+    k0 = core(s0["send"])
+
+    a1, b0e, c0m, sa0["part"], y1, _ = meet(a1, b0e, c0m, sa0["part"], y1, k0)
+    ya0 = exchange(sa0["part"])
+    (b0,) = choose(b0e, m0, (0, all_columns))
     b1, c0e = across(b0), outer_z(c0m)
-    qa1 = core(a1)
-    qb0 = core(b0)
-    s2 = forward(a1, qa1, b0, qb0)
-    y2a = exchange(s2["parts"][0], y1b)
-    (sum0,) = combine(s0, s2["parts"])
-    s1 = backward(s1, (y1a, y1b), s2["parts"])
-
-    b1, c0e = after((b1, c0e), y2a, s1["hidden"])
-    y2b = exchange(s2["parts"][1], y2a)
-    c0 = choose(c0e, c0m)
-    c1 = across(c0)
-    qb1 = core(b1)
-    qc0 = core(c0)
-    s3 = forward(b1, qb1, c0, qc0)
-    y3a = exchange(s3["parts"][0], y2b)
-    there0, suma0 = combine(s1, s3["parts"])
-    s2 = backward(s2, (y2a, y2b), s3["parts"])
-
-    q_c1 = core(after(c1, s2["hidden"]))
-    y3b = exchange(s3["parts"][1], y3a, q_c1)
-    r0 = across(after(there0, c1))
-    suma1, sumb0 = combine(s2, c1)
-    ra = across(after(suma1, r0))
-    s4 = forward(c1, q_c1)
-    y4 = exchange(s4["parts"][0], y3b, r0)
-    s3 = backward(s3, (y3a, y3b), s4["parts"])
-    sumb1, sumc0 = combine(s3)
-    from_a = outer_z(add(suma0, ra))
-    rb = across(sumb1)
-    from_c0 = outer_z(sumc0, part=(0, 3))
-    s4 = backward(s4, (y4,), sumb1, ra)
-    (sumc1,) = combine(s4)
-    near_c1, across_c1 = swap(sumc1, 6, (0, 3)), swap(sumc1, 2, (1, 2))
-
-    states = (s0, s1, s2, s3, s4)
+    sa1, sb0 = forward(a1, core(a1), b0, core(b0))
+    s1 = backward(s1, y1)
+
+    sa1["part"], s1["send"], ya0 = meet(sa1["part"], s1["send"], ya0)
+    ya1 = exchange(sa1["part"])
+    k1 = core(s1["send"])
+    sa0 = backward(sa0, ya0)
+    ka0 = core(sa0["send"])
+
+    b1, c0e, sb0["part"], ya1, k1, ka0 = meet(b1, c0e, sb0["part"], ya1, k1, ka0)
+    yb0 = exchange(sb0["part"])
+    cuts = (0, all_columns), (0, features), (features, all_columns)
+    c0, c0c, c0t = choose(c0e, c0m, *cuts)
+    c1c, c1t = across(c0c), across(c0t)
+    sb1, sc0 = forward(b1, core(b1), c0, core(c0))
+    sa1 = backward(sa1, ya1)
+
+    sb1["part"], sa1["send"], yb0 = meet(sb1["part"], sa1["send"], yb0)
+    yb1 = exchange(sb1["part"])
+    ka1 = core(sa1["send"])
+    qc1 = core(c1c), core(c1t)
+    sb0 = backward(sb0, yb0)
+    kb0 = core(sb0["send"])
+
+    sc0["part"], ka1, yb1, kb0, *qc1 = meet(sc0["part"], ka1, yb1, kb0, *qc1)
+    yc0 = exchange(sc0["part"])
+    ra = across(add(sa1["keep"], ka1))
+    sum1 = add(s1["keep"], k1)
+    sumb0 = add(sb0["keep"], kb0)
+    sb1 = backward(sb1, yb1)
+    kb1 = core(sb1["send"])
+    (sc1,) = forward((c1c, c1t), tuple(qc1))
+
+    sc1["part"], kb1, yc0, ra, sum1, sumb0 = meet(sc1["part"], kb1, yc0, ra, sum1, sumb0)
+    yc1 = exchange(sc1["part"])
+    rb = across(add(sb1["keep"], kb1))
+    from_a = outer_z(add(sa0["keep"], ka0, ra))
+    sc0 = backward(sc0, yc0)
+    kc0 = core(sc0["send"])
+
+    yc1, kc0, rb, from_a = meet(yc1, kc0, rb, from_a)
+    sc1 = backward(sc1, yc1)
+    kc1 = core(sc1["send"])
+    sumc0 = add(sc0["keep"], kc0)
+    sumb = add(sumb0, rb)
+    b_edge, b_middle = swap(sumb, 8, (0, 3)), swap(sumb, 12, (1, 2))
+
+    sumc1 = add(sc1["keep"], kc1)
+    rc = across(sumc1)
+    states = (s0, s1, sa0, sa1, sb0, sb1, sc0, sc1)
     inputs, scaled, hidden, grad_gate, grad_up = (
         tuple(s[key] for s in states)
         for key in ("inputs", "scaled", "hidden", "grad_gate", "grad_up")
     )
-    gate_grad = outer(after(grad_gate, sumc1), inputs)
-    sumb = add(sumb0, after(rb, gate_grad))
-    from_b = swap(sumb, 8, (0, 3)), swap(sumb, 12, (1, 2))
-    up_grad = outer(after(grad_up, sumb, from_a, from_c0), inputs)
-    sumc = add(sumc0, from_c0, *after((near_c1, across_c1), up_grad))
-    from_c = swap(sumc, 8, (1, 2))
-    down_grad = outer(after(hidden, sumc, *from_b), scaled)
-    total = add(sum0, r0, from_a, *from_b, after(from_c, down_grad))
-    features = tokens.shape[1]
-    by_expert = total[:, features : features + experts].astype(F32)
+    grad_gate, _ = meet(grad_gate, sumc1)
+    gate_grad = outer(grad_gate, inputs)
+
+    rc, sum1, _ = meet(rc, sum1, gate_grad)
+    sumc = add(sumc0, rc)
+    c_edge = outer_z(sumc, part=(0, 3))
+    r0 = across(sum1)
+    grad_up, _ = meet(grad_up, sumc)
+    up_grad = outer(grad_up, inputs)
+
+    c_edge, b_edge, b_middle, _ = meet(c_edge, b_edge, b_middle, up_grad)
+    sumc = add(sumc, c_edge)
+    far = swap(sumc, 8, (1, 2))
+    hidden, _ = meet(hidden, sumc)
+    down_grad = outer(hidden, scaled)
+    far, r0, _ = meet(far, r0, down_grad)
+    token_grads, by_expert = finish(s0["keep"], k0, r0, from_a, b_edge, b_middle, far)
     chosen = expert_ids[:, :, None] == jnp.arange(experts, dtype=jnp.int32)[None, None, :]
-    prob_grads = jnp.sum(jnp.where(chosen, by_expert[:, None, :], 0.0), axis=2)
+    prob_grads = jnp.sum(jnp.where(chosen, by_expert[:, None, :experts], 0.0), axis=2)
     return (
-        total[:, :features],
+        token_grads,
         prob_grads,
         gate_grad[None],
         up_grad[None],

time: 249 us -> 214 us (0.86)
  waiting for transfers between devices: 125 us -> 89.4 us
    ppermute x8, waiting for transfers between devices: 40.8 us -> 17.8 us  [exchange(): return lax.ppermute(part, 'dp', [(0, 1), (1, 0)])]
    ppermute x32 -> x36, waiting for transfers between devices: 84.1 us -> 71.6 us  [swap(): return lax.ppermute(value, 'expert', pairs)]
    ppermute x32 -> x36, starting transfers between devices: 35.1 us -> 36.8 us  [swap(): return lax.ppermute(value, 'expert', pairs)]
    pallas_call x22 -> x27, Pallas kernels: 44.7 us -> 44 us  [kernel_call(): pl.pallas_call(body, in_specs=[pl.BlockSpec(memory_space=pltpu.VMEM)] * l...]
  transfers between devices with their start and end apart: 40 -> 44, of which waited for: 22 -> 22; matrix products, arithmetic and copies ran while one was open for 0% -> 0% of each run, Pallas kernels for 25% -> 28%
where the time goes in v3:
time: 214 us; the launch traced here: 213 us
  waiting for transfers between devices  89.4 us (42%)
  Pallas kernels  64 us (30%)
  starting transfers between devices  48.9 us (23%)
  local copies, waits for them, and re-layouts  9.4 us (4%)
    ppermute x36, waiting for transfers between devices, swap(): return lax.ppermute(value, 'expert', pairs)  71.6 us
    pallas_call x27, Pallas kernels, kernel_call(): pl.pallas_call(body, in_specs=[pl.BlockSpec(memory_space=pltpu.VMEM)] * l...  44 us
    ppermute x36, starting transfers between devices, swap(): return lax.ppermute(value, 'expert', pairs)  36.8 us
    pallas_call x3, Pallas kernels, outer(): pl.pallas_call(functools.partial(outer_kernel, len(lefts)), grid=(width /...  20.1 us
    ppermute x8, waiting for transfers between devices, exchange(): return lax.ppermute(part, 'dp', [(0, 1), (1, 0)])  17.8 us
    ppermute x8, starting transfers between devices, exchange(): return lax.ppermute(part, 'dp', [(0, 1), (1, 0)])  12.1 us
    unnamed x20, local copies, waits for them, and re-layouts  9.35 us
  transfers between devices with their start and end apart: 44, of which 22 were waited for; matrix products, arithmetic and copies ran while one was open for 0% of the time, Pallas kernels for 28%

profile of v3, /device:TPU:0, one launch (start us, length us, event | category | flops | bytes accessed | tf_op | source)
XLA Modules:
  0.0 213.3 jit_solution(16277653807999503278)
XLA Ops:
  5.1 2.6 %collective-permute-start.1 = (bf16[128,4224]{1,0:T(8,128)(2,1)S(1)}, bf16[128,4224]{1,0:T(8,128)(2,1)S(1)}, u32[]{:S(2)}, u32[]{:S(2)}) collective-permute-start(bf16[128,4224]{1,0:T(8,128)(2,1)S(1)} %pack.1.refs_0_), channel_id=1, source_target_pairs={{0,2},{1,3},{2,0},{3,1},{4,6},{5,7},{6,4},{7,5},{8,10},{9,11},{10,... | collective-permute-start | bytes 3244040 | tf_op jit(solution)/shard_map/ppermute | solution.py:402
  15.7 4.3 %front.5 = (bf16[144,2048]{1,0:T(8,128)(2,1)S(1)}, bf16[144,2048]{1,0:T(8,128)(2,1)S(1)}, bf16[256,144]{1,0:T(8,128)(2,1)S(1)}, f32[144,128]{1,0:T(8,128)S(1)}, bf16[136,2304]{1,0:T(8,128)(2,1)S(1)}) custom-call(bf16[128,4224]{1,0:T(8,128)(2,1)S(1)} %pack.1.refs_0_, bf16[128,4224]{1,0:T(8,128)(2,1)S(1)} %collective-permute-done.refs_1_, ...), custom_call_target="tpu_custom_call" | custom-call | flops 1000 | bytes 1000 | tf_op jit(solution)/shard_map/front/pallas_call | solution.py:117
  21.5 10.6 %collective-permute-done.1.refs_0_ = bf16[128,4224]{1,0:T(8,128)(2,1)S(1)} collective-permute-done((bf16[128,4224]{1,0:T(8,128)(2,1)S(1)}, bf16[128,4224]{1,0:T(8,128)(2,1)S(1)}, u32[]{:S(2)}, u32[]{:S(2)}) %collective-permute-start.1) | collective-permute-done | bytes 1081376 | tf_op jit(solution)/shard_map/ppermute | solution.py:402
  37.7 5.6 %collective-permute-start.7 = (bf16[128,4224]{1,0:T(8,128)(2,1)S(1)}, bf16[128,4224]{1,0:T(8,128)(2,1)S(1)}, u32[]{:S(2)}, u32[]{:S(2)}) collective-permute-start(bf16[128,4224]{1,0:T(8,128)(2,1)S(1)} %collective-permute-done.3.second), channel_id=1, source_target_pairs={{0,4},{1,5},{2,6},{3,7},{4,0},{5,1},{6,2},{7,3},{8,12},{9,13},{10,... | collective-permute-start | bytes 3244040 | tf_op jit(solution)/shard_map/ppermute | solution.py:402
  43.3 4.7 %front.6 = (bf16[144,2048]{1,0:T(8,128)(2,1)S(1)}, bf16[144,2048]{1,0:T(8,128)(2,1)S(1)}, bf16[256,144]{1,0:T(8,128)(2,1)S(1)}, f32[144,128]{1,0:T(8,128)S(1)}, ...) custom-call(bf16[128,4224]{1,0:T(8,128)(2,1)S(1)} %collective-permut, ...), custom_call_target="tpu_custom_call" | custom-call | flops 1000 | bytes 1000 | tf_op jit(solution)/shard_map/front/pallas_call | solution.py:117
  53.9 8.4 %collective-permute-done.6.refs_0_ = bf16[128,4224]{1,0:T(8,128)(2,1)S(1)} collective-permute-done((bf16[128,4224]{1,0:T(8,128)(2,1)S(1)}, bf16[128,4224]{1,0:T(8,128)(2,1)S(1)}, u32[]{:S(2)}, u32[]{:S(2)}) %collective-permute-start.6) | collective-permute-done | bytes 1081376 | tf_op jit(solution)/shard_map/ppermute | solution.py:402
  62.2 4.5 %collective-permute-done.7.first = bf16[128,4224]{1,0:T(8,128)(2,1)S(1)} collective-permute-done((bf16[128,4224]{1,0:T(8,128)(2,1)S(1)}, bf16[128,4224]{1,0:T(8,128)(2,1)S(1)}, u32[]{:S(2)}, u32[]{:S(2)}) %collective-permute-start.7) | collective-permute-done | bytes 1081376 | tf_op jit(solution)/shard_map/ppermute | solution.py:402
  74.4 4.7 %front.7 = (bf16[144,2048]{1,0:T(8,128)(2,1)S(1)}, bf16[144,2048]{1,0:T(8,128)(2,1)S(1)}, bf16[256,144]{1,0:T(8,128)(2,1)S(1)}, f32[144,128]{1,0:T(8,128)S(1)}, ...) custom-call(bf16[128,4224]{1,0:T(8,128)(2,1)S(1)} %collective-permut, ...), custom_call_target="tpu_custom_call" | custom-call | flops 1000 | bytes 1000 | tf_op jit(solution)/shard_map/front/pallas_call | solution.py:117
  79.2 4.3 %collective-permute-done.16.peer = bf16[136,2304]{1,0:T(8,128)(2,1)S(1)} collective-permute-done((bf16[136,2304]{1,0:T(8,128)(2,1)S(1)}, bf16[136,2304]{1,0:T(8,128)(2,1)S(1)}, u32[]{:S(2)}, u32[]{:S(2)}) %collective-permute-start.16) | collective-permute-done | bytes 626720 | tf_op jit(solution)/shard_map/ppermute | solution.py:413
  87.8 6.7 %collective-permute-done.12.refs_0_ = bf16[128,4224]{1,0:T(8,128)(2,1)S(1)} collective-permute-done((bf16[128,4224]{1,0:T(8,128)(2,1)S(1)}, bf16[128,4224]{1,0:T(8,128)(2,1)S(1)}, u32[]{:S(2)}, u32[]{:S(2)}) %collective-permute-start.12) | collective-permute-done | bytes 1081376 | tf_op jit(solution)/shard_map/ppermute | solution.py:402
  95.7 3.1 %collective-permute-done.17.peer = bf16[136,2304]{1,0:T(8,128)(2,1)S(1)} collective-permute-done((bf16[136,2304]{1,0:T(8,128)(2,1)S(1)}, bf16[136,2304]{1,0:T(8,128)(2,1)S(1)}, u32[]{:S(2)}, u32[]{:S(2)}) %collective-permute-start.17) | collective-permute-done | bytes 626720 | tf_op jit(solution)/shard_map/ppermute | solution.py:413
  105.5 4.7 %front.8 = (bf16[144,2048]{1,0:T(8,128)(2,1)S(1)}, bf16[144,2048]{1,0:T(8,128)(2,1)S(1)}, bf16[256,144]{1,0:T(8,128)(2,1)S(1)}, f32[144,128]{1,0:T(8,128)S(1)}, ...) custom-call(bf16[128,4224]{1,0:T(8,128)(2,1)S(1)} %collective-permut, ...), custom_call_target="tpu_custom_call" | custom-call | flops 1000 | bytes 1000 | tf_op jit(solution)/shard_map/front/pallas_call | solution.py:117
  110.2 5.6 %collective-permute-done.22.peer = bf16[136,2304]{1,0:T(8,128)(2,1)S(1)} collective-permute-done((bf16[136,2304]{1,0:T(8,128)(2,1)S(1)}, bf16[136,2304]{1,0:T(8,128)(2,1)S(1)}, u32[]{:S(2)}, u32[]{:S(2)}) %collective-permute-start.22) | collective-permute-done | bytes 626720 | tf_op jit(solution)/shard_map/ppermute | solution.py:413
  120.2 6.6 %collective-permute-done.26.refs_0_ = bf16[128,2048]{1,0:T(8,128)(2,1)S(1)} collective-permute-done((bf16[128,2048]{1,0:T(8,128)(2,1)S(1)}, bf16[128,2048]{1,0:T(8,128)(2,1)S(1)}, u32[]{:S(2)}, u32[]{:S(2)}) %collective-permute-start.26) | collective-permute-done | bytes 524320 | tf_op jit(solution)/shard_map/ppermute | solution.py:402
  136.9 4.3 %front.9 = (bf16[144,2048]{1,0:T(8,128)(2,1)S(1)}, bf16[144,2048]{1,0:T(8,128)(2,1)S(1)}, bf16[256,144]{1,0:T(8,128)(2,1)S(1)}, f32[144,128]{1,0:T(8,128)S(1)}, bf16[136,2304]{1,0:T(8,128)(2,1)S(1)}) custom-call(bf16[128,2048]{1,0:T(8,128)(2,1)S(1)} %collective-permute-done.26.refs_0_, bf16[128,2176]{1,0:T(8,128)(2,1)S(1)} %collective-permute-done.28.refs_1_, ...), custom_call_target="tpu_custom_call" | custom-call | flops 1000 | bytes 1000 | tf_op jit(solution)/shard_map/front/pallas_call | solution.py:117
  141.2 4.1 %collective-permute-done.32.refs_2_ = bf16[128,2176]{1,0:T(8,128)(2,1)S(1)} collective-permute-done((bf16[128,2176]{1,0:T(8,128)(2,1)S(1)}, bf16[128,2176]{1,0:T(8,128)(2,1)S(1)}, u32[]{:S(2)}, u32[]{:S(2)}) %collective-permute-start.32) | collective-permute-done | bytes 557088 | tf_op jit(solution)/shard_map/ppermute | solution.py:402
  152.8 6.0 %collective-permute-done.36.refs_3_ = bf16[128,2176]{1,0:T(8,128)(2,1)S(1)} collective-permute-done((bf16[128,2176]{1,0:T(8,128)(2,1)S(1)}, bf16[128,2176]{1,0:T(8,128)(2,1)S(1)}, u32[]{:S(2)}, u32[]{:S(2)}) %collective-permute-start.36) | collective-permute-done | bytes 557088 | tf_op jit(solution)/shard_map/ppermute | solution.py:402
  166.4 3.6 %collective-permute-start.40 = (bf16[128,2176]{1,0:T(8,128)(2,1)S(1)}, bf16[128,2176]{1,0:T(8,128)(2,1)S(1)}, u32[]{:S(2)}, u32[]{:S(2)}) collective-permute-start(bf16[128,2176]{1,0:T(8,128)(2,1)S(1)} %add.18), channel_id=1, source_target_pairs={{0,8},{1,9},{2,10},{3,11},{12,4},{13,5},{14,6},{15,7},{16,24},{17,... | collective-permute-start | bytes 1671176 | tf_op jit(solution)/shard_map/ppermute | solution.py:402
  171.1 6.7 %outer.3 = bf16[768,2048]{1,0:T(8,128)(2,1)} custom-call(bf16[144,768]{1,0:T(8,128)(2,1)S(1)} %get-tuple-element.243.refs_0_, bf16[144,768]{1,0:T(8,128)(2,1)S(1)} %get-tuple-element.244.refs_1_, bf16[144,768]{1,0:T(8,128)(2,1)S(1)} %get-tuple-element.245.refs_2_, bf16[144,768]{1,0:T(8,128)(2,1)S(1)} %get-tuple-element.246.refs_3_, ...), custom_call_target="tpu_custom_call" | custom-call | flops 1000 | bytes 1000 | tf_op jit(solution)/shard_map/outer/pallas_call | solution.py:347
  179.6 2.4 %collective-permute-start.39 = (bf16[128,2176]{1,0:T(8,128)(2,1)S(1)}, bf16[128,2176]{1,0:T(8,128)(2,1)S(1)}, u32[]{:S(2)}, u32[]{:S(2)}) collective-permute-start(bf16[128,2176]{1,0:T(8,128)(2,1)S(1)} %add.17.refs_0_), channel_id=1, source_target_pairs={{0,4},{1,5},{2,6},{3,7},{12,8},{13,9},{14,10},{15,11},{16,20},{17,... | collective-permute-start | bytes 1671176 | tf_op jit(solution)/shard_map/ppermute | solution.py:402
  183.6 6.7 %outer.4 = bf16[768,2048]{1,0:T(8,128)(2,1)} custom-call(bf16[144,768]{1,0:T(8,128)(2,1)S(1)} %get-tuple-element.270.refs_0_, bf16[144,768]{1,0:T(8,128)(2,1)S(1)} %get-tuple-element.271.refs_1_, bf16[144,768]{1,0:T(8,128)(2,1)S(1)} %get-tuple-element.272.refs_2_, bf16[144,768]{1,0:T(8,128)(2,1)S(1)} %get-tuple-element.273.refs_3_, ...), custom_call_target="tpu_custom_call" | custom-call | flops 1000 | bytes 1000 | tf_op jit(solution)/shard_map/outer/pallas_call | solution.py:347
  190.2 3.6 %collective-permute-done.39.refs_1_ = bf16[128,2176]{1,0:T(8,128)(2,1)S(1)} collective-permute-done((bf16[128,2176]{1,0:T(8,128)(2,1)S(1)}, bf16[128,2176]{1,0:T(8,128)(2,1)S(1)}, u32[]{:S(2)}, u32[]{:S(2)}) %collective-permute-start.39) | collective-permute-done | bytes 557088 | tf_op jit(solution)/shard_map/ppermute | solution.py:402
  195.3 6.7 %outer.5 = bf16[768,2048]{1,0:T(8,128)(2,1)} custom-call(bf16[144,768]{1,0:T(8,128)(2,1)S(1)} %get-tuple-element.288.refs_0_, bf16[144,768]{1,0:T(8,128)(2,1)S(1)} %get-tuple-element.289.refs_1_, bf16[144,768]{1,0:T(8,128)(2,1)S(1)} %get-tuple-element.290.refs_2_, bf16[144,768]{1,0:T(8,128)(2,1)S(1)} %get-tuple-element.291.refs_3_, ...), custom_call_target="tpu_custom_call" | custom-call | flops 1000 | bytes 1000 | tf_op jit(solution)/shard_map/outer/pallas_call | solution.py:347
  202.0 9.4 %collective-permute-done.42.refs_6_ = bf16[128,2176]{1,0:T(8,128)(2,1)S(1)} collective-permute-done((bf16[128,2176]{1,0:T(8,128)(2,1)S(1)}, bf16[128,2176]{1,0:T(8,128)(2,1)S(1)}, u32[]{:S(2)}, u32[]{:S(2)}) %collective-permute-start.42) | collective-permute-done | bytes 557088 | tf_op jit(solution)/shard_map/ppermute | solution.py:402
  (116 shorter events, 82.5 us)
Async XLA Ops:
  5.1 27.0 %collective-permute-start.1 = (bf16[128,4224]{1,0:T(8,128)(2,1)S(1)}, bf16[128,4224]{1,0:T(8,128)(2,1)S(1)}, u32[]{:S(2)}, u32[]{:S(2)}) collective-permute-start(bf16[128,4224]{1,0:T(8,128)(2,1)S(1)} %pack.1.refs_0_), channel_id=1, source_target_pairs={{0,2},{1,3},{2,0},{3,1},{4,6},{5,7},{6,4},{7,5},{8,10},{9,11},{10,... | collective-permute-start | bytes 3244040 | tf_op jit(solution)/shard_map/ppermute | solution.py:402
  7.7 25.9 %collective-permute-start.2 = (bf16[128,4224]{1,0:T(8,128)(2,1)S(1)}, bf16[128,4224]{1,0:T(8,128)(2,1)S(1)}, u32[]{:S(2)}, u32[]{:S(2)}) collective-permute-start(bf16[128,4224]{1,0:T(8,128)(2,1)S(1)} %pack.1.refs_0_), channel_id=1, source_target_pairs={{0,4},{1,5},{2,6},{3,7},{4,0},{5,1},{6,2},{7,3},{8,12},{9,13},{10,... | collective-permute-start | bytes 3244040 | tf_op jit(solution)/shard_map/ppermute | solution.py:402
  9.3 24.4 %collective-permute-start.3 = (bf16[128,4224]{1,0:T(8,128)(2,1)S(1)}, bf16[128,4224]{1,0:T(8,128)(2,1)S(1)}, u32[]{:S(2)}, u32[]{:S(2)}) collective-permute-start(bf16[128,4224]{1,0:T(8,128)(2,1)S(1)} %pack.1.refs_0_), channel_id=1, source_target_pairs={{4,8},{5,9},{6,10},{7,11},{8,4},{9,5},{10,6},{11,7},{20,24},{21,25... | collective-permute-start | bytes 3244040 | tf_op jit(solution)/shard_map/ppermute | solution.py:402
  20.0 16.0 %collective-permute-start.4 = (bf16[136,2304]{1,0:T(8,128)(2,1)S(1)}, bf16[136,2304]{1,0:T(8,128)(2,1)S(1)}, u32[]{:S(2)}, u32[]{:S(2)}) collective-permute-start(bf16[136,2304]{1,0:T(8,128)(2,1)S(1)} %get-tuple-element.158.own), channel_id=1, source_target_pairs={{0,16},{16,0},{1,17},{17,1},{2,18},{18,2},{3,19},{19,3},{4,20},{20... | collective-permute-start | bytes 1880072 | tf_op jit(solution)/shard_map/ppermute | solution.py:413
  36.5 25.8 %collective-permute-start.6 = (bf16[128,4224]{1,0:T(8,128)(2,1)S(1)}, bf16[128,4224]{1,0:T(8,128)(2,1)S(1)}, u32[]{:S(2)}, u32[]{:S(2)}) collective-permute-start(bf16[128,4224]{1,0:T(8,128)(2,1)S(1)} %collective-permute-done.2.refs_2_), channel_id=1, source_target_pairs={{0,2},{1,3},{2,0},{3,1},{4,6},{5,7},{6,4},{7,5},{8,10},{9,11},{10,... | collective-permute-start | bytes 3244040 | tf_op jit(solution)/shard_map/ppermute | solution.py:402
  37.0 25.2 %collective-permute-start.8 = (bf16[128,4224]{1,0:T(8,128)(2,1)S(1)}, bf16[128,4224]{1,0:T(8,128)(2,1)S(1)}, u32[]{:S(2)}, u32[]{:S(2)}) collective-permute-start(bf16[128,4224]{1,0:T(8,128)(2,1)S(1)} %collective-permute-done.2.refs_2_), channel_id=1, source_target_pairs={{4,8},{5,9},{6,10},{7,11},{8,4},{9,5},{10,6},{11,7},{20,24},{21,25... | collective-permute-start | bytes 3244040 | tf_op jit(solution)/shard_map/ppermute | solution.py:402
  37.7 29.0 %collective-permute-start.7 = (bf16[128,4224]{1,0:T(8,128)(2,1)S(1)}, bf16[128,4224]{1,0:T(8,128)(2,1)S(1)}, u32[]{:S(2)}, u32[]{:S(2)}) collective-permute-start(bf16[128,4224]{1,0:T(8,128)(2,1)S(1)} %collective-permute-done.3.second), channel_id=1, source_target_pairs={{0,4},{1,5},{2,6},{3,7},{4,0},{5,1},{6,2},{7,3},{8,12},{9,13},{10,... | collective-permute-start | bytes 3244040 | tf_op jit(solution)/shard_map/ppermute | solution.py:402
  48.1 18.7 %collective-permute-start.11 = (bf16[136,2304]{1,0:T(8,128)(2,1)S(1)}, bf16[136,2304]{1,0:T(8,128)(2,1)S(1)}, u32[]{:S(2)}, u32[]{:S(2)}) collective-permute-start(bf16[136,2304]{1,0:T(8,128)(2,1)S(1)} %get-tuple-element.168.own), channel_id=1, source_target_pairs={{0,16},{16,0},{1,17},{17,1},{2,18},{18,2},{3,19},{19,3},{4,20},{20... | collective-permute-start | bytes 1880072 | tf_op jit(solution)/shard_map/ppermute | solution.py:413
  67.4 16.1 %collective-permute-start.16 = (bf16[136,2304]{1,0:T(8,128)(2,1)S(1)}, bf16[136,2304]{1,0:T(8,128)(2,1)S(1)}, u32[]{:S(2)}, u32[]{:S(2)}) collective-permute-start(bf16[136,2304]{1,0:T(8,128)(2,1)S(1)} %get-tuple-element.178.own), channel_id=1, source_target_pairs={{0,16},{16,0},{1,17},{17,1},{2,18},{18,2},{3,19},{19,3},{4,20},{20... | collective-permute-start | bytes 1880072 | tf_op jit(solution)/shard_map/ppermute | solution.py:413
  68.9 25.6 %collective-permute-start.12 = (bf16[128,4224]{1,0:T(8,128)(2,1)S(1)}, bf16[128,4224]{1,0:T(8,128)(2,1)S(1)}, u32[]{:S(2)}, u32[]{:S(2)}) collective-permute-start(bf16[128,4224]{1,0:T(8,128)(2,1)S(1)} %choose.2.refs_2_), channel_id=1, source_target_pairs={{0,2},{1,3},{2,0},{3,1},{4,6},{5,7},{6,4},{7,5},{8,10},{9,11},{10,... | collective-permute-start | bytes 3244040 | tf_op jit(solution)/shard_map/ppermute | solution.py:402
  70.4 25.3 %collective-permute-start.13 = (bf16[128,4224]{1,0:T(8,128)(2,1)S(1)}, bf16[128,4224]{1,0:T(8,128)(2,1)S(1)}, u32[]{:S(2)}, u32[]{:S(2)}) collective-permute-start(bf16[128,4224]{1,0:T(8,128)(2,1)S(1)} %collective-permute-done.8.second), channel_id=1, source_target_pairs={{0,4},{1,5},{2,6},{3,7},{4,0},{5,1},{6,2},{7,3},{8,12},{9,13},{10,... | collective-permute-start | bytes 3244040 | tf_op jit(solution)/shard_map/ppermute | solution.py:402
  83.5 15.3 %collective-permute-start.17 = (bf16[136,2304]{1,0:T(8,128)(2,1)S(1)}, bf16[136,2304]{1,0:T(8,128)(2,1)S(1)}, u32[]{:S(2)}, u32[]{:S(2)}) collective-permute-start(bf16[136,2304]{1,0:T(8,128)(2,1)S(1)} %get-tuple-element.179.own), channel_id=1, source_target_pairs={{0,16},{16,0},{1,17},{17,1},{2,18},{18,2},{3,19},{19,3},{4,20},{20... | collective-permute-start | bytes 1880072 | tf_op jit(solution)/shard_map/ppermute | solution.py:413
  99.7 16.1 %collective-permute-start.22 = (bf16[136,2304]{1,0:T(8,128)(2,1)S(1)}, bf16[136,2304]{1,0:T(8,128)(2,1)S(1)}, u32[]{:S(2)}, u32[]{:S(2)}) collective-permute-start(bf16[136,2304]{1,0:T(8,128)(2,1)S(1)} %get-tuple-element.194.own), channel_id=1, source_target_pairs={{0,16},{16,0},{1,17},{17,1},{2,18},{18,2},{3,19},{19,3},{4,20},{20... | collective-permute-start | bytes 1880072 | tf_op jit(solution)/shard_map/ppermute | solution.py:413
  101.2 16.1 %collective-permute-start.28 = (bf16[128,2176]{1,0:T(8,128)(2,1)S(1)}, bf16[128,2176]{1,0:T(8,128)(2,1)S(1)}, u32[]{:S(2)}, u32[]{:S(2)}) collective-permute-start(bf16[128,2176]{1,0:T(8,128)(2,1)S(1)} %get-tuple-element.202), channel_id=1, source_target_pairs={{0,2},{1,3},{2,0},{3,1},{4,6},{5,7},{6,4},{7,5},{8,10},{9,11},{10,... | collective-permute-start | bytes 1671176 | tf_op jit(solution)/shard_map/ppermute | solution.py:402
  102.7 24.1 %collective-permute-start.26 = (bf16[128,2048]{1,0:T(8,128)(2,1)S(1)}, bf16[128,2048]{1,0:T(8,128)(2,1)S(1)}, u32[]{:S(2)}, u32[]{:S(2)}) collective-permute-start(bf16[128,2048]{1,0:T(8,128)(2,1)S(1)} %get-tuple-element.201), channel_id=1, source_target_pairs={{0,2},{1,3},{2,0},{3,1},{4,6},{5,7},{6,4},{7,5},{8,10},{9,11},{10,... | collective-permute-start | bytes 1572872 | tf_op jit(solution)/shard_map/ppermute | solution.py:402
  115.8 15.3 %collective-permute-start.24 = (bf16[136,2304]{1,0:T(8,128)(2,1)S(1)}, bf16[136,2304]{1,0:T(8,128)(2,1)S(1)}, u32[]{:S(2)}, u32[]{:S(2)}) collective-permute-start(bf16[136,2304]{1,0:T(8,128)(2,1)S(1)} %get-tuple-element.196.own), channel_id=1, source_target_pairs={{0,16},{16,0},{1,17},{17,1},{2,18},{18,2},{3,19},{19,3},{4,20},{20... | collective-permute-start | bytes 1880072 | tf_op jit(solution)/shard_map/ppermute | solution.py:413
  131.1 14.3 %collective-permute-start.31 = (bf16[136,2304]{1,0:T(8,128)(2,1)S(1)}, bf16[136,2304]{1,0:T(8,128)(2,1)S(1)}, u32[]{:S(2)}, u32[]{:S(2)}) collective-permute-start(bf16[136,2304]{1,0:T(8,128)(2,1)S(1)} %get-tuple-element.203.own), channel_id=1, source_target_pairs={{0,16},{16,0},{1,17},{17,1},{2,18},{18,2},{3,19},{19,3},{4,20},{20... | collective-permute-start | bytes 1880072 | tf_op jit(solution)/shard_map/ppermute | solution.py:413
  145.4 14.9 %collective-permute-start.33 = (bf16[136,2304]{1,0:T(8,128)(2,1)S(1)}, bf16[136,2304]{1,0:T(8,128)(2,1)S(1)}, u32[]{:S(2)}, u32[]{:S(2)}) collective-permute-start(bf16[136,2304]{1,0:T(8,128)(2,1)S(1)} %get-tuple-element.221.own), channel_id=1, source_target_pairs={{0,16},{16,0},{1,17},{17,1},{2,18},{18,2},{3,19},{19,3},{4,20},{20... | collective-permute-start | bytes 1880072 | tf_op jit(solution)/shard_map/ppermute | solution.py:413
  164.7 14.7 %collective-permute-start.38 = (bf16[128,2176]{1,0:T(8,128)(2,1)S(1)}, bf16[128,2176]{1,0:T(8,128)(2,1)S(1)}, u32[]{:S(2)}, u32[]{:S(2)}) collective-permute-start(bf16[128,2176]{1,0:T(8,128)(2,1)S(1)} %add.16), channel_id=1, source_target_pairs={{0,2},{1,3},{2,0},{3,1},{4,6},{5,7},{6,4},{7,5},{8,10},{9,11},{10,... | collective-permute-start | bytes 1671176 | tf_op jit(solution)/shard_map/ppermute | solution.py:402
  166.4 23.8 %collective-permute-start.40 = (bf16[128,2176]{1,0:T(8,128)(2,1)S(1)}, bf16[128,2176]{1,0:T(8,128)(2,1)S(1)}, u32[]{:S(2)}, u32[]{:S(2)}) collective-permute-start(bf16[128,2176]{1,0:T(8,128)(2,1)S(1)} %add.18), channel_id=1, source_target_pairs={{0,8},{1,9},{2,10},{3,11},{12,4},{13,5},{14,6},{15,7},{16,24},{17,... | collective-permute-start | bytes 1671176 | tf_op jit(solution)/shard_map/ppermute | solution.py:402
  170.0 20.2 %collective-permute-start.41 = (bf16[128,2176]{1,0:T(8,128)(2,1)S(1)}, bf16[128,2176]{1,0:T(8,128)(2,1)S(1)}, u32[]{:S(2)}, u32[]{:S(2)}) collective-permute-start(bf16[128,2176]{1,0:T(8,128)(2,1)S(1)} %add.18), channel_id=1, source_target_pairs={{4,8},{5,9},{6,10},{7,11},{8,4},{9,5},{10,6},{11,7},{20,24},{21,25... | collective-permute-start | bytes 1671176 | tf_op jit(solution)/shard_map/ppermute | solution.py:402
  179.6 14.3 %collective-permute-start.39 = (bf16[128,2176]{1,0:T(8,128)(2,1)S(1)}, bf16[128,2176]{1,0:T(8,128)(2,1)S(1)}, u32[]{:S(2)}, u32[]{:S(2)}) collective-permute-start(bf16[128,2176]{1,0:T(8,128)(2,1)S(1)} %add.17.refs_0_), channel_id=1, source_target_pairs={{0,4},{1,5},{2,6},{3,7},{12,8},{13,9},{14,10},{15,11},{16,20},{17,... | collective-permute-start | bytes 1671176 | tf_op jit(solution)/shard_map/ppermute | solution.py:402
  182.0 20.0 %collective-permute-start.43 = (bf16[128,2176]{1,0:T(8,128)(2,1)S(1)}, bf16[128,2176]{1,0:T(8,128)(2,1)S(1)}, u32[]{:S(2)}, u32[]{:S(2)}) collective-permute-start(bf16[128,2176]{1,0:T(8,128)(2,1)S(1)} %add.11), channel_id=1, source_target_pairs={{0,2},{1,3},{2,0},{3,1},{4,6},{5,7},{6,4},{7,5},{8,10},{9,11},{10,... | collective-permute-start | bytes 1671176 | tf_op jit(solution)/shard_map/ppermute | solution.py:402
  194.0 17.4 %collective-permute-start.42 = (bf16[128,2176]{1,0:T(8,128)(2,1)S(1)}, bf16[128,2176]{1,0:T(8,128)(2,1)S(1)}, u32[]{:S(2)}, u32[]{:S(2)}) collective-permute-start(bf16[128,2176]{1,0:T(8,128)(2,1)S(1)} %add.19), channel_id=1, source_target_pairs={{4,12},{5,13},{6,14},{7,15},{8,0},{9,1},{10,2},{11,3},{20,28},{21,... | collective-permute-start | bytes 1671176 | tf_op jit(solution)/shard_map/ppermute | solution.py:402
  (29 other events, 243.8 us)

commit v4 on v3

--- a/solution.py
+++ b/solution.py
@@ -176,7 +176,7 @@
     return kernel_call(pack_kernel, operands, [((rows, 2 * width + LANES), BF16)], name="pack")[0]
 
 
-def front_kernel(slots, layout, *refs):
+def front_kernel(slots, layout, joined, *refs):
     sources = refs[: sum(layout)]
     w_gate, w_up, w_down = refs[len(sources) : len(sources) + 3]
     *outs, acc, picks = refs[len(sources) + 3 :]
@@ -199,7 +199,7 @@
         <= lax.broadcasted_iota(jnp.int32, (block, block), 0)
     ).astype(BF16)
     for p in range(pairs):
-        spread, weights = outs[5 * p + 2], outs[5 * p + 3]
+        spread, weights = outs[4 * p + 2], outs[4 * p + 3]
         total = jnp.zeros((rows, LANES), F32)
         for b, (_, source, offset) in enumerate(blocks[2 * p : 2 * p + 2]):
             routing = source[:, pl.ds(offset + width, LANES)].astype(F32)
@@ -223,7 +223,7 @@
         here = pl.ds(start, tile)
         rows_in, grads_in = [], []
         for p in range(pairs):
-            inputs, scaled, _, weights, _ = outs[5 * p : 5 * p + 5]
+            inputs, scaled, _, weights = outs[4 * p : 4 * p + 4]
             (first_c, first_t, first_at), (second_c, second_t, second_at) = blocks[2 * p : 2 * p + 2]
             stacked = jnp.concatenate(
                 [
@@ -245,12 +245,16 @@
         acc[:, 2 * units :] += contract_last(jnp.concatenate(grads_in, axis=0), w_down[:, here])
 
     tiles(width, tile, step)
-    for p in range(pairs):
-        part = outs[5 * p + 4]
-        part[...] = acc[p * rows : p * rows + part.shape[0]].astype(BF16)
-
-
-def front(blocks, w_gate, w_up, w_down, slots):
+    if joined:
+        outs[-1][...] = jnp.concatenate(
+            [acc[p * rows : p * rows + 2 * slots] for p in range(pairs)], axis=0
+        ).astype(BF16)
+    else:
+        for p in range(pairs):
+            outs[4 * pairs + p][...] = acc[p * rows : p * rows + 2 * slots].astype(BF16)
+
+
+def front(blocks, w_gate, w_up, w_down, slots, joined):
     blocks = [b if isinstance(b, tuple) else (b,) for b in blocks]
     layout = [len(b) for b in blocks]
     sources = [array for b in blocks for array in b]
@@ -259,51 +263,58 @@
     pairs = len(blocks) // 2
     rows = -(-2 * slots // 16) * 16
     results = kernel_call(
-        functools.partial(front_kernel, slots, layout),
+        functools.partial(front_kernel, slots, layout, joined),
         (*sources, w_gate, w_up, w_down),
         [
             ((rows, width), BF16),
             ((rows, width), BF16),
             ((2 * block, rows), BF16),
             ((rows, LANES), F32),
-            ((2 * slots, 3 * units), BF16),
         ]
-        * pairs,
+        * pairs
+        + [((2 * slots * (pairs if joined else 1), 3 * units), BF16)] * (1 if joined else pairs),
         scratch=[
             pltpu.VMEM((pairs * rows, 3 * units), F32),
             pltpu.VMEM((pairs, rows, 2 * block), BF16),
         ],
         name="front",
     )
-    names = ("inputs", "scaled", "spread", "weights", "part")
-    return [dict(zip(names, results[5 * p : 5 * p + 5])) for p in range(pairs)]
-
-
-def back_kernel(own, peer, weights, spread, w_gate, w_up, *refs):
-    hidden, grad_gate, grad_up, keep, send = refs
+    names = ("inputs", "scaled", "spread", "weights")
+    states = [dict(zip(names, results[4 * p : 4 * p + 4])) for p in range(pairs)]
+    return states, results[4 * pairs :]
+
+
+def back_kernel(pairs, own, peer, *refs):
+    weights, spreads = refs[:pairs], refs[pairs : 2 * pairs]
+    w_gate, w_up, hidden, grad_gate, grad_up, *outs = refs[2 * pairs :]
     units, width = w_gate.shape
-    filled = own.shape[0]
-    tokens, rows = spread.shape
+    filled = own.shape[0] // pairs
+    tokens, rows = spreads[0].shape
     tile = 1024
     expert = lax.axis_index("expert")
 
     def place(term, columns):
-        placed = jnp.dot(spread[...], term, preferred_element_type=F32).astype(BF16)
-        keep[:, columns] = placed[: tokens // 2]
-        send[:, columns] = placed[tokens // 2 :]
+        for p in range(pairs):
+            here = term[p * rows : (p + 1) * rows]
+            placed = jnp.dot(spreads[p][...], here, preferred_element_type=F32).astype(BF16)
+            outs[2 * p][:, columns] = placed[: tokens // 2]
+            outs[2 * p + 1][:, columns] = placed[tokens // 2 :]
 
     def value(i):
         columns = pl.ds(i * units, units)
         total = own[:, columns].astype(F32) + peer[:, columns].astype(F32)
-        if rows > filled:
-            total = jnp.concatenate([total, jnp.zeros((rows - filled, units), F32)], axis=0)
-        return total
-
-    h, gg, gu, prob = activations(value(0), value(1), value(2), weights[:, :1])
+        if rows == filled:
+            return total
+        pad = jnp.zeros((rows - filled, units), F32)
+        pieces = [total[p * filled : (p + 1) * filled] for p in range(pairs)]
+        return jnp.concatenate([piece for each in pieces for piece in (each, pad)], axis=0)
+
+    scales = jnp.concatenate([weight[:, :1] for weight in weights], axis=0)
+    h, gg, gu, prob = activations(value(0), value(1), value(2), scales)
     hidden[...] = h
     grad_gate[...] = gg
     grad_up[...] = gu
-    lane = lax.broadcasted_iota(jnp.int32, (rows, LANES), 1)
+    lane = lax.broadcasted_iota(jnp.int32, (pairs * rows, LANES), 1)
     place(jnp.where(lane == expert, prob, 0.0).astype(BF16), pl.ds(width, LANES))
 
     def step(start):
@@ -315,22 +326,30 @@
     tiles(width, tile, step)
 
 
-def back(state, peer, w_gate, w_up):
+def back(states, own, peer, w_gate, w_up):
     units, width = w_gate.shape
-    tokens, rows = state["spread"].shape
+    pairs = len(states)
+    tokens, rows = states[0]["spread"].shape
     half = (tokens // 2, width + LANES)
     results = kernel_call(
-        back_kernel,
-        (state["part"], peer, state["weights"], state["spread"], w_gate, w_up),
-        [((rows, units), BF16)] * 3 + [(half, BF16)] * 2,
+        functools.partial(back_kernel, pairs),
+        (
+            own,
+            peer,
+            *[state["weights"] for state in states],
+            *[state["spread"] for state in states],
+            w_gate,
+            w_up,
+        ),
+        [((pairs * rows, units), BF16)] * 3 + [(half, BF16)] * (2 * pairs),
         name="back",
     )
-    return state | dict(zip(("hidden", "grad_gate", "grad_up", "keep", "send"), results))
+    return results[:3], [results[3 + 2 * p : 5 + 2 * p] for p in range(pairs)]
 
 
 def outer_kernel(count, *refs):
-    lefts, rights = refs[:count], refs[count : 2 * count]
-    out, turned = refs[2 * count :]
+    *terms, out, turned = refs
+    lefts, rights = terms[:count], terms[count:]
 
     @pl.when(pl.program_id(0) == 0)
     def _():
@@ -405,15 +424,21 @@
     across = functools.partial(swap, bits=2)
     outer_z = functools.partial(swap, bits=4)
     inner_z = functools.partial(swap, bits=12, part=(1, 2))
-
-    def forward(*blocks):
-        return front(blocks, weight_gate, weight_up, weight_down, slots)
+    to_edge = functools.partial(swap, bits=4, part=(1, 2))
+
+    rights, lefts = [], []
+
+    def forward(*blocks, joined=False):
+        return front(blocks, weight_gate, weight_up, weight_down, slots, joined)
 
     def exchange(part):
         return lax.ppermute(part, "dp", [(0, 1), (1, 0)])
 
-    def backward(state, peer):
-        return back(state, peer, weight_gate, weight_up)
+    def backward(states, own, peer):
+        left, sums = back(states, own, peer, weight_gate, weight_up)
+        rights.extend((state["inputs"], state["scaled"]) for state in states)
+        lefts.append(left)
+        return sums, left[0]
 
     features = tokens.shape[1]
     all_columns = 2 * features + LANES
@@ -421,91 +446,88 @@
     p0 = pack(tokens, cotangent, router_probs, expert_ids)
     q0 = core(p0)
     p1, a0, m0 = across(p0), outer_z(p0), inner_z(p0)
-    (s0,) = forward(p0, q0)
-    y0 = exchange(s0["part"])
-
-    p1, a0, m0, y0 = meet(p1, a0, m0, y0)
-    a1, b0e, c0m = across(a0), outer_z(m0), inner_z(a0)
-    s1, sa0 = forward(p1, core(p1), a0, core(a0))
-    y1 = exchange(s1["part"])
-    s0 = backward(s0, y0)
-    k0 = core(s0["send"])
-
-    a1, b0e, c0m, sa0["part"], y1, _ = meet(a1, b0e, c0m, sa0["part"], y1, k0)
-    ya0 = exchange(sa0["part"])
+    (state0,), (part0,) = forward(p0, q0)
+
+    p1, a0, m0, part0 = meet(p1, a0, m0, part0)
+    a1, b0e, c0m = across(a0), to_edge(m0), inner_z(a0)
+    states1, (part1,) = forward(p1, core(p1), a0, core(a0), joined=True)
+    y1 = exchange(part1)
+
     (b0,) = choose(b0e, m0, (0, all_columns))
-    b1, c0e = across(b0), outer_z(c0m)
-    sa1, sb0 = forward(a1, core(a1), b0, core(b0))
-    s1 = backward(s1, y1)
-
-    sa1["part"], s1["send"], ya0 = meet(sa1["part"], s1["send"], ya0)
-    ya1 = exchange(sa1["part"])
-    k1 = core(s1["send"])
-    sa0 = backward(sa0, ya0)
-    ka0 = core(sa0["send"])
-
-    b1, c0e, sb0["part"], ya1, k1, ka0 = meet(b1, c0e, sb0["part"], ya1, k1, ka0)
-    yb0 = exchange(sb0["part"])
-    cuts = (0, all_columns), (0, features), (features, all_columns)
-    c0, c0c, c0t = choose(c0e, c0m, *cuts)
+    a1, b0, c0m, _ = meet(a1, b0, c0m, part1)
+    b1, c0e = across(b0), to_edge(c0m)
+    (state_a1, state_b0), (part_a1, part_b0) = forward(a1, core(a1), b0, core(b0))
+
+    y1, part_a1 = meet(y1, part_a1)
+    ya1 = exchange(part_a1)
+    ((keep1, send1), (keep_a0, send_a0)), done = backward(states1, part1, y1)
+    k1, ka0 = core(send1), core(send_a0)
+
+    columns = (0, all_columns), (0, features), (features, all_columns)
+    c0, c0c, c0t = choose(c0e, c0m, *columns)
+    b1, c0, c0c, c0t, ya1, part_b0, k1, ka0 = meet(
+        b1, c0, c0c, c0t, ya1, part_b0, k1, ka0
+    )
+    yb0 = exchange(part_b0)
     c1c, c1t = across(c0c), across(c0t)
-    sb1, sc0 = forward(b1, core(b1), c0, core(c0))
-    sa1 = backward(sa1, ya1)
-
-    sb1["part"], sa1["send"], yb0 = meet(sb1["part"], sa1["send"], yb0)
-    yb1 = exchange(sb1["part"])
-    ka1 = core(sa1["send"])
+    (state_b1, state_c0), (part_b1, part_c0) = forward(b1, core(b1), c0, core(c0))
+    ((keep_a1, send_a1),), done = backward((state_a1,), part_a1, ya1)
+
+    yb0, part_b1, send_a1 = meet(yb0, part_b1, send_a1)
+    yb1 = exchange(part_b1)
+    ka1 = core(send_a1)
     qc1 = core(c1c), core(c1t)
-    sb0 = backward(sb0, yb0)
-    kb0 = core(sb0["send"])
-
-    sc0["part"], ka1, yb1, kb0, *qc1 = meet(sc0["part"], ka1, yb1, kb0, *qc1)
-    yc0 = exchange(sc0["part"])
-    ra = across(add(sa1["keep"], ka1))
-    sum1 = add(s1["keep"], k1)
-    sumb0 = add(sb0["keep"], kb0)
-    sb1 = backward(sb1, yb1)
-    kb1 = core(sb1["send"])
-    (sc1,) = forward((c1c, c1t), tuple(qc1))
-
-    sc1["part"], kb1, yc0, ra, sum1, sumb0 = meet(sc1["part"], kb1, yc0, ra, sum1, sumb0)
-    yc1 = exchange(sc1["part"])
-    rb = across(add(sb1["keep"], kb1))
-    from_a = outer_z(add(sa0["keep"], ka0, ra))
-    sc0 = backward(sc0, yc0)
-    kc0 = core(sc0["send"])
-
-    yc1, kc0, rb, from_a = meet(yc1, kc0, rb, from_a)
-    sc1 = backward(sc1, yc1)
-    kc1 = core(sc1["send"])
-    sumc0 = add(sc0["keep"], kc0)
+    ((keep_b0, send_b0),), done = backward((state_b0,), part_b0, yb0)
+    kb0 = core(send_b0)
+
+    part_c0, ka1, yb1, kb0, *qc1 = meet(part_c0, ka1, yb1, kb0, *qc1)
+    yc0 = exchange(part_c0)
+    ra = across(add(keep_a1, ka1))
+    sum1 = add(keep1, k1)
+    sumb0 = add(keep_b0, kb0)
+    ((keep_b1, send_b1),), done = backward((state_b1,), part_b1, yb1)
+    kb1 = core(send_b1)
+    (state_c1,), (part_c1,) = forward((c1c, c1t), tuple(qc1))
+
+    suma = add(keep_a0, ka0, ra)
+    part_c1, yc0, suma, sum1, sumb0, keep_b1 = meet(part_c1, yc0, suma, sum1, sumb0, keep_b1)
+    yc1 = exchange(part_c1)
+    rb = across(add(keep_b1, kb1))
+    from_a = outer_z(suma)
+    ((keep_c0, send_c0),), done = backward((state_c0,), part_c0, yc0)
+    kc0 = core(send_c0)
+
+    yc1, rb, from_a, part0, keep_c0 = meet(yc1, rb, from_a, part0, keep_c0)
+    y0 = exchange(part0)
+    ((keep_c1, send_c1),), done = backward((state_c1,), part_c1, yc1)
+    kc1 = core(send_c1)
+    sumc0 = add(keep_c0, kc0)
     sumb = add(sumb0, rb)
     b_edge, b_middle = swap(sumb, 8, (0, 3)), swap(sumb, 12, (1, 2))
 
-    sumc1 = add(sc1["keep"], kc1)
+    sumc1 = add(keep_c1, kc1)
     rc = across(sumc1)
-    states = (s0, s1, sa0, sa1, sb0, sb1, sc0, sc1)
-    inputs, scaled, hidden, grad_gate, grad_up = (
-        tuple(s[key] for s in states)
-        for key in ("inputs", "scaled", "hidden", "grad_gate", "grad_up")
-    )
-    grad_gate, _ = meet(grad_gate, sumc1)
-    gate_grad = outer(grad_gate, inputs)
-
-    rc, sum1, _ = meet(rc, sum1, gate_grad)
+    rc, sum1, y0 = meet(rc, sum1, y0)
     sumc = add(sumc0, rc)
     c_edge = outer_z(sumc, part=(0, 3))
     r0 = across(sum1)
+    y0, _ = meet(y0, sumc)
+    ((keep0, send0),), done = backward((state0,), part0, y0)
+    k0 = core(send0)
+
+    inputs, scaled = zip(*rights)
+    hidden, grad_gate, grad_up = zip(*lefts)
+    gate_grad = outer(grad_gate, inputs)
+
+    c_edge, b_edge, b_middle, _ = meet(c_edge, b_edge, b_middle, gate_grad)
+    sumc = add(sumc, c_edge)
+    far = swap(sumc, 8, (1, 2))
     grad_up, _ = meet(grad_up, sumc)
     up_grad = outer(grad_up, inputs)
-
-    c_edge, b_edge, b_middle, _ = meet(c_edge, b_edge, b_middle, up_grad)
-    sumc = add(sumc, c_edge)
-    far = swap(sumc, 8, (1, 2))
-    hidden, _ = meet(hidden, sumc)
+    hidden, _ = meet(hidden, up_grad)
     down_grad = outer(hidden, scaled)
-    far, r0, _ = meet(far, r0, down_grad)
-    token_grads, by_expert = finish(s0["keep"], k0, r0, from_a, b_edge, b_middle, far)
+    far, r0, k0, _ = meet(far, r0, k0, down_grad)
+    token_grads, by_expert = finish(keep0, k0, r0, from_a, b_edge, b_middle, far)
     chosen = expert_ids[:, :, None] == jnp.arange(experts, dtype=jnp.int32)[None, None, :]
     prob_grads = jnp.sum(jnp.where(chosen, by_expert[:, None, :experts], 0.0), axis=2)
     return (

time: 214 us -> 209 us (0.977)
  starting transfers between devices: 48.9 us -> 40.7 us
  waiting for transfers between devices: 89.4 us -> 93.1 us
    ppermute x36, starting transfers between devices: 36.8 us -> 31.1 us  [swap(): return lax.ppermute(value, 'expert', pairs)]
    ppermute x36, waiting for transfers between devices: 71.6 us -> 77.2 us  [swap(): return lax.ppermute(value, 'expert', pairs)]
    ppermute x8 -> x7, starting transfers between devices: 12.1 us -> 9.63 us  [exchange(): return lax.ppermute(part, 'dp', [(0, 1), (1, 0)])]
    ppermute x8 -> x7, waiting for transfers between devices: 17.8 us -> 15.9 us  [exchange(): return lax.ppermute(part, 'dp', [(0, 1), (1, 0)])]
    pallas_call x27 -> x26, Pallas kernels: 44 us -> 43.3 us  [kernel_call(): pl.pallas_call(body, in_specs=[pl.BlockSpec(memory_space=pltpu.VMEM)] * l...]
  transfers between devices with their start and end apart: 44 -> 43, of which waited for: 22 -> 19; matrix products, arithmetic and copies ran while one was open for 0% -> 0% of each run, Pallas kernels for 28% -> 29%
where the time goes in v4:
time: 209 us; the launch traced here: 208 us
  waiting for transfers between devices  93.1 us (45%)
  Pallas kernels  63.3 us (30%)
  starting transfers between devices  40.7 us (19%)
  local copies, waits for them, and re-layouts  9.39 us (4%)
    ppermute x36, waiting for transfers between devices, swap(): return lax.ppermute(value, 'expert', pairs)  77.2 us
    pallas_call x26, Pallas kernels, kernel_call(): pl.pallas_call(body, in_specs=[pl.BlockSpec(memory_space=pltpu.VMEM)] * l...  43.3 us
    ppermute x36, starting transfers between devices, swap(): return lax.ppermute(value, 'expert', pairs)  31.1 us
    pallas_call x3, Pallas kernels, outer(): pl.pallas_call(functools.partial(outer_kernel, len(lefts)), grid=(width /...  20 us
    ppermute x7, waiting for transfers between devices, exchange(): return lax.ppermute(part, 'dp', [(0, 1), (1, 0)])  15.9 us
    ppermute x7, starting transfers between devices, exchange(): return lax.ppermute(part, 'dp', [(0, 1), (1, 0)])  9.63 us
    unnamed x20, local copies, waits for them, and re-layouts  9.34 us
  transfers between devices with their start and end apart: 43, of which 19 were waited for; matrix products, arithmetic and copies ran while one was open for 0% of the time, Pallas kernels for 29%

profile of v4, /device:TPU:0, one launch (start us, length us, event | category | flops | bytes accessed | tf_op | source)
XLA Modules:
  0.0 208.2 jit_solution(1209122474525792170)
XLA Ops:
  5.1 2.6 %collective-permute-start = (bf16[128,4224]{1,0:T(8,128)(2,1)S(1)}, bf16[128,4224]{1,0:T(8,128)(2,1)S(1)}, u32[]{:S(2)}, u32[]{:S(2)}) collective-permute-start(bf16[128,4224]{1,0:T(8,128)(2,1)S(1)} %pack.1.refs_0_), channel_id=1, source_target_pairs={{0,2},{1,3},{2,0},{3,1},{4,6},{5,7},{6,4},{7,5},{8,10},{9,11},{10,... | collective-permute-start | bytes 3244040 | tf_op jit(solution)/shard_map/ppermute | solution.py:421
  15.7 4.3 %front.5 = (bf16[144,2048]{1,0:T(8,128)(2,1)S(1)}, bf16[144,2048]{1,0:T(8,128)(2,1)S(1)}, bf16[256,144]{1,0:T(8,128)(2,1)S(1)}, f32[144,128]{1,0:T(8,128)S(1)}, bf16[136,2304]{1,0:T(8,128)(2,1)S(1)}) custom-call(bf16[128,4224]{1,0:T(8,128)(2,1)S(1)} %pack.1.refs_0_, bf16[128,4224]{1,0:T(8,128)(2,1)S(1)} %collective-permute-done.3.refs_1_, ...), custom_call_target="tpu_custom_call" | custom-call | flops 1000 | bytes 1000 | tf_op jit(solution)/shard_map/front/pallas_call | solution.py:117
  20.0 12.2 %collective-permute-done.refs_0_ = bf16[128,4224]{1,0:T(8,128)(2,1)S(1)} collective-permute-done((bf16[128,4224]{1,0:T(8,128)(2,1)S(1)}, bf16[128,4224]{1,0:T(8,128)(2,1)S(1)}, u32[]{:S(2)}, u32[]{:S(2)}) %collective-permute-start) | collective-permute-done | bytes 1081376 | tf_op jit(solution)/shard_map/ppermute | solution.py:421
  37.9 4.7 %front.6 = (bf16[144,2048]{1,0:T(8,128)(2,1)S(1)}, bf16[144,2048]{1,0:T(8,128)(2,1)S(1)}, bf16[256,144]{1,0:T(8,128)(2,1)S(1)}, f32[144,128]{1,0:T(8,128)S(1)}, ...) custom-call(bf16[128,4224]{1,0:T(8,128)(2,1)S(1)} %collective-permut, ...), custom_call_target="tpu_custom_call" | custom-call | flops 1000 | bytes 1000 | tf_op jit(solution)/shard_map/front/pallas_call | solution.py:117
  44.2 19.8 %collective-permute-done.5.first = bf16[128,4224]{1,0:T(8,128)(2,1)S(1)} collective-permute-done((bf16[128,4224]{1,0:T(8,128)(2,1)S(1)}, bf16[128,4224]{1,0:T(8,128)(2,1)S(1)}, u32[]{:S(2)}, u32[]{:S(2)}) %collective-permute-start.5) | collective-permute-done | bytes 1081376 | tf_op jit(solution)/shard_map/ppermute | solution.py:421
  68.4 4.7 %front.7 = (bf16[144,2048]{1,0:T(8,128)(2,1)S(1)}, bf16[144,2048]{1,0:T(8,128)(2,1)S(1)}, bf16[256,144]{1,0:T(8,128)(2,1)S(1)}, f32[144,128]{1,0:T(8,128)S(1)}, ...) custom-call(bf16[128,4224]{1,0:T(8,128)(2,1)S(1)} %collective-permut, ...), custom_call_target="tpu_custom_call" | custom-call | flops 1000 | bytes 1000 | tf_op jit(solution)/shard_map/front/pallas_call | solution.py:117
  74.8 3.7 %back.7 = (bf16[288,768]{1,0:T(8,128)(2,1)S(1)}, bf16[288,768]{1,0:T(8,128)(2,1)S(1)}, bf16[288,768]{1,0:T(8,128)(2,1)S(1)}, bf16[128,2176]{1,0:T(8,128)(2,1)S(1...) custom-call(bf16[272,2304]{1,0:T(8,128)(2,1)S(1)} %get-tuple-element.151.own, ...), custom_call_target="tpu_custom_call" | custom-call | flops 1000 | bytes 1000 | tf_op jit(solution)/shard_map/back/pallas_call | solution.py:117
  79.0 14.8 %collective-permute-done.10.first = bf16[128,4224]{1,0:T(8,128)(2,1)S(1)} collective-permute-done((bf16[128,4224]{1,0:T(8,128)(2,1)S(1)}, bf16[128,4224]{1,0:T(8,128)(2,1)S(1)}, u32[]{:S(2)}, u32[]{:S(2)}) %collective-permute-start.10) | collective-permute-done | bytes 1081376 | tf_op jit(solution)/shard_map/ppermute | solution.py:421
  100.6 4.7 %front.8 = (bf16[144,2048]{1,0:T(8,128)(2,1)S(1)}, bf16[144,2048]{1,0:T(8,128)(2,1)S(1)}, bf16[256,144]{1,0:T(8,128)(2,1)S(1)}, f32[144,128]{1,0:T(8,128)S(1)}, ...) custom-call(bf16[128,4224]{1,0:T(8,128)(2,1)S(1)} %collective-permut, ...), custom_call_target="tpu_custom_call" | custom-call | flops 1000 | bytes 1000 | tf_op jit(solution)/shard_map/front/pallas_call | solution.py:117
  105.4 5.6 %collective-permute-done.21.peer = bf16[136,2304]{1,0:T(8,128)(2,1)S(1)} collective-permute-done((bf16[136,2304]{1,0:T(8,128)(2,1)S(1)}, bf16[136,2304]{1,0:T(8,128)(2,1)S(1)}, u32[]{:S(2)}, u32[]{:S(2)}) %collective-permute-start.21) | collective-permute-done | bytes 626720 | tf_op jit(solution)/shard_map/ppermute | solution.py:435
  112.9 2.2 %back.9 = (bf16[144,768]{1,0:T(8,128)(2,1)S(1)}, bf16[144,768]{1,0:T(8,128)(2,1)S(1)}, bf16[144,768]{1,0:T(8,128)(2,1)S(1)}, bf16[128,2176]{1,0:T(8,128)(2,1)S(1)}, bf16[128,2176]{1,0:T(8,128)(2,1)S(1)}) custom-call(bf16[136,2304]{1,0:T(8,128)(2,1)S(1)} %get-tuple-element.173.own, bf16[136,2304]{1,0:T(8,128)(2,1)S(1)} %collective-permute-done.21.peer, ...), custom_call_target="tpu_custom_call" | custom-call | flops 1000 | bytes 1000 | tf_op jit(solution)/shard_map/back/pallas_call | solution.py:117
  115.3 6.6 %collective-permute-done.17.refs_0_ = bf16[128,2048]{1,0:T(8,128)(2,1)S(1)} collective-permute-done((bf16[128,2048]{1,0:T(8,128)(2,1)S(1)}, bf16[128,2048]{1,0:T(8,128)(2,1)S(1)}, u32[]{:S(2)}, u32[]{:S(2)}) %collective-permute-start.17) | collective-permute-done | bytes 524320 | tf_op jit(solution)/shard_map/ppermute | solution.py:421
  123.8 2.4 %collective-permute-done.23.peer = bf16[136,2304]{1,0:T(8,128)(2,1)S(1)} collective-permute-done((bf16[136,2304]{1,0:T(8,128)(2,1)S(1)}, bf16[136,2304]{1,0:T(8,128)(2,1)S(1)}, u32[]{:S(2)}, u32[]{:S(2)}) %collective-permute-start.23) | collective-permute-done | bytes 626720 | tf_op jit(solution)/shard_map/ppermute | solution.py:435
  132.0 4.3 %front.9 = (bf16[144,2048]{1,0:T(8,128)(2,1)S(1)}, bf16[144,2048]{1,0:T(8,128)(2,1)S(1)}, bf16[256,144]{1,0:T(8,128)(2,1)S(1)}, f32[144,128]{1,0:T(8,128)S(1)}, bf16[136,2304]{1,0:T(8,128)(2,1)S(1)}) custom-call(bf16[128,2048]{1,0:T(8,128)(2,1)S(1)} %collective-permute-done.17.refs_0_, bf16[128,2176]{1,0:T(8,128)(2,1)S(1)} %collective-permute-done.18.refs_1_, ...), custom_call_target="tpu_custom_call" | custom-call | flops 1000 | bytes 1000 | tf_op jit(solution)/shard_map/front/pallas_call | solution.py:117
  136.3 4.1 %collective-permute-done.28.refs_2_ = bf16[128,2176]{1,0:T(8,128)(2,1)S(1)} collective-permute-done((bf16[128,2176]{1,0:T(8,128)(2,1)S(1)}, bf16[128,2176]{1,0:T(8,128)(2,1)S(1)}, u32[]{:S(2)}, u32[]{:S(2)}) %collective-permute-start.28) | collective-permute-done | bytes 557088 | tf_op jit(solution)/shard_map/ppermute | solution.py:421
  145.3 2.3 %back.11 = (bf16[144,768]{1,0:T(8,128)(2,1)S(1)}, bf16[144,768]{1,0:T(8,128)(2,1)S(1)}, bf16[144,768]{1,0:T(8,128)(2,1)S(1)}, bf16[128,2176]{1,0:T(8,128)(2,1)S(1)}, bf16[128,2176]{1,0:T(8,128)(2,1)S(1)}) custom-call(bf16[136,2304]{1,0:T(8,128)(2,1)S(1)} %get-tuple-element.188.own, bf16[136,2304]{1,0:T(8,128)(2,1)S(1)} %collective-permute-done.27.peer, ...), custom_call_target="tpu_custom_call" | custom-call | flops 1000 | bytes 1000 | tf_op jit(solution)/shard_map/back/pallas_call | solution.py:117
  147.5 6.4 %collective-permute-done.31.refs_1_ = bf16[128,2176]{1,0:T(8,128)(2,1)S(1)} collective-permute-done((bf16[128,2176]{1,0:T(8,128)(2,1)S(1)}, bf16[128,2176]{1,0:T(8,128)(2,1)S(1)}, u32[]{:S(2)}, u32[]{:S(2)}) %collective-permute-start.31) | collective-permute-done | bytes 557088 | tf_op jit(solution)/shard_map/ppermute | solution.py:421
  160.2 4.6 %collective-permute-start.38 = (bf16[128,2176]{1,0:T(8,128)(2,1)S(1)}, bf16[128,2176]{1,0:T(8,128)(2,1)S(1)}, u32[]{:S(2)}, u32[]{:S(2)}) collective-permute-start(bf16[128,2176]{1,0:T(8,128)(2,1)S(1)} %add.18), channel_id=1, source_target_pairs={{0,8},{1,9},{2,10},{3,11},{12,4},{13,5},{14,6},{15,7},{16,24},{17,... | collective-permute-start | bytes 1671176 | tf_op jit(solution)/shard_map/ppermute | solution.py:421
  165.9 8.0 %collective-permute-done.35.peer = bf16[136,2304]{1,0:T(8,128)(2,1)S(1)} collective-permute-done((bf16[136,2304]{1,0:T(8,128)(2,1)S(1)}, bf16[136,2304]{1,0:T(8,128)(2,1)S(1)}, u32[]{:S(2)}, u32[]{:S(2)}) %collective-permute-start.35) | collective-permute-done | bytes 626720 | tf_op jit(solution)/shard_map/ppermute | solution.py:435
  174.4 3.5 %collective-permute-start.37 = (bf16[128,2176]{1,0:T(8,128)(2,1)S(1)}, bf16[128,2176]{1,0:T(8,128)(2,1)S(1)}, u32[]{:S(2)}, u32[]{:S(2)}) collective-permute-start(bf16[128,2176]{1,0:T(8,128)(2,1)S(1)} %add.17.refs_0_), channel_id=1, source_target_pairs={{0,4},{1,5},{2,6},{3,7},{12,8},{13,9},{14,10},{15,11},{16,20},{17,... | collective-permute-start | bytes 1671176 | tf_op jit(solution)/shard_map/ppermute | solution.py:421
  180.8 6.7 %outer.3 = bf16[768,2048]{1,0:T(8,128)(2,1)} custom-call(bf16[288,768]{1,0:T(8,128)(2,1)S(1)} %get-tuple-element.227.refs_0_, bf16[144,768]{1,0:T(8,128)(2,1)S(1)} %get-tuple-element.228.refs_1_, bf16[144,768]{1,0:T(8,128)(2,1)S(1)} %get-tuple-element.229.refs_2_, bf16[144,768]{1,0:T(8,128)(2,1)S(1)} %get-tuple-element.230.refs_3_, ...), custom_call_target="tpu_custom_call" | custom-call | flops 1000 | bytes 1000 | tf_op jit(solution)/shard_map/outer/pallas_call | solution.py:366
  190.7 6.7 %outer.4 = bf16[768,2048]{1,0:T(8,128)(2,1)} custom-call(bf16[288,768]{1,0:T(8,128)(2,1)S(1)} %get-tuple-element.259.refs_0_, bf16[144,768]{1,0:T(8,128)(2,1)S(1)} %get-tuple-element.260.refs_1_, bf16[144,768]{1,0:T(8,128)(2,1)S(1)} %get-tuple-element.261.refs_2_, bf16[144,768]{1,0:T(8,128)(2,1)S(1)} %get-tuple-element.262.refs_3_, ...), custom_call_target="tpu_custom_call" | custom-call | flops 1000 | bytes 1000 | tf_op jit(solution)/shard_map/outer/pallas_call | solution.py:366
  197.3 6.7 %outer.5 = bf16[768,2048]{1,0:T(8,128)(2,1)} custom-call(bf16[288,768]{1,0:T(8,128)(2,1)S(1)} %get-tuple-element.266.refs_0_, bf16[144,768]{1,0:T(8,128)(2,1)S(1)} %get-tuple-element.267.refs_1_, bf16[144,768]{1,0:T(8,128)(2,1)S(1)} %get-tuple-element.268.refs_2_, bf16[144,768]{1,0:T(8,128)(2,1)S(1)} %get-tuple-element.269.refs_3_, ...), custom_call_target="tpu_custom_call" | custom-call | flops 1000 | bytes 1000 | tf_op jit(solution)/shard_map/outer/pallas_call | solution.py:366
  204.0 2.3 %collective-permute-done.40.refs_6_ = bf16[128,2176]{1,0:T(8,128)(2,1)S(1)} collective-permute-done((bf16[128,2176]{1,0:T(8,128)(2,1)S(1)}, bf16[128,2176]{1,0:T(8,128)(2,1)S(1)}, u32[]{:S(2)}, u32[]{:S(2)}) %collective-permute-start.40) | collective-permute-done | bytes 557088 | tf_op jit(solution)/shard_map/ppermute | solution.py:421
  (113 shorter events, 63.4 us)
Async XLA Ops:
  5.1 27.0 %collective-permute-start = (bf16[128,4224]{1,0:T(8,128)(2,1)S(1)}, bf16[128,4224]{1,0:T(8,128)(2,1)S(1)}, u32[]{:S(2)}, u32[]{:S(2)}) collective-permute-start(bf16[128,4224]{1,0:T(8,128)(2,1)S(1)} %pack.1.refs_0_), channel_id=1, source_target_pairs={{0,2},{1,3},{2,0},{3,1},{4,6},{5,7},{6,4},{7,5},{8,10},{9,11},{10,... | collective-permute-start | bytes 3244040 | tf_op jit(solution)/shard_map/ppermute | solution.py:421
  7.7 25.9 %collective-permute-start.1 = (bf16[128,4224]{1,0:T(8,128)(2,1)S(1)}, bf16[128,4224]{1,0:T(8,128)(2,1)S(1)}, u32[]{:S(2)}, u32[]{:S(2)}) collective-permute-start(bf16[128,4224]{1,0:T(8,128)(2,1)S(1)} %pack.1.refs_0_), channel_id=1, source_target_pairs={{0,4},{1,5},{2,6},{3,7},{4,0},{5,1},{6,2},{7,3},{8,12},{9,13},{10,... | collective-permute-start | bytes 3244040 | tf_op jit(solution)/shard_map/ppermute | solution.py:421
  9.3 24.4 %collective-permute-start.2 = (bf16[128,4224]{1,0:T(8,128)(2,1)S(1)}, bf16[128,4224]{1,0:T(8,128)(2,1)S(1)}, u32[]{:S(2)}, u32[]{:S(2)}) collective-permute-start(bf16[128,4224]{1,0:T(8,128)(2,1)S(1)} %pack.1.refs_0_), channel_id=1, source_target_pairs={{4,8},{5,9},{6,10},{7,11},{8,4},{9,5},{10,6},{11,7},{20,24},{21,25... | collective-permute-start | bytes 3244040 | tf_op jit(solution)/shard_map/ppermute | solution.py:421
  34.1 29.9 %collective-permute-start.5 = (bf16[128,4224]{1,0:T(8,128)(2,1)S(1)}, bf16[128,4224]{1,0:T(8,128)(2,1)S(1)}, u32[]{:S(2)}, u32[]{:S(2)}) collective-permute-start(bf16[128,4224]{1,0:T(8,128)(2,1)S(1)} %collective-permute-done.2.second), channel_id=1, source_target_pairs={{4,0},{5,1},{6,2},{7,3},{8,12},{9,13},{10,14},{11,15},{20,16},{21,... | collective-permute-start | bytes 3244040 | tf_op jit(solution)/shard_map/ppermute | solution.py:421
  35.4 28.7 %collective-permute-start.4 = (bf16[128,4224]{1,0:T(8,128)(2,1)S(1)}, bf16[128,4224]{1,0:T(8,128)(2,1)S(1)}, u32[]{:S(2)}, u32[]{:S(2)}) collective-permute-start(bf16[128,4224]{1,0:T(8,128)(2,1)S(1)} %collective-permute-done.1.refs_2_), channel_id=1, source_target_pairs={{0,2},{1,3},{2,0},{3,1},{4,6},{5,7},{6,4},{7,5},{8,10},{9,11},{10,... | collective-permute-start | bytes 3244040 | tf_op jit(solution)/shard_map/ppermute | solution.py:421
  35.9 28.3 %collective-permute-start.6 = (bf16[128,4224]{1,0:T(8,128)(2,1)S(1)}, bf16[128,4224]{1,0:T(8,128)(2,1)S(1)}, u32[]{:S(2)}, u32[]{:S(2)}) collective-permute-start(bf16[128,4224]{1,0:T(8,128)(2,1)S(1)} %collective-permute-done.1.refs_2_), channel_id=1, source_target_pairs={{4,8},{5,9},{6,10},{7,11},{8,4},{9,5},{10,6},{11,7},{20,24},{21,25... | collective-permute-start | bytes 3244040 | tf_op jit(solution)/shard_map/ppermute | solution.py:421
  42.6 30.6 %collective-permute-start.11 = (bf16[272,2304]{1,0:T(8,128)(2,1)S(1)}, bf16[272,2304]{1,0:T(8,128)(2,1)S(1)}, u32[]{:S(2)}, u32[]{:S(2)}) collective-permute-start(bf16[272,2304]{1,0:T(8,128)(2,1)S(1)} %get-tuple-element.151.own), channel_id=1, source_target_pairs={{0,16},{16,0},{1,17},{17,1},{2,18},{18,2},{3,19},{19,3},{4,20},{20... | collective-permute-start | bytes 3760136 | tf_op jit(solution)/shard_map/ppermute | solution.py:435
  64.7 29.2 %collective-permute-start.10 = (bf16[128,4224]{1,0:T(8,128)(2,1)S(1)}, bf16[128,4224]{1,0:T(8,128)(2,1)S(1)}, u32[]{:S(2)}, u32[]{:S(2)}) collective-permute-start(bf16[128,4224]{1,0:T(8,128)(2,1)S(1)} %collective-permute-done.6.second), channel_id=1, source_target_pairs={{4,0},{5,1},{6,2},{7,3},{8,12},{9,13},{10,14},{11,15},{20,16},{21,... | collective-permute-start | bytes 3244040 | tf_op jit(solution)/shard_map/ppermute | solution.py:421
  66.0 28.2 %collective-permute-start.9 = (bf16[128,4224]{1,0:T(8,128)(2,1)S(1)}, bf16[128,4224]{1,0:T(8,128)(2,1)S(1)}, u32[]{:S(2)}, u32[]{:S(2)}) collective-permute-start(bf16[128,4224]{1,0:T(8,128)(2,1)S(1)} %choose.2.refs_2_), channel_id=1, source_target_pairs={{0,2},{1,3},{2,0},{3,1},{4,6},{5,7},{6,4},{7,5},{8,10},{9,11},{10,... | collective-permute-start | bytes 3244040 | tf_op jit(solution)/shard_map/ppermute | solution.py:421
  73.2 21.0 %collective-permute-start.14 = (bf16[136,2304]{1,0:T(8,128)(2,1)S(1)}, bf16[136,2304]{1,0:T(8,128)(2,1)S(1)}, u32[]{:S(2)}, u32[]{:S(2)}) collective-permute-start(bf16[136,2304]{1,0:T(8,128)(2,1)S(1)} %get-tuple-element.159.own), channel_id=1, source_target_pairs={{0,16},{16,0},{1,17},{17,1},{2,18},{18,2},{3,19},{19,3},{4,20},{20... | collective-permute-start | bytes 1880072 | tf_op jit(solution)/shard_map/ppermute | solution.py:435
  78.5 15.7 %collective-permute-start.15 = (bf16[128,2176]{1,0:T(8,128)(2,1)S(1)}, bf16[128,2176]{1,0:T(8,128)(2,1)S(1)}, u32[]{:S(2)}, u32[]{:S(2)}) collective-permute-start(bf16[128,2176]{1,0:T(8,128)(2,1)S(1)} %get-tuple-element.166), channel_id=1, source_target_pairs={{0,1},{1,0},{2,3},{3,2},{4,5},{5,4},{6,7},{7,6},{8,9},{9,8},{10,11... | collective-permute-start | bytes 1671176 | tf_op jit(solution)/shard_map/ppermute | solution.py:421
  78.5 15.7 %collective-permute-start.16 = (bf16[128,2176]{1,0:T(8,128)(2,1)S(1)}, bf16[128,2176]{1,0:T(8,128)(2,1)S(1)}, u32[]{:S(2)}, u32[]{:S(2)}) collective-permute-start(bf16[128,2176]{1,0:T(8,128)(2,1)S(1)} %get-tuple-element.167), channel_id=1, source_target_pairs={{0,1},{1,0},{2,3},{3,2},{4,5},{5,4},{6,7},{7,6},{8,9},{9,8},{10,11... | collective-permute-start | bytes 1671176 | tf_op jit(solution)/shard_map/ppermute | solution.py:421
  94.8 16.1 %collective-permute-start.21 = (bf16[136,2304]{1,0:T(8,128)(2,1)S(1)}, bf16[136,2304]{1,0:T(8,128)(2,1)S(1)}, u32[]{:S(2)}, u32[]{:S(2)}) collective-permute-start(bf16[136,2304]{1,0:T(8,128)(2,1)S(1)} %get-tuple-element.173.own), channel_id=1, source_target_pairs={{0,16},{16,0},{1,17},{17,1},{2,18},{18,2},{3,19},{19,3},{4,20},{20... | collective-permute-start | bytes 1880072 | tf_op jit(solution)/shard_map/ppermute | solution.py:435
  96.3 16.1 %collective-permute-start.18 = (bf16[128,2176]{1,0:T(8,128)(2,1)S(1)}, bf16[128,2176]{1,0:T(8,128)(2,1)S(1)}, u32[]{:S(2)}, u32[]{:S(2)}) collective-permute-start(bf16[128,2176]{1,0:T(8,128)(2,1)S(1)} %get-tuple-element.169), channel_id=1, source_target_pairs={{0,2},{1,3},{2,0},{3,1},{4,6},{5,7},{6,4},{7,5},{8,10},{9,11},{10,... | collective-permute-start | bytes 1671176 | tf_op jit(solution)/shard_map/ppermute | solution.py:421
  97.8 24.1 %collective-permute-start.17 = (bf16[128,2048]{1,0:T(8,128)(2,1)S(1)}, bf16[128,2048]{1,0:T(8,128)(2,1)S(1)}, u32[]{:S(2)}, u32[]{:S(2)}) collective-permute-start(bf16[128,2048]{1,0:T(8,128)(2,1)S(1)} %get-tuple-element.168), channel_id=1, source_target_pairs={{0,2},{1,3},{2,0},{3,1},{4,6},{5,7},{6,4},{7,5},{8,10},{9,11},{10,... | collective-permute-start | bytes 1572872 | tf_op jit(solution)/shard_map/ppermute | solution.py:421
  110.9 15.3 %collective-permute-start.23 = (bf16[136,2304]{1,0:T(8,128)(2,1)S(1)}, bf16[136,2304]{1,0:T(8,128)(2,1)S(1)}, u32[]{:S(2)}, u32[]{:S(2)}) collective-permute-start(bf16[136,2304]{1,0:T(8,128)(2,1)S(1)} %get-tuple-element.180.own), channel_id=1, source_target_pairs={{0,16},{16,0},{1,17},{17,1},{2,18},{18,2},{3,19},{19,3},{4,20},{20... | collective-permute-start | bytes 1880072 | tf_op jit(solution)/shard_map/ppermute | solution.py:435
  157.4 16.5 %collective-permute-start.35 = (bf16[136,2304]{1,0:T(8,128)(2,1)S(1)}, bf16[136,2304]{1,0:T(8,128)(2,1)S(1)}, u32[]{:S(2)}, u32[]{:S(2)}) collective-permute-start(bf16[136,2304]{1,0:T(8,128)(2,1)S(1)} %get-tuple-element.210.own), channel_id=1, source_target_pairs={{0,16},{16,0},{1,17},{17,1},{2,18},{18,2},{3,19},{19,3},{4,20},{20... | collective-permute-start | bytes 1880072 | tf_op jit(solution)/shard_map/ppermute | solution.py:435
  159.5 14.7 %collective-permute-start.34 = (bf16[128,2176]{1,0:T(8,128)(2,1)S(1)}, bf16[128,2176]{1,0:T(8,128)(2,1)S(1)}, u32[]{:S(2)}, u32[]{:S(2)}) collective-permute-start(bf16[128,2176]{1,0:T(8,128)(2,1)S(1)} %add.15), channel_id=1, source_target_pairs={{0,2},{1,3},{2,0},{3,1},{4,6},{5,7},{6,4},{7,5},{8,10},{9,11},{10,... | collective-permute-start | bytes 1671176 | tf_op jit(solution)/shard_map/ppermute | solution.py:421
  160.2 27.2 %collective-permute-start.38 = (bf16[128,2176]{1,0:T(8,128)(2,1)S(1)}, bf16[128,2176]{1,0:T(8,128)(2,1)S(1)}, u32[]{:S(2)}, u32[]{:S(2)}) collective-permute-start(bf16[128,2176]{1,0:T(8,128)(2,1)S(1)} %add.18), channel_id=1, source_target_pairs={{0,8},{1,9},{2,10},{3,11},{12,4},{13,5},{14,6},{15,7},{16,24},{17,... | collective-permute-start | bytes 1671176 | tf_op jit(solution)/shard_map/ppermute | solution.py:421
  164.9 22.6 %collective-permute-start.39 = (bf16[128,2176]{1,0:T(8,128)(2,1)S(1)}, bf16[128,2176]{1,0:T(8,128)(2,1)S(1)}, u32[]{:S(2)}, u32[]{:S(2)}) collective-permute-start(bf16[128,2176]{1,0:T(8,128)(2,1)S(1)} %add.18), channel_id=1, source_target_pairs={{4,8},{5,9},{6,10},{7,11},{8,4},{9,5},{10,6},{11,7},{20,24},{21,25... | collective-permute-start | bytes 1671176 | tf_op jit(solution)/shard_map/ppermute | solution.py:421
  174.4 14.9 %collective-permute-start.37 = (bf16[128,2176]{1,0:T(8,128)(2,1)S(1)}, bf16[128,2176]{1,0:T(8,128)(2,1)S(1)}, u32[]{:S(2)}, u32[]{:S(2)}) collective-permute-start(bf16[128,2176]{1,0:T(8,128)(2,1)S(1)} %add.17.refs_0_), channel_id=1, source_target_pairs={{0,4},{1,5},{2,6},{3,7},{12,8},{13,9},{14,10},{15,11},{16,20},{17,... | collective-permute-start | bytes 1671176 | tf_op jit(solution)/shard_map/ppermute | solution.py:421
  177.8 26.2 %collective-permute-start.41 = (bf16[128,2176]{1,0:T(8,128)(2,1)S(1)}, bf16[128,2176]{1,0:T(8,128)(2,1)S(1)}, u32[]{:S(2)}, u32[]{:S(2)}) collective-permute-start(bf16[128,2176]{1,0:T(8,128)(2,1)S(1)} %add.12), channel_id=1, source_target_pairs={{0,2},{1,3},{2,0},{3,1},{4,6},{5,7},{6,4},{7,5},{8,10},{9,11},{10,... | collective-permute-start | bytes 1671176 | tf_op jit(solution)/shard_map/ppermute | solution.py:421
  180.7 23.3 %collective-permute-start.42 = (bf16[128,2176]{1,0:T(8,128)(2,1)S(1)}, bf16[128,2176]{1,0:T(8,128)(2,1)S(1)}, u32[]{:S(2)}, u32[]{:S(2)}) collective-permute-start(bf16[128,2176]{1,0:T(8,128)(2,1)S(1)} %get-tuple-element.244), channel_id=1, source_target_pairs={{0,1},{1,0},{2,3},{3,2},{4,5},{5,4},{6,7},{7,6},{8,9},{9,8},{10,11... | collective-permute-start | bytes 1671176 | tf_op jit(solution)/shard_map/ppermute | solution.py:421
  189.4 16.9 %collective-permute-start.40 = (bf16[128,2176]{1,0:T(8,128)(2,1)S(1)}, bf16[128,2176]{1,0:T(8,128)(2,1)S(1)}, u32[]{:S(2)}, u32[]{:S(2)}) collective-permute-start(bf16[128,2176]{1,0:T(8,128)(2,1)S(1)} %add.19), channel_id=1, source_target_pairs={{4,12},{5,13},{6,14},{7,15},{8,0},{9,1},{10,2},{11,3},{20,28},{21,... | collective-permute-start | bytes 1671176 | tf_op jit(solution)/shard_map/ppermute | solution.py:421
  (28 other events, 226.1 us)

commit v5 on v4

--- a/solution.py
+++ b/solution.py
@@ -158,22 +158,51 @@
         body(pl.multiple_of(k * tile, tile))
 
 
-def pack_kernel(tokens, cotangent, probs, ids, out):
+def pack_kernel(tokens, cotangent, probs, ids, out, ids_here, packed, sems):
     rows, width = tokens.shape
-    out[:, :width] = cotangent[...]
-    out[:, width : 2 * width] = tokens[...]
+    moves = (
+        (ids, ids_here),
+        (cotangent, packed.at[:, pl.ds(0, width)]),
+        (tokens, packed.at[:, pl.ds(width, width)]),
+        (packed, out),
+    )
+    copies = [
+        pltpu.make_async_copy(source, target, sems.at[i])
+        for i, (source, target) in enumerate(moves)
+    ]
+    for copy in copies[:3]:
+        copy.start()
+    copies[0].wait()
     lane = lax.broadcasted_iota(jnp.int32, (rows, LANES), 1)
     routing = jnp.full((rows, LANES), -1.0, F32)
-    weights = probs[...].astype(F32)
-    for k in range(ids.shape[1]):
-        routing = jnp.where(lane == ids[:, k : k + 1], weights[:, k : k + 1], routing)
-    out[:, 2 * width :] = routing.astype(BF16)
+    weights, choices = probs[...].astype(F32).T, ids_here[...].T
+    for k in range(choices.shape[1]):
+        routing = jnp.where(lane == choices[:, k : k + 1], weights[:, k : k + 1], routing)
+    packed[:, pl.ds(2 * width, LANES)] = routing.astype(BF16)
+    copies[1].wait()
+    copies[2].wait()
+    copies[3].start()
+    copies[3].wait()
 
 
 def pack(tokens, cotangent, probs, ids):
     rows, width = tokens.shape
-    operands = (tokens, cotangent, probs, ids)
-    return kernel_call(pack_kernel, operands, [((rows, 2 * width + LANES), BF16)], name="pack")[0]
+    columns = 2 * width + LANES
+    return pl.pallas_call(
+        pack_kernel,
+        in_specs=[pl.BlockSpec(memory_space=pl.ANY)] * 2
+        + [pl.BlockSpec(memory_space=pltpu.VMEM), pl.BlockSpec(memory_space=pl.ANY)],
+        out_specs=pl.BlockSpec(memory_space=pl.ANY),
+        out_shape=jax.ShapeDtypeStruct((rows, columns), BF16),
+        scratch_shapes=[
+            pltpu.VMEM(ids.shape, ids.dtype),
+            pltpu.VMEM((rows, columns), BF16),
+            pltpu.SemaphoreType.DMA((4,)),
+        ],
+        compiler_params=pltpu.CompilerParams(vmem_limit_bytes=60 * 1024 * 1024),
+        cost_estimate=pl.CostEstimate(flops=1000, bytes_accessed=1000, transcendentals=0),
+        name="pack",
+    )(tokens, cotangent, probs, ids)
 
 
 def front_kernel(slots, layout, joined, *refs):
@@ -443,7 +472,7 @@
     features = tokens.shape[1]
     all_columns = 2 * features + LANES
 
-    p0 = pack(tokens, cotangent, router_probs, expert_ids)
+    p0 = pack(tokens, cotangent, router_probs.T, expert_ids.T)
     q0 = core(p0)
     p1, a0, m0 = across(p0), outer_z(p0), inner_z(p0)
     (state0,), (part0,) = forward(p0, q0)
@@ -507,7 +536,7 @@
 
     sumc1 = add(keep_c1, kc1)
     rc = across(sumc1)
-    rc, sum1, y0 = meet(rc, sum1, y0)
+    rc, sum1 = meet(rc, sum1)
     sumc = add(sumc0, rc)
     c_edge = outer_z(sumc, part=(0, 3))
     r0 = across(sum1)
@@ -521,13 +550,16 @@
 
     c_edge, b_edge, b_middle, _ = meet(c_edge, b_edge, b_middle, gate_grad)
     sumc = add(sumc, c_edge)
+    sumc, k0 = meet(sumc, k0)
     far = swap(sumc, 8, (1, 2))
     grad_up, _ = meet(grad_up, sumc)
     up_grad = outer(grad_up, inputs)
     hidden, _ = meet(hidden, up_grad)
     down_grad = outer(hidden, scaled)
-    far, r0, k0, _ = meet(far, r0, k0, down_grad)
-    token_grads, by_expert = finish(keep0, k0, r0, from_a, b_edge, b_middle, far)
+    r0, _ = meet(r0, down_grad)
+    near = add(keep0, k0, r0, from_a, b_edge, b_middle)
+    far, near = meet(far, near)
+    token_grads, by_expert = finish(near, far)
     chosen = expert_ids[:, :, None] == jnp.arange(experts, dtype=jnp.int32)[None, None, :]
     prob_grads = jnp.sum(jnp.where(chosen, by_expert[:, None, :experts], 0.0), axis=2)
     return (

time: 209 us -> 207 us (level)
  Pallas kernels: 63.3 us -> 65.8 us
  local copies, waits for them, and re-layouts: 9.39 us -> 6.96 us
    ppermute x7, waiting for transfers between devices: 15.9 us -> 7.96 us  [exchange(): return lax.ppermute(part, 'dp', [(0, 1), (1, 0)])]
    ppermute x36, waiting for transfers between devices: 77.2 us -> 83.9 us  [swap(): return lax.ppermute(value, 'expert', pairs)]
    pallas_call x0 -> x1, Pallas kernels: none -> 2.91 us  [pack(): pl.pallas_call(pack_kernel, in_specs=[pl.BlockSpec(memory_space=pl.ANY)]...]
    unnamed x20 -> x16, local copies, waits for them, and re-layouts: 9.34 us -> 6.92 us
  transfers between devices with their start and end apart: 43 -> 43, of which waited for: 19 -> 18; matrix products, arithmetic and copies ran while one was open for 0% -> 0% of each run, Pallas kernels for 29% -> 29%
where the time goes in v5:
time: 207 us
  waiting for transfers between devices  91.8 us (44%)
  Pallas kernels  65.8 us (32%)
  starting transfers between devices  40.8 us (20%)
  local copies, waits for them, and re-layouts  6.96 us (3%)
    ppermute x36, waiting for transfers between devices, swap(): return lax.ppermute(value, 'expert', pairs)  83.9 us
    pallas_call x26, Pallas kernels, kernel_call(): pl.pallas_call(body, in_specs=[pl.BlockSpec(memory_space=pltpu.VMEM)] * l...  42.9 us
    ppermute x36, starting transfers between devices, swap(): return lax.ppermute(value, 'expert', pairs)  31.1 us
    pallas_call x3, Pallas kernels, outer(): pl.pallas_call(functools.partial(outer_kernel, len(lefts)), grid=(width /...  20 us
    ppermute x7, starting transfers between devices, exchange(): return lax.ppermute(part, 'dp', [(0, 1), (1, 0)])  9.66 us
    ppermute x7, waiting for transfers between devices, exchange(): return lax.ppermute(part, 'dp', [(0, 1), (1, 0)])  7.96 us
    unnamed x16, local copies, waits for them, and re-layouts  6.92 us
  transfers between devices with their start and end apart: 43, of which 18 were waited for; matrix products, arithmetic and copies ran while one was open for 0% of the time, Pallas kernels for 29%

profile of v5, /device:TPU:0, one launch (start us, length us, event | category | flops | bytes accessed | tf_op | source)
XLA Modules:
  0.0 207.0 jit_solution(14819079931628619857)
XLA Ops:
  0.6 2.9 %pack.1.refs_0_ = bf16[128,4224]{1,0:T(8,128)(2,1)} custom-call(bf16[128,2048]{1,0:T(8,128)(2,1)} %tokens.1, bf16[128,2048]{1,0:T(8,128)(2,1)} %cotangent.1, bf16[8,128]{1,0:T(8,128)(2,1)} %bitcast.43, s32[8,128]{1,0:T(8,128)} %bitcast.42), custom_call_target="tpu_custom_call" | custom-call | flops 1000 | bytes 1000 | tf_op jit(solution)/shard_map/pack/pallas_call | solution.py:191
  4.1 2.6 %collective-permute-start = (bf16[128,4224]{1,0:T(8,128)(2,1)}, bf16[128,4224]{1,0:T(8,128)(2,1)S(1)}, u32[]{:S(2)}, u32[]{:S(2)}) collective-permute-start(bf16[128,4224]{1,0:T(8,128)(2,1)} %pack.1.refs_0_), channel_id=1, source_target_pairs={{0,2},{1,3},{2,0},{3,1},{4,6},{5,7},{6,4},{7,5},{8,10},{9,11},{10,... | collective-permute-start | bytes 3244040 | tf_op jit(solution)/shard_map/ppermute | solution.py:450
  15.9 4.3 %front.5 = (bf16[144,2048]{1,0:T(8,128)(2,1)S(1)}, bf16[144,2048]{1,0:T(8,128)(2,1)S(1)}, bf16[256,144]{1,0:T(8,128)(2,1)S(1)}, f32[144,128]{1,0:T(8,128)S(1)}, bf16[136,2304]{1,0:T(8,128)(2,1)S(1)}) custom-call(bf16[128,4224]{1,0:T(8,128)(2,1)S(1)} %copy-done.6, bf16[128,4224]{1,0:T(8,128)(2,1)S(1)} %collective-permute-done.3.refs_1_, ...), custom_call_target="tpu_custom_call" | custom-call | flops 1000 | bytes 1000 | tf_op jit(solution)/shard_map/front/pallas_call | solution.py:117
  20.1 11.2 %collective-permute-done.refs_0_ = bf16[128,4224]{1,0:T(8,128)(2,1)S(1)} collective-permute-done((bf16[128,4224]{1,0:T(8,128)(2,1)}, bf16[128,4224]{1,0:T(8,128)(2,1)S(1)}, u32[]{:S(2)}, u32[]{:S(2)}) %collective-permute-start) | collective-permute-done | bytes 1081376 | tf_op jit(solution)/shard_map/ppermute | solution.py:450
  37.0 4.7 %front.6 = (bf16[144,2048]{1,0:T(8,128)(2,1)S(1)}, bf16[144,2048]{1,0:T(8,128)(2,1)S(1)}, bf16[256,144]{1,0:T(8,128)(2,1)S(1)}, f32[144,128]{1,0:T(8,128)S(1)}, ...) custom-call(bf16[128,4224]{1,0:T(8,128)(2,1)S(1)} %collective-permut, ...), custom_call_target="tpu_custom_call" | custom-call | flops 1000 | bytes 1000 | tf_op jit(solution)/shard_map/front/pallas_call | solution.py:117
  43.3 19.8 %collective-permute-done.5.first = bf16[128,4224]{1,0:T(8,128)(2,1)S(1)} collective-permute-done((bf16[128,4224]{1,0:T(8,128)(2,1)S(1)}, bf16[128,4224]{1,0:T(8,128)(2,1)S(1)}, u32[]{:S(2)}, u32[]{:S(2)}) %collective-permute-start.5) | collective-permute-done | bytes 1081376 | tf_op jit(solution)/shard_map/ppermute | solution.py:450
  67.6 4.7 %front.7 = (bf16[144,2048]{1,0:T(8,128)(2,1)S(1)}, bf16[144,2048]{1,0:T(8,128)(2,1)S(1)}, bf16[256,144]{1,0:T(8,128)(2,1)S(1)}, f32[144,128]{1,0:T(8,128)S(1)}, ...) custom-call(bf16[128,4224]{1,0:T(8,128)(2,1)S(1)} %collective-permut, ...), custom_call_target="tpu_custom_call" | custom-call | flops 1000 | bytes 1000 | tf_op jit(solution)/shard_map/front/pallas_call | solution.py:117
  73.9 3.7 %back.7 = (bf16[288,768]{1,0:T(8,128)(2,1)S(1)}, bf16[288,768]{1,0:T(8,128)(2,1)S(1)}, bf16[288,768]{1,0:T(8,128)(2,1)S(1)}, bf16[128,2176]{1,0:T(8,128)(2,1)S(1...) custom-call(bf16[272,2304]{1,0:T(8,128)(2,1)S(1)} %get-tuple-element.152.own, ...), custom_call_target="tpu_custom_call" | custom-call | flops 1000 | bytes 1000 | tf_op jit(solution)/shard_map/back/pallas_call | solution.py:117
  78.1 14.9 %collective-permute-done.10.first = bf16[128,4224]{1,0:T(8,128)(2,1)S(1)} collective-permute-done((bf16[128,4224]{1,0:T(8,128)(2,1)S(1)}, bf16[128,4224]{1,0:T(8,128)(2,1)S(1)}, u32[]{:S(2)}, u32[]{:S(2)}) %collective-permute-start.10) | collective-permute-done | bytes 1081376 | tf_op jit(solution)/shard_map/ppermute | solution.py:450
  99.8 4.7 %front.8 = (bf16[144,2048]{1,0:T(8,128)(2,1)S(1)}, bf16[144,2048]{1,0:T(8,128)(2,1)S(1)}, bf16[256,144]{1,0:T(8,128)(2,1)S(1)}, f32[144,128]{1,0:T(8,128)S(1)}, ...) custom-call(bf16[128,4224]{1,0:T(8,128)(2,1)S(1)} %collective-permut, ...), custom_call_target="tpu_custom_call" | custom-call | flops 1000 | bytes 1000 | tf_op jit(solution)/shard_map/front/pallas_call | solution.py:117
  104.5 5.6 %collective-permute-done.21.peer = bf16[136,2304]{1,0:T(8,128)(2,1)S(1)} collective-permute-done((bf16[136,2304]{1,0:T(8,128)(2,1)S(1)}, bf16[136,2304]{1,0:T(8,128)(2,1)S(1)}, u32[]{:S(2)}, u32[]{:S(2)}) %collective-permute-start.21) | collective-permute-done | bytes 626720 | tf_op jit(solution)/shard_map/ppermute | solution.py:464
  114.4 6.6 %collective-permute-done.17.refs_0_ = bf16[128,2048]{1,0:T(8,128)(2,1)S(1)} collective-permute-done((bf16[128,2048]{1,0:T(8,128)(2,1)S(1)}, bf16[128,2048]{1,0:T(8,128)(2,1)S(1)}, u32[]{:S(2)}, u32[]{:S(2)}) %collective-permute-start.17) | collective-permute-done | bytes 524320 | tf_op jit(solution)/shard_map/ppermute | solution.py:450
  123.0 2.4 %collective-permute-done.23.peer = bf16[136,2304]{1,0:T(8,128)(2,1)S(1)} collective-permute-done((bf16[136,2304]{1,0:T(8,128)(2,1)S(1)}, bf16[136,2304]{1,0:T(8,128)(2,1)S(1)}, u32[]{:S(2)}, u32[]{:S(2)}) %collective-permute-start.23) | collective-permute-done | bytes 626720 | tf_op jit(solution)/shard_map/ppermute | solution.py:464
  128.5 2.2 %back.10 = (bf16[144,768]{1,0:T(8,128)(2,1)S(1)}, bf16[144,768]{1,0:T(8,128)(2,1)S(1)}, bf16[144,768]{1,0:T(8,128)(2,1)S(1)}, bf16[128,2176]{1,0:T(8,128)(2,1)S(1)}, bf16[128,2176]{1,0:T(8,128)(2,1)S(1)}) custom-call(bf16[136,2304]{1,0:T(8,128)(2,1)S(1)} %get-tuple-element.181.own, bf16[136,2304]{1,0:T(8,128)(2,1)S(1)} %collective-permute-done.23.peer, ...), custom_call_target="tpu_custom_call" | custom-call | flops 1000 | bytes 1000 | tf_op jit(solution)/shard_map/back/pallas_call | solution.py:117
  131.2 4.3 %front.9 = (bf16[144,2048]{1,0:T(8,128)(2,1)S(1)}, bf16[144,2048]{1,0:T(8,128)(2,1)S(1)}, bf16[256,144]{1,0:T(8,128)(2,1)S(1)}, f32[144,128]{1,0:T(8,128)S(1)}, bf16[136,2304]{1,0:T(8,128)(2,1)S(1)}) custom-call(bf16[128,2048]{1,0:T(8,128)(2,1)S(1)} %collective-permute-done.17.refs_0_, bf16[128,2176]{1,0:T(8,128)(2,1)S(1)} %collective-permute-done.18.refs_1_, ...), custom_call_target="tpu_custom_call" | custom-call | flops 1000 | bytes 1000 | tf_op jit(solution)/shard_map/front/pallas_call | solution.py:117
  135.5 4.2 %collective-permute-done.28.refs_2_ = bf16[128,2176]{1,0:T(8,128)(2,1)S(1)} collective-permute-done((bf16[128,2176]{1,0:T(8,128)(2,1)S(1)}, bf16[128,2176]{1,0:T(8,128)(2,1)S(1)}, u32[]{:S(2)}, u32[]{:S(2)}) %collective-permute-start.28) | collective-permute-done | bytes 557088 | tf_op jit(solution)/shard_map/ppermute | solution.py:450
  144.4 2.2 %back.11 = (bf16[144,768]{1,0:T(8,128)(2,1)S(1)}, bf16[144,768]{1,0:T(8,128)(2,1)S(1)}, bf16[144,768]{1,0:T(8,128)(2,1)S(1)}, bf16[128,2176]{1,0:T(8,128)(2,1)S(1)}, bf16[128,2176]{1,0:T(8,128)(2,1)S(1)}) custom-call(bf16[136,2304]{1,0:T(8,128)(2,1)S(1)} %get-tuple-element.189.own, bf16[136,2304]{1,0:T(8,128)(2,1)S(1)} %collective-permute-done.27.peer, ...), custom_call_target="tpu_custom_call" | custom-call | flops 1000 | bytes 1000 | tf_op jit(solution)/shard_map/back/pallas_call | solution.py:117
  146.7 6.4 %collective-permute-done.31.refs_1_ = bf16[128,2176]{1,0:T(8,128)(2,1)S(1)} collective-permute-done((bf16[128,2176]{1,0:T(8,128)(2,1)S(1)}, bf16[128,2176]{1,0:T(8,128)(2,1)S(1)}, u32[]{:S(2)}, u32[]{:S(2)}) %collective-permute-start.31) | collective-permute-done | bytes 557088 | tf_op jit(solution)/shard_map/ppermute | solution.py:450
  159.4 4.6 %collective-permute-start.37 = (bf16[128,2176]{1,0:T(8,128)(2,1)S(1)}, bf16[128,2176]{1,0:T(8,128)(2,1)S(1)}, u32[]{:S(2)}, u32[]{:S(2)}) collective-permute-start(bf16[128,2176]{1,0:T(8,128)(2,1)S(1)} %add.19), channel_id=1, source_target_pairs={{0,8},{1,9},{2,10},{3,11},{12,4},{13,5},{14,6},{15,7},{16,24},{17,... | collective-permute-start | bytes 1671176 | tf_op jit(solution)/shard_map/ppermute | solution.py:450
  165.1 8.3 %collective-permute-done.35.refs_1_ = bf16[128,2176]{1,0:T(8,128)(2,1)S(1)} collective-permute-done((bf16[128,2176]{1,0:T(8,128)(2,1)S(1)}, bf16[128,2176]{1,0:T(8,128)(2,1)S(1)}, u32[]{:S(2)}, u32[]{:S(2)}) %collective-permute-start.35) | collective-permute-done | bytes 557088 | tf_op jit(solution)/shard_map/ppermute | solution.py:450
  173.5 3.5 %collective-permute-start.36 = (bf16[128,2176]{1,0:T(8,128)(2,1)S(1)}, bf16[128,2176]{1,0:T(8,128)(2,1)S(1)}, u32[]{:S(2)}, u32[]{:S(2)}) collective-permute-start(bf16[128,2176]{1,0:T(8,128)(2,1)S(1)} %add.18.refs_0_), channel_id=1, source_target_pairs={{0,4},{1,5},{2,6},{3,7},{12,8},{13,9},{14,10},{15,11},{16,20},{17,... | collective-permute-start | bytes 1671176 | tf_op jit(solution)/shard_map/ppermute | solution.py:450
  179.9 6.7 %outer.3 = bf16[768,2048]{1,0:T(8,128)(2,1)} custom-call(bf16[288,768]{1,0:T(8,128)(2,1)S(1)} %get-tuple-element.222.refs_0_, bf16[144,768]{1,0:T(8,128)(2,1)S(1)} %get-tuple-element.223.refs_1_, bf16[144,768]{1,0:T(8,128)(2,1)S(1)} %get-tuple-element.224.refs_2_, bf16[144,768]{1,0:T(8,128)(2,1)S(1)} %get-tuple-element.225.refs_3_, ...), custom_call_target="tpu_custom_call" | custom-call | flops 1000 | bytes 1000 | tf_op jit(solution)/shard_map/outer/pallas_call | solution.py:395
  189.7 6.7 %outer.4 = bf16[768,2048]{1,0:T(8,128)(2,1)} custom-call(bf16[288,768]{1,0:T(8,128)(2,1)S(1)} %get-tuple-element.261.refs_0_, bf16[144,768]{1,0:T(8,128)(2,1)S(1)} %get-tuple-element.262.refs_1_, bf16[144,768]{1,0:T(8,128)(2,1)S(1)} %get-tuple-element.263.refs_2_, bf16[144,768]{1,0:T(8,128)(2,1)S(1)} %get-tuple-element.264.refs_3_, ...), custom_call_target="tpu_custom_call" | custom-call | flops 1000 | bytes 1000 | tf_op jit(solution)/shard_map/outer/pallas_call | solution.py:395
  196.4 6.7 %outer.5 = bf16[768,2048]{1,0:T(8,128)(2,1)} custom-call(bf16[288,768]{1,0:T(8,128)(2,1)S(1)} %get-tuple-element.268.refs_0_, bf16[144,768]{1,0:T(8,128)(2,1)S(1)} %get-tuple-element.269.refs_1_, bf16[144,768]{1,0:T(8,128)(2,1)S(1)} %get-tuple-element.270.refs_2_, bf16[144,768]{1,0:T(8,128)(2,1)S(1)} %get-tuple-element.271.refs_3_, ...), custom_call_target="tpu_custom_call" | custom-call | flops 1000 | bytes 1000 | tf_op jit(solution)/shard_map/outer/pallas_call | solution.py:395
  (110 shorter events, 62.3 us)
Async XLA Ops:
  4.1 27.2 %collective-permute-start = (bf16[128,4224]{1,0:T(8,128)(2,1)}, bf16[128,4224]{1,0:T(8,128)(2,1)S(1)}, u32[]{:S(2)}, u32[]{:S(2)}) collective-permute-start(bf16[128,4224]{1,0:T(8,128)(2,1)} %pack.1.refs_0_), channel_id=1, source_target_pairs={{0,2},{1,3},{2,0},{3,1},{4,6},{5,7},{6,4},{7,5},{8,10},{9,11},{10,... | collective-permute-start | bytes 3244040 | tf_op jit(solution)/shard_map/ppermute | solution.py:450
  6.6 26.1 %collective-permute-start.1 = (bf16[128,4224]{1,0:T(8,128)(2,1)}, bf16[128,4224]{1,0:T(8,128)(2,1)S(1)}, u32[]{:S(2)}, u32[]{:S(2)}) collective-permute-start(bf16[128,4224]{1,0:T(8,128)(2,1)} %pack.1.refs_0_), channel_id=1, source_target_pairs={{0,4},{1,5},{2,6},{3,7},{4,0},{5,1},{6,2},{7,3},{8,12},{9,13},{10,... | collective-permute-start | bytes 3244040 | tf_op jit(solution)/shard_map/ppermute | solution.py:450
  8.2 24.6 %collective-permute-start.2 = (bf16[128,4224]{1,0:T(8,128)(2,1)}, bf16[128,4224]{1,0:T(8,128)(2,1)S(1)}, u32[]{:S(2)}, u32[]{:S(2)}) collective-permute-start(bf16[128,4224]{1,0:T(8,128)(2,1)} %pack.1.refs_0_), channel_id=1, source_target_pairs={{4,8},{5,9},{6,10},{7,11},{8,4},{9,5},{10,6},{11,7},{20,24},{21,25... | collective-permute-start | bytes 3244040 | tf_op jit(solution)/shard_map/ppermute | solution.py:450
  33.3 29.9 %collective-permute-start.5 = (bf16[128,4224]{1,0:T(8,128)(2,1)S(1)}, bf16[128,4224]{1,0:T(8,128)(2,1)S(1)}, u32[]{:S(2)}, u32[]{:S(2)}) collective-permute-start(bf16[128,4224]{1,0:T(8,128)(2,1)S(1)} %collective-permute-done.2.second), channel_id=1, source_target_pairs={{4,0},{5,1},{6,2},{7,3},{8,12},{9,13},{10,14},{11,15},{20,16},{21,... | collective-permute-start | bytes 3244040 | tf_op jit(solution)/shard_map/ppermute | solution.py:450
  34.6 28.7 %collective-permute-start.4 = (bf16[128,4224]{1,0:T(8,128)(2,1)S(1)}, bf16[128,4224]{1,0:T(8,128)(2,1)S(1)}, u32[]{:S(2)}, u32[]{:S(2)}) collective-permute-start(bf16[128,4224]{1,0:T(8,128)(2,1)S(1)} %collective-permute-done.1.refs_2_), channel_id=1, source_target_pairs={{0,2},{1,3},{2,0},{3,1},{4,6},{5,7},{6,4},{7,5},{8,10},{9,11},{10,... | collective-permute-start | bytes 3244040 | tf_op jit(solution)/shard_map/ppermute | solution.py:450
  35.0 28.2 %collective-permute-start.6 = (bf16[128,4224]{1,0:T(8,128)(2,1)S(1)}, bf16[128,4224]{1,0:T(8,128)(2,1)S(1)}, u32[]{:S(2)}, u32[]{:S(2)}) collective-permute-start(bf16[128,4224]{1,0:T(8,128)(2,1)S(1)} %collective-permute-done.1.refs_2_), channel_id=1, source_target_pairs={{4,8},{5,9},{6,10},{7,11},{8,4},{9,5},{10,6},{11,7},{20,24},{21,25... | collective-permute-start | bytes 3244040 | tf_op jit(solution)/shard_map/ppermute | solution.py:450
  41.7 30.5 %collective-permute-start.11 = (bf16[272,2304]{1,0:T(8,128)(2,1)S(1)}, bf16[272,2304]{1,0:T(8,128)(2,1)S(1)}, u32[]{:S(2)}, u32[]{:S(2)}) collective-permute-start(bf16[272,2304]{1,0:T(8,128)(2,1)S(1)} %get-tuple-element.152.own), channel_id=1, source_target_pairs={{0,16},{16,0},{1,17},{17,1},{2,18},{18,2},{3,19},{19,3},{4,20},{20... | collective-permute-start | bytes 3760136 | tf_op jit(solution)/shard_map/ppermute | solution.py:464
  63.9 29.2 %collective-permute-start.10 = (bf16[128,4224]{1,0:T(8,128)(2,1)S(1)}, bf16[128,4224]{1,0:T(8,128)(2,1)S(1)}, u32[]{:S(2)}, u32[]{:S(2)}) collective-permute-start(bf16[128,4224]{1,0:T(8,128)(2,1)S(1)} %collective-permute-done.6.second), channel_id=1, source_target_pairs={{4,0},{5,1},{6,2},{7,3},{8,12},{9,13},{10,14},{11,15},{20,16},{21,... | collective-permute-start | bytes 3244040 | tf_op jit(solution)/shard_map/ppermute | solution.py:450
  65.1 28.2 %collective-permute-start.9 = (bf16[128,4224]{1,0:T(8,128)(2,1)S(1)}, bf16[128,4224]{1,0:T(8,128)(2,1)S(1)}, u32[]{:S(2)}, u32[]{:S(2)}) collective-permute-start(bf16[128,4224]{1,0:T(8,128)(2,1)S(1)} %choose.2.refs_2_), channel_id=1, source_target_pairs={{0,2},{1,3},{2,0},{3,1},{4,6},{5,7},{6,4},{7,5},{8,10},{9,11},{10,... | collective-permute-start | bytes 3244040 | tf_op jit(solution)/shard_map/ppermute | solution.py:450
  72.3 21.1 %collective-permute-start.14 = (bf16[136,2304]{1,0:T(8,128)(2,1)S(1)}, bf16[136,2304]{1,0:T(8,128)(2,1)S(1)}, u32[]{:S(2)}, u32[]{:S(2)}) collective-permute-start(bf16[136,2304]{1,0:T(8,128)(2,1)S(1)} %get-tuple-element.160.own), channel_id=1, source_target_pairs={{0,16},{16,0},{1,17},{17,1},{2,18},{18,2},{3,19},{19,3},{4,20},{20... | collective-permute-start | bytes 1880072 | tf_op jit(solution)/shard_map/ppermute | solution.py:464
  77.5 15.8 %collective-permute-start.15 = (bf16[128,2176]{1,0:T(8,128)(2,1)S(1)}, bf16[128,2176]{1,0:T(8,128)(2,1)S(1)}, u32[]{:S(2)}, u32[]{:S(2)}) collective-permute-start(bf16[128,2176]{1,0:T(8,128)(2,1)S(1)} %get-tuple-element.167), channel_id=1, source_target_pairs={{0,1},{1,0},{2,3},{3,2},{4,5},{5,4},{6,7},{7,6},{8,9},{9,8},{10,11... | collective-permute-start | bytes 1671176 | tf_op jit(solution)/shard_map/ppermute | solution.py:450
  77.6 15.7 %collective-permute-start.16 = (bf16[128,2176]{1,0:T(8,128)(2,1)S(1)}, bf16[128,2176]{1,0:T(8,128)(2,1)S(1)}, u32[]{:S(2)}, u32[]{:S(2)}) collective-permute-start(bf16[128,2176]{1,0:T(8,128)(2,1)S(1)} %get-tuple-element.168), channel_id=1, source_target_pairs={{0,1},{1,0},{2,3},{3,2},{4,5},{5,4},{6,7},{7,6},{8,9},{9,8},{10,11... | collective-permute-start | bytes 1671176 | tf_op jit(solution)/shard_map/ppermute | solution.py:450
  94.0 16.1 %collective-permute-start.21 = (bf16[136,2304]{1,0:T(8,128)(2,1)S(1)}, bf16[136,2304]{1,0:T(8,128)(2,1)S(1)}, u32[]{:S(2)}, u32[]{:S(2)}) collective-permute-start(bf16[136,2304]{1,0:T(8,128)(2,1)S(1)} %get-tuple-element.174.own), channel_id=1, source_target_pairs={{0,16},{16,0},{1,17},{17,1},{2,18},{18,2},{3,19},{19,3},{4,20},{20... | collective-permute-start | bytes 1880072 | tf_op jit(solution)/shard_map/ppermute | solution.py:464
  95.5 16.1 %collective-permute-start.18 = (bf16[128,2176]{1,0:T(8,128)(2,1)S(1)}, bf16[128,2176]{1,0:T(8,128)(2,1)S(1)}, u32[]{:S(2)}, u32[]{:S(2)}) collective-permute-start(bf16[128,2176]{1,0:T(8,128)(2,1)S(1)} %get-tuple-element.170), channel_id=1, source_target_pairs={{0,2},{1,3},{2,0},{3,1},{4,6},{5,7},{6,4},{7,5},{8,10},{9,11},{10,... | collective-permute-start | bytes 1671176 | tf_op jit(solution)/shard_map/ppermute | solution.py:450
  97.0 24.1 %collective-permute-start.17 = (bf16[128,2048]{1,0:T(8,128)(2,1)S(1)}, bf16[128,2048]{1,0:T(8,128)(2,1)S(1)}, u32[]{:S(2)}, u32[]{:S(2)}) collective-permute-start(bf16[128,2048]{1,0:T(8,128)(2,1)S(1)} %get-tuple-element.169), channel_id=1, source_target_pairs={{0,2},{1,3},{2,0},{3,1},{4,6},{5,7},{6,4},{7,5},{8,10},{9,11},{10,... | collective-permute-start | bytes 1572872 | tf_op jit(solution)/shard_map/ppermute | solution.py:450
  110.1 15.3 %collective-permute-start.23 = (bf16[136,2304]{1,0:T(8,128)(2,1)S(1)}, bf16[136,2304]{1,0:T(8,128)(2,1)S(1)}, u32[]{:S(2)}, u32[]{:S(2)}) collective-permute-start(bf16[136,2304]{1,0:T(8,128)(2,1)S(1)} %get-tuple-element.181.own), channel_id=1, source_target_pairs={{0,16},{16,0},{1,17},{17,1},{2,18},{18,2},{3,19},{19,3},{4,20},{20... | collective-permute-start | bytes 1880072 | tf_op jit(solution)/shard_map/ppermute | solution.py:464
  125.3 14.5 %collective-permute-start.27 = (bf16[136,2304]{1,0:T(8,128)(2,1)S(1)}, bf16[136,2304]{1,0:T(8,128)(2,1)S(1)}, u32[]{:S(2)}, u32[]{:S(2)}) collective-permute-start(bf16[136,2304]{1,0:T(8,128)(2,1)S(1)} %get-tuple-element.189.own), channel_id=1, source_target_pairs={{0,16},{16,0},{1,17},{17,1},{2,18},{18,2},{3,19},{19,3},{4,20},{20... | collective-permute-start | bytes 1880072 | tf_op jit(solution)/shard_map/ppermute | solution.py:464
  156.6 20.4 %collective-permute-start.39 = (bf16[136,2304]{1,0:T(8,128)(2,1)S(1)}, bf16[136,2304]{1,0:T(8,128)(2,1)S(1)}, u32[]{:S(2)}, u32[]{:S(2)}) collective-permute-start(bf16[136,2304]{1,0:T(8,128)(2,1)S(1)} %get-tuple-element.228.own), channel_id=1, source_target_pairs={{0,16},{16,0},{1,17},{17,1},{2,18},{18,2},{3,19},{19,3},{4,20},{20... | collective-permute-start | bytes 1880072 | tf_op jit(solution)/shard_map/ppermute | solution.py:464
  158.6 14.7 %collective-permute-start.35 = (bf16[128,2176]{1,0:T(8,128)(2,1)S(1)}, bf16[128,2176]{1,0:T(8,128)(2,1)S(1)}, u32[]{:S(2)}, u32[]{:S(2)}) collective-permute-start(bf16[128,2176]{1,0:T(8,128)(2,1)S(1)} %add.17), channel_id=1, source_target_pairs={{0,2},{1,3},{2,0},{3,1},{4,6},{5,7},{6,4},{7,5},{8,10},{9,11},{10,... | collective-permute-start | bytes 1671176 | tf_op jit(solution)/shard_map/ppermute | solution.py:450
  159.4 27.2 %collective-permute-start.37 = (bf16[128,2176]{1,0:T(8,128)(2,1)S(1)}, bf16[128,2176]{1,0:T(8,128)(2,1)S(1)}, u32[]{:S(2)}, u32[]{:S(2)}) collective-permute-start(bf16[128,2176]{1,0:T(8,128)(2,1)S(1)} %add.19), channel_id=1, source_target_pairs={{0,8},{1,9},{2,10},{3,11},{12,4},{13,5},{14,6},{15,7},{16,24},{17,... | collective-permute-start | bytes 1671176 | tf_op jit(solution)/shard_map/ppermute | solution.py:450
  164.0 22.6 %collective-permute-start.38 = (bf16[128,2176]{1,0:T(8,128)(2,1)S(1)}, bf16[128,2176]{1,0:T(8,128)(2,1)S(1)}, u32[]{:S(2)}, u32[]{:S(2)}) collective-permute-start(bf16[128,2176]{1,0:T(8,128)(2,1)S(1)} %add.19), channel_id=1, source_target_pairs={{4,8},{5,9},{6,10},{7,11},{8,4},{9,5},{10,6},{11,7},{20,24},{21,25... | collective-permute-start | bytes 1671176 | tf_op jit(solution)/shard_map/ppermute | solution.py:450
  173.5 14.8 %collective-permute-start.36 = (bf16[128,2176]{1,0:T(8,128)(2,1)S(1)}, bf16[128,2176]{1,0:T(8,128)(2,1)S(1)}, u32[]{:S(2)}, u32[]{:S(2)}) collective-permute-start(bf16[128,2176]{1,0:T(8,128)(2,1)S(1)} %add.18.refs_0_), channel_id=1, source_target_pairs={{0,4},{1,5},{2,6},{3,7},{12,8},{13,9},{14,10},{15,11},{16,20},{17,... | collective-permute-start | bytes 1671176 | tf_op jit(solution)/shard_map/ppermute | solution.py:450
  179.3 23.8 %collective-permute-start.42 = (bf16[128,2176]{1,0:T(8,128)(2,1)S(1)}, bf16[128,2176]{1,0:T(8,128)(2,1)S(1)}, u32[]{:S(2)}, u32[]{:S(2)}) collective-permute-start(bf16[128,2176]{1,0:T(8,128)(2,1)S(1)} %add.13), channel_id=1, source_target_pairs={{0,2},{1,3},{2,0},{3,1},{4,6},{5,7},{6,4},{7,5},{8,10},{9,11},{10,... | collective-permute-start | bytes 1671176 | tf_op jit(solution)/shard_map/ppermute | solution.py:450
  188.4 17.0 %collective-permute-start.41 = (bf16[128,2176]{1,0:T(8,128)(2,1)S(1)}, bf16[128,2176]{1,0:T(8,128)(2,1)S(1)}, u32[]{:S(2)}, u32[]{:S(2)}) collective-permute-start(bf16[128,2176]{1,0:T(8,128)(2,1)S(1)} %add.20), channel_id=1, source_target_pairs={{4,12},{5,13},{6,14},{7,15},{8,0},{9,1},{10,2},{11,3},{20,28},{21,... | collective-permute-start | bytes 1671176 | tf_op jit(solution)/shard_map/ppermute | solution.py:450
  (27 other events, 218.5 us)

commit v6 on v5

--- a/solution.py
+++ b/solution.py
@@ -453,7 +453,6 @@
     across = functools.partial(swap, bits=2)
     outer_z = functools.partial(swap, bits=4)
     inner_z = functools.partial(swap, bits=12, part=(1, 2))
-    to_edge = functools.partial(swap, bits=4, part=(1, 2))
 
     rights, lefts = [], []
 
@@ -478,13 +477,13 @@
     (state0,), (part0,) = forward(p0, q0)
 
     p1, a0, m0, part0 = meet(p1, a0, m0, part0)
-    a1, b0e, c0m = across(a0), to_edge(m0), inner_z(a0)
+    a1, b0e, c0m = across(a0), outer_z(m0), inner_z(a0)
     states1, (part1,) = forward(p1, core(p1), a0, core(a0), joined=True)
     y1 = exchange(part1)
 
     (b0,) = choose(b0e, m0, (0, all_columns))
     a1, b0, c0m, _ = meet(a1, b0, c0m, part1)
-    b1, c0e = across(b0), to_edge(c0m)
+    b1, c0e = across(b0), outer_z(c0m)
     (state_a1, state_b0), (part_a1, part_b0) = forward(a1, core(a1), b0, core(b0))
 
     y1, part_a1 = meet(y1, part_a1)

time: 207 us -> 205 us (level)
  waiting for transfers between devices: 91.8 us -> 86.8 us
  starting transfers between devices: 40.8 us -> 43.3 us
    ppermute x36, waiting for transfers between devices: 83.9 us -> 78.5 us  [swap(): return lax.ppermute(value, 'expert', pairs)]
    ppermute x36, starting transfers between devices: 31.1 us -> 33.8 us  [swap(): return lax.ppermute(value, 'expert', pairs)]
where the time goes in v6:
time: 205 us
  waiting for transfers between devices  86.8 us (42%)
  Pallas kernels  65.8 us (32%)
  starting transfers between devices  43.3 us (21%)
  local copies, waits for them, and re-layouts  6.96 us (3%)
    ppermute x36, waiting for transfers between devices, swap(): return lax.ppermute(value, 'expert', pairs)  78.5 us
    pallas_call x26, Pallas kernels, kernel_call(): pl.pallas_call(body, in_specs=[pl.BlockSpec(memory_space=pltpu.VMEM)] * l...  42.8 us
    ppermute x36, starting transfers between devices, swap(): return lax.ppermute(value, 'expert', pairs)  33.8 us
    pallas_call x3, Pallas kernels, outer(): pl.pallas_call(functools.partial(outer_kernel, len(lefts)), grid=(width /...  20 us
    ppermute x7, starting transfers between devices, exchange(): return lax.ppermute(part, 'dp', [(0, 1), (1, 0)])  9.59 us
    ppermute x7, waiting for transfers between devices, exchange(): return lax.ppermute(part, 'dp', [(0, 1), (1, 0)])  8.33 us
    unnamed x16, local copies, waits for them, and re-layouts  6.92 us
  transfers between devices with their start and end apart: 43, of which 18 were waited for; matrix products, arithmetic and copies ran while one was open for 0% of the time, Pallas kernels for 29%

profile of v6, /device:TPU:0, one launch (start us, length us, event | category | flops | bytes accessed | tf_op | source)
XLA Modules:
  0.0 204.6 jit_solution(1595761059439795880)
XLA Ops:
  0.6 2.9 %pack.1.refs_0_ = bf16[128,4224]{1,0:T(8,128)(2,1)} custom-call(bf16[128,2048]{1,0:T(8,128)(2,1)} %tokens.1, bf16[128,2048]{1,0:T(8,128)(2,1)} %cotangent.1, bf16[8,128]{1,0:T(8,128)(2,1)} %bitcast.43, s32[8,128]{1,0:T(8,128)} %bitcast.42), custom_call_target="tpu_custom_call" | custom-call | flops 1000 | bytes 1000 | tf_op jit(solution)/shard_map/pack/pallas_call | solution.py:191
  4.1 2.6 %collective-permute-start = (bf16[128,4224]{1,0:T(8,128)(2,1)}, bf16[128,4224]{1,0:T(8,128)(2,1)S(1)}, u32[]{:S(2)}, u32[]{:S(2)}) collective-permute-start(bf16[128,4224]{1,0:T(8,128)(2,1)} %pack.1.refs_0_), channel_id=1, source_target_pairs={{0,2},{1,3},{2,0},{3,1},{4,6},{5,7},{6,4},{7,5},{8,10},{9,11},{10,... | collective-permute-start | bytes 3244040 | tf_op jit(solution)/shard_map/ppermute | solution.py:450
  15.9 4.3 %front.5 = (bf16[144,2048]{1,0:T(8,128)(2,1)S(1)}, bf16[144,2048]{1,0:T(8,128)(2,1)S(1)}, bf16[256,144]{1,0:T(8,128)(2,1)S(1)}, f32[144,128]{1,0:T(8,128)S(1)}, bf16[136,2304]{1,0:T(8,128)(2,1)S(1)}) custom-call(bf16[128,4224]{1,0:T(8,128)(2,1)S(1)} %copy-done.6, bf16[128,4224]{1,0:T(8,128)(2,1)S(1)} %collective-permute-done.3.refs_1_, ...), custom_call_target="tpu_custom_call" | custom-call | flops 1000 | bytes 1000 | tf_op jit(solution)/shard_map/front/pallas_call | solution.py:117
  20.1 11.2 %collective-permute-done.refs_0_ = bf16[128,4224]{1,0:T(8,128)(2,1)S(1)} collective-permute-done((bf16[128,4224]{1,0:T(8,128)(2,1)}, bf16[128,4224]{1,0:T(8,128)(2,1)S(1)}, u32[]{:S(2)}, u32[]{:S(2)}) %collective-permute-start) | collective-permute-done | bytes 1081376 | tf_op jit(solution)/shard_map/ppermute | solution.py:450
  33.3 4.6 %collective-permute-start.5 = (bf16[128,4224]{1,0:T(8,128)(2,1)S(1)}, bf16[128,4224]{1,0:T(8,128)(2,1)S(1)}, u32[]{:S(2)}, u32[]{:S(2)}) collective-permute-start(bf16[128,4224]{1,0:T(8,128)(2,1)S(1)} %collective-permute-done.2.second), channel_id=1, source_target_pairs={{0,4},{1,5},{2,6},{3,7},{4,0},{5,1},{6,2},{7,3},{8,12},{9,13},{10,... | collective-permute-start | bytes 3244040 | tf_op jit(solution)/shard_map/ppermute | solution.py:450
  39.2 4.7 %front.6 = (bf16[144,2048]{1,0:T(8,128)(2,1)S(1)}, bf16[144,2048]{1,0:T(8,128)(2,1)S(1)}, bf16[256,144]{1,0:T(8,128)(2,1)S(1)}, f32[144,128]{1,0:T(8,128)S(1)}, ...) custom-call(bf16[128,4224]{1,0:T(8,128)(2,1)S(1)} %collective-permut, ...), custom_call_target="tpu_custom_call" | custom-call | flops 1000 | bytes 1000 | tf_op jit(solution)/shard_map/front/pallas_call | solution.py:117
  45.5 16.4 %collective-permute-done.5.first = bf16[128,4224]{1,0:T(8,128)(2,1)S(1)} collective-permute-done((bf16[128,4224]{1,0:T(8,128)(2,1)S(1)}, bf16[128,4224]{1,0:T(8,128)(2,1)S(1)}, u32[]{:S(2)}, u32[]{:S(2)}) %collective-permute-start.5) | collective-permute-done | bytes 1081376 | tf_op jit(solution)/shard_map/ppermute | solution.py:450
  63.9 2.4 %collective-permute-start.10 = (bf16[128,4224]{1,0:T(8,128)(2,1)S(1)}, bf16[128,4224]{1,0:T(8,128)(2,1)S(1)}, u32[]{:S(2)}, u32[]{:S(2)}) collective-permute-start(bf16[128,4224]{1,0:T(8,128)(2,1)S(1)} %collective-permute-done.6.second), channel_id=1, source_target_pairs={{0,4},{1,5},{2,6},{3,7},{4,0},{5,1},{6,2},{7,3},{8,12},{9,13},{10,... | collective-permute-start | bytes 3244040 | tf_op jit(solution)/shard_map/ppermute | solution.py:450
  67.8 4.7 %front.7 = (bf16[144,2048]{1,0:T(8,128)(2,1)S(1)}, bf16[144,2048]{1,0:T(8,128)(2,1)S(1)}, bf16[256,144]{1,0:T(8,128)(2,1)S(1)}, f32[144,128]{1,0:T(8,128)S(1)}, ...) custom-call(bf16[128,4224]{1,0:T(8,128)(2,1)S(1)} %collective-permut, ...), custom_call_target="tpu_custom_call" | custom-call | flops 1000 | bytes 1000 | tf_op jit(solution)/shard_map/front/pallas_call | solution.py:117
  74.4 3.7 %back.7 = (bf16[288,768]{1,0:T(8,128)(2,1)S(1)}, bf16[288,768]{1,0:T(8,128)(2,1)S(1)}, bf16[288,768]{1,0:T(8,128)(2,1)S(1)}, bf16[128,2176]{1,0:T(8,128)(2,1)S(1...) custom-call(bf16[272,2304]{1,0:T(8,128)(2,1)S(1)} %get-tuple-element.152.own, ...), custom_call_target="tpu_custom_call" | custom-call | flops 1000 | bytes 1000 | tf_op jit(solution)/shard_map/back/pallas_call | solution.py:117
  78.6 11.7 %collective-permute-done.10.first = bf16[128,4224]{1,0:T(8,128)(2,1)S(1)} collective-permute-done((bf16[128,4224]{1,0:T(8,128)(2,1)S(1)}, bf16[128,4224]{1,0:T(8,128)(2,1)S(1)}, u32[]{:S(2)}, u32[]{:S(2)}) %collective-permute-start.10) | collective-permute-done | bytes 1081376 | tf_op jit(solution)/shard_map/ppermute | solution.py:450
  98.2 4.7 %front.8 = (bf16[144,2048]{1,0:T(8,128)(2,1)S(1)}, bf16[144,2048]{1,0:T(8,128)(2,1)S(1)}, bf16[256,144]{1,0:T(8,128)(2,1)S(1)}, f32[144,128]{1,0:T(8,128)S(1)}, ...) custom-call(bf16[128,4224]{1,0:T(8,128)(2,1)S(1)} %collective-permut, ...), custom_call_target="tpu_custom_call" | custom-call | flops 1000 | bytes 1000 | tf_op jit(solution)/shard_map/front/pallas_call | solution.py:117
  102.9 5.6 %collective-permute-done.21.peer = bf16[136,2304]{1,0:T(8,128)(2,1)S(1)} collective-permute-done((bf16[136,2304]{1,0:T(8,128)(2,1)S(1)}, bf16[136,2304]{1,0:T(8,128)(2,1)S(1)}, u32[]{:S(2)}, u32[]{:S(2)}) %collective-permute-start.21) | collective-permute-done | bytes 626720 | tf_op jit(solution)/shard_map/ppermute | solution.py:463
  112.8 6.6 %collective-permute-done.17.refs_0_ = bf16[128,2048]{1,0:T(8,128)(2,1)S(1)} collective-permute-done((bf16[128,2048]{1,0:T(8,128)(2,1)S(1)}, bf16[128,2048]{1,0:T(8,128)(2,1)S(1)}, u32[]{:S(2)}, u32[]{:S(2)}) %collective-permute-start.17) | collective-permute-done | bytes 524320 | tf_op jit(solution)/shard_map/ppermute | solution.py:450
  121.4 2.4 %collective-permute-done.23.peer = bf16[136,2304]{1,0:T(8,128)(2,1)S(1)} collective-permute-done((bf16[136,2304]{1,0:T(8,128)(2,1)S(1)}, bf16[136,2304]{1,0:T(8,128)(2,1)S(1)}, u32[]{:S(2)}, u32[]{:S(2)}) %collective-permute-start.23) | collective-permute-done | bytes 626720 | tf_op jit(solution)/shard_map/ppermute | solution.py:463
  129.6 4.3 %front.9 = (bf16[144,2048]{1,0:T(8,128)(2,1)S(1)}, bf16[144,2048]{1,0:T(8,128)(2,1)S(1)}, bf16[256,144]{1,0:T(8,128)(2,1)S(1)}, f32[144,128]{1,0:T(8,128)S(1)}, bf16[136,2304]{1,0:T(8,128)(2,1)S(1)}) custom-call(bf16[128,2048]{1,0:T(8,128)(2,1)S(1)} %collective-permute-done.17.refs_0_, bf16[128,2176]{1,0:T(8,128)(2,1)S(1)} %collective-permute-done.18.refs_1_, ...), custom_call_target="tpu_custom_call" | custom-call | flops 1000 | bytes 1000 | tf_op jit(solution)/shard_map/front/pallas_call | solution.py:117
  133.9 4.2 %collective-permute-done.28.refs_2_ = bf16[128,2176]{1,0:T(8,128)(2,1)S(1)} collective-permute-done((bf16[128,2176]{1,0:T(8,128)(2,1)S(1)}, bf16[128,2176]{1,0:T(8,128)(2,1)S(1)}, u32[]{:S(2)}, u32[]{:S(2)}) %collective-permute-start.28) | collective-permute-done | bytes 557088 | tf_op jit(solution)/shard_map/ppermute | solution.py:450
  144.2 7.3 %collective-permute-done.31.refs_1_ = bf16[128,2176]{1,0:T(8,128)(2,1)S(1)} collective-permute-done((bf16[128,2176]{1,0:T(8,128)(2,1)S(1)}, bf16[128,2176]{1,0:T(8,128)(2,1)S(1)}, u32[]{:S(2)}, u32[]{:S(2)}) %collective-permute-start.31) | collective-permute-done | bytes 557088 | tf_op jit(solution)/shard_map/ppermute | solution.py:450
  157.8 3.7 %collective-permute-start.37 = (bf16[128,2176]{1,0:T(8,128)(2,1)S(1)}, bf16[128,2176]{1,0:T(8,128)(2,1)S(1)}, u32[]{:S(2)}, u32[]{:S(2)}) collective-permute-start(bf16[128,2176]{1,0:T(8,128)(2,1)S(1)} %add.19), channel_id=1, source_target_pairs={{0,8},{1,9},{2,10},{3,11},{12,4},{13,5},{14,6},{15,7},{16,24},{17,... | collective-permute-start | bytes 1671176 | tf_op jit(solution)/shard_map/ppermute | solution.py:450
  162.6 9.2 %collective-permute-done.35.refs_1_ = bf16[128,2176]{1,0:T(8,128)(2,1)S(1)} collective-permute-done((bf16[128,2176]{1,0:T(8,128)(2,1)S(1)}, bf16[128,2176]{1,0:T(8,128)(2,1)S(1)}, u32[]{:S(2)}, u32[]{:S(2)}) %collective-permute-start.35) | collective-permute-done | bytes 557088 | tf_op jit(solution)/shard_map/ppermute | solution.py:450
  171.9 2.6 %collective-permute-start.36 = (bf16[128,2176]{1,0:T(8,128)(2,1)S(1)}, bf16[128,2176]{1,0:T(8,128)(2,1)S(1)}, u32[]{:S(2)}, u32[]{:S(2)}) collective-permute-start(bf16[128,2176]{1,0:T(8,128)(2,1)S(1)} %add.18.refs_0_), channel_id=1, source_target_pairs={{0,4},{1,5},{2,6},{3,7},{12,8},{13,9},{14,10},{15,11},{16,20},{17,... | collective-permute-start | bytes 1671176 | tf_op jit(solution)/shard_map/ppermute | solution.py:450
  177.4 6.7 %outer.3 = bf16[768,2048]{1,0:T(8,128)(2,1)} custom-call(bf16[288,768]{1,0:T(8,128)(2,1)S(1)} %get-tuple-element.222.refs_0_, bf16[144,768]{1,0:T(8,128)(2,1)S(1)} %get-tuple-element.223.refs_1_, bf16[144,768]{1,0:T(8,128)(2,1)S(1)} %get-tuple-element.224.refs_2_, bf16[144,768]{1,0:T(8,128)(2,1)S(1)} %get-tuple-element.225.refs_3_, ...), custom_call_target="tpu_custom_call" | custom-call | flops 1000 | bytes 1000 | tf_op jit(solution)/shard_map/outer/pallas_call | solution.py:395
  187.3 6.7 %outer.4 = bf16[768,2048]{1,0:T(8,128)(2,1)} custom-call(bf16[288,768]{1,0:T(8,128)(2,1)S(1)} %get-tuple-element.261.refs_0_, bf16[144,768]{1,0:T(8,128)(2,1)S(1)} %get-tuple-element.262.refs_1_, bf16[144,768]{1,0:T(8,128)(2,1)S(1)} %get-tuple-element.263.refs_2_, bf16[144,768]{1,0:T(8,128)(2,1)S(1)} %get-tuple-element.264.refs_3_, ...), custom_call_target="tpu_custom_call" | custom-call | flops 1000 | bytes 1000 | tf_op jit(solution)/shard_map/outer/pallas_call | solution.py:395
  193.9 6.7 %outer.5 = bf16[768,2048]{1,0:T(8,128)(2,1)} custom-call(bf16[288,768]{1,0:T(8,128)(2,1)S(1)} %get-tuple-element.268.refs_0_, bf16[144,768]{1,0:T(8,128)(2,1)S(1)} %get-tuple-element.269.refs_1_, bf16[144,768]{1,0:T(8,128)(2,1)S(1)} %get-tuple-element.270.refs_2_, bf16[144,768]{1,0:T(8,128)(2,1)S(1)} %get-tuple-element.271.refs_3_, ...), custom_call_target="tpu_custom_call" | custom-call | flops 1000 | bytes 1000 | tf_op jit(solution)/shard_map/outer/pallas_call | solution.py:395
  (110 shorter events, 64.0 us)
Async XLA Ops:
  4.1 27.2 %collective-permute-start = (bf16[128,4224]{1,0:T(8,128)(2,1)}, bf16[128,4224]{1,0:T(8,128)(2,1)S(1)}, u32[]{:S(2)}, u32[]{:S(2)}) collective-permute-start(bf16[128,4224]{1,0:T(8,128)(2,1)} %pack.1.refs_0_), channel_id=1, source_target_pairs={{0,2},{1,3},{2,0},{3,1},{4,6},{5,7},{6,4},{7,5},{8,10},{9,11},{10,... | collective-permute-start | bytes 3244040 | tf_op jit(solution)/shard_map/ppermute | solution.py:450
  6.6 26.1 %collective-permute-start.1 = (bf16[128,4224]{1,0:T(8,128)(2,1)}, bf16[128,4224]{1,0:T(8,128)(2,1)S(1)}, u32[]{:S(2)}, u32[]{:S(2)}) collective-permute-start(bf16[128,4224]{1,0:T(8,128)(2,1)} %pack.1.refs_0_), channel_id=1, source_target_pairs={{0,4},{1,5},{2,6},{3,7},{4,0},{5,1},{6,2},{7,3},{8,12},{9,13},{10,... | collective-permute-start | bytes 3244040 | tf_op jit(solution)/shard_map/ppermute | solution.py:450
  8.2 24.6 %collective-permute-start.2 = (bf16[128,4224]{1,0:T(8,128)(2,1)}, bf16[128,4224]{1,0:T(8,128)(2,1)S(1)}, u32[]{:S(2)}, u32[]{:S(2)}) collective-permute-start(bf16[128,4224]{1,0:T(8,128)(2,1)} %pack.1.refs_0_), channel_id=1, source_target_pairs={{4,8},{5,9},{6,10},{7,11},{8,4},{9,5},{10,6},{11,7},{20,24},{21,25... | collective-permute-start | bytes 3244040 | tf_op jit(solution)/shard_map/ppermute | solution.py:450
  33.3 28.6 %collective-permute-start.5 = (bf16[128,4224]{1,0:T(8,128)(2,1)S(1)}, bf16[128,4224]{1,0:T(8,128)(2,1)S(1)}, u32[]{:S(2)}, u32[]{:S(2)}) collective-permute-start(bf16[128,4224]{1,0:T(8,128)(2,1)S(1)} %collective-permute-done.2.second), channel_id=1, source_target_pairs={{0,4},{1,5},{2,6},{3,7},{4,0},{5,1},{6,2},{7,3},{8,12},{9,13},{10,... | collective-permute-start | bytes 3244040 | tf_op jit(solution)/shard_map/ppermute | solution.py:450
  37.9 25.5 %collective-permute-start.4 = (bf16[128,4224]{1,0:T(8,128)(2,1)S(1)}, bf16[128,4224]{1,0:T(8,128)(2,1)S(1)}, u32[]{:S(2)}, u32[]{:S(2)}) collective-permute-start(bf16[128,4224]{1,0:T(8,128)(2,1)S(1)} %collective-permute-done.1.refs_2_), channel_id=1, source_target_pairs={{0,2},{1,3},{2,0},{3,1},{4,6},{5,7},{6,4},{7,5},{8,10},{9,11},{10,... | collective-permute-start | bytes 3244040 | tf_op jit(solution)/shard_map/ppermute | solution.py:450
  38.4 25.0 %collective-permute-start.6 = (bf16[128,4224]{1,0:T(8,128)(2,1)S(1)}, bf16[128,4224]{1,0:T(8,128)(2,1)S(1)}, u32[]{:S(2)}, u32[]{:S(2)}) collective-permute-start(bf16[128,4224]{1,0:T(8,128)(2,1)S(1)} %collective-permute-done.1.refs_2_), channel_id=1, source_target_pairs={{4,8},{5,9},{6,10},{7,11},{8,4},{9,5},{10,6},{11,7},{20,24},{21,25... | collective-permute-start | bytes 3244040 | tf_op jit(solution)/shard_map/ppermute | solution.py:450
  43.9 29.0 %collective-permute-start.11 = (bf16[272,2304]{1,0:T(8,128)(2,1)S(1)}, bf16[272,2304]{1,0:T(8,128)(2,1)S(1)}, u32[]{:S(2)}, u32[]{:S(2)}) collective-permute-start(bf16[272,2304]{1,0:T(8,128)(2,1)S(1)} %get-tuple-element.152.own), channel_id=1, source_target_pairs={{0,16},{16,0},{1,17},{17,1},{2,18},{18,2},{3,19},{19,3},{4,20},{20... | collective-permute-start | bytes 3760136 | tf_op jit(solution)/shard_map/ppermute | solution.py:463
  63.9 26.4 %collective-permute-start.10 = (bf16[128,4224]{1,0:T(8,128)(2,1)S(1)}, bf16[128,4224]{1,0:T(8,128)(2,1)S(1)}, u32[]{:S(2)}, u32[]{:S(2)}) collective-permute-start(bf16[128,4224]{1,0:T(8,128)(2,1)S(1)} %collective-permute-done.6.second), channel_id=1, source_target_pairs={{0,4},{1,5},{2,6},{3,7},{4,0},{5,1},{6,2},{7,3},{8,12},{9,13},{10,... | collective-permute-start | bytes 3244040 | tf_op jit(solution)/shard_map/ppermute | solution.py:450
  66.3 25.5 %collective-permute-start.9 = (bf16[128,4224]{1,0:T(8,128)(2,1)S(1)}, bf16[128,4224]{1,0:T(8,128)(2,1)S(1)}, u32[]{:S(2)}, u32[]{:S(2)}) collective-permute-start(bf16[128,4224]{1,0:T(8,128)(2,1)S(1)} %choose.2.refs_2_), channel_id=1, source_target_pairs={{0,2},{1,3},{2,0},{3,1},{4,6},{5,7},{6,4},{7,5},{8,10},{9,11},{10,... | collective-permute-start | bytes 3244040 | tf_op jit(solution)/shard_map/ppermute | solution.py:450
  72.9 18.9 %collective-permute-start.14 = (bf16[136,2304]{1,0:T(8,128)(2,1)S(1)}, bf16[136,2304]{1,0:T(8,128)(2,1)S(1)}, u32[]{:S(2)}, u32[]{:S(2)}) collective-permute-start(bf16[136,2304]{1,0:T(8,128)(2,1)S(1)} %get-tuple-element.160.own), channel_id=1, source_target_pairs={{0,16},{16,0},{1,17},{17,1},{2,18},{18,2},{3,19},{19,3},{4,20},{20... | collective-permute-start | bytes 1880072 | tf_op jit(solution)/shard_map/ppermute | solution.py:463
  78.0 13.8 %collective-permute-start.15 = (bf16[128,2176]{1,0:T(8,128)(2,1)S(1)}, bf16[128,2176]{1,0:T(8,128)(2,1)S(1)}, u32[]{:S(2)}, u32[]{:S(2)}) collective-permute-start(bf16[128,2176]{1,0:T(8,128)(2,1)S(1)} %get-tuple-element.167), channel_id=1, source_target_pairs={{0,1},{1,0},{2,3},{3,2},{4,5},{5,4},{6,7},{7,6},{8,9},{9,8},{10,11... | collective-permute-start | bytes 1671176 | tf_op jit(solution)/shard_map/ppermute | solution.py:450
  92.4 16.1 %collective-permute-start.21 = (bf16[136,2304]{1,0:T(8,128)(2,1)S(1)}, bf16[136,2304]{1,0:T(8,128)(2,1)S(1)}, u32[]{:S(2)}, u32[]{:S(2)}) collective-permute-start(bf16[136,2304]{1,0:T(8,128)(2,1)S(1)} %get-tuple-element.174.own), channel_id=1, source_target_pairs={{0,16},{16,0},{1,17},{17,1},{2,18},{18,2},{3,19},{19,3},{4,20},{20... | collective-permute-start | bytes 1880072 | tf_op jit(solution)/shard_map/ppermute | solution.py:463
  93.9 16.1 %collective-permute-start.18 = (bf16[128,2176]{1,0:T(8,128)(2,1)S(1)}, bf16[128,2176]{1,0:T(8,128)(2,1)S(1)}, u32[]{:S(2)}, u32[]{:S(2)}) collective-permute-start(bf16[128,2176]{1,0:T(8,128)(2,1)S(1)} %get-tuple-element.170), channel_id=1, source_target_pairs={{0,2},{1,3},{2,0},{3,1},{4,6},{5,7},{6,4},{7,5},{8,10},{9,11},{10,... | collective-permute-start | bytes 1671176 | tf_op jit(solution)/shard_map/ppermute | solution.py:450
  95.4 24.1 %collective-permute-start.17 = (bf16[128,2048]{1,0:T(8,128)(2,1)S(1)}, bf16[128,2048]{1,0:T(8,128)(2,1)S(1)}, u32[]{:S(2)}, u32[]{:S(2)}) collective-permute-start(bf16[128,2048]{1,0:T(8,128)(2,1)S(1)} %get-tuple-element.169), channel_id=1, source_target_pairs={{0,2},{1,3},{2,0},{3,1},{4,6},{5,7},{6,4},{7,5},{8,10},{9,11},{10,... | collective-permute-start | bytes 1572872 | tf_op jit(solution)/shard_map/ppermute | solution.py:450
  108.5 15.3 %collective-permute-start.23 = (bf16[136,2304]{1,0:T(8,128)(2,1)S(1)}, bf16[136,2304]{1,0:T(8,128)(2,1)S(1)}, u32[]{:S(2)}, u32[]{:S(2)}) collective-permute-start(bf16[136,2304]{1,0:T(8,128)(2,1)S(1)} %get-tuple-element.181.own), channel_id=1, source_target_pairs={{0,16},{16,0},{1,17},{17,1},{2,18},{18,2},{3,19},{19,3},{4,20},{20... | collective-permute-start | bytes 1880072 | tf_op jit(solution)/shard_map/ppermute | solution.py:463
  123.7 14.5 %collective-permute-start.27 = (bf16[136,2304]{1,0:T(8,128)(2,1)S(1)}, bf16[136,2304]{1,0:T(8,128)(2,1)S(1)}, u32[]{:S(2)}, u32[]{:S(2)}) collective-permute-start(bf16[136,2304]{1,0:T(8,128)(2,1)S(1)} %get-tuple-element.189.own), channel_id=1, source_target_pairs={{0,16},{16,0},{1,17},{17,1},{2,18},{18,2},{3,19},{19,3},{4,20},{20... | collective-permute-start | bytes 1880072 | tf_op jit(solution)/shard_map/ppermute | solution.py:463
  138.2 14.4 %collective-permute-start.29 = (bf16[136,2304]{1,0:T(8,128)(2,1)S(1)}, bf16[136,2304]{1,0:T(8,128)(2,1)S(1)}, u32[]{:S(2)}, u32[]{:S(2)}) collective-permute-start(bf16[136,2304]{1,0:T(8,128)(2,1)S(1)} %get-tuple-element.202.own), channel_id=1, source_target_pairs={{0,16},{16,0},{1,17},{17,1},{2,18},{18,2},{3,19},{19,3},{4,20},{20... | collective-permute-start | bytes 1880072 | tf_op jit(solution)/shard_map/ppermute | solution.py:463
  155.0 19.5 %collective-permute-start.39 = (bf16[136,2304]{1,0:T(8,128)(2,1)S(1)}, bf16[136,2304]{1,0:T(8,128)(2,1)S(1)}, u32[]{:S(2)}, u32[]{:S(2)}) collective-permute-start(bf16[136,2304]{1,0:T(8,128)(2,1)S(1)} %get-tuple-element.228.own), channel_id=1, source_target_pairs={{0,16},{16,0},{1,17},{17,1},{2,18},{18,2},{3,19},{19,3},{4,20},{20... | collective-permute-start | bytes 1880072 | tf_op jit(solution)/shard_map/ppermute | solution.py:463
  157.1 14.7 %collective-permute-start.35 = (bf16[128,2176]{1,0:T(8,128)(2,1)S(1)}, bf16[128,2176]{1,0:T(8,128)(2,1)S(1)}, u32[]{:S(2)}, u32[]{:S(2)}) collective-permute-start(bf16[128,2176]{1,0:T(8,128)(2,1)S(1)} %add.17), channel_id=1, source_target_pairs={{0,2},{1,3},{2,0},{3,1},{4,6},{5,7},{6,4},{7,5},{8,10},{9,11},{10,... | collective-permute-start | bytes 1671176 | tf_op jit(solution)/shard_map/ppermute | solution.py:450
  157.8 26.3 %collective-permute-start.37 = (bf16[128,2176]{1,0:T(8,128)(2,1)S(1)}, bf16[128,2176]{1,0:T(8,128)(2,1)S(1)}, u32[]{:S(2)}, u32[]{:S(2)}) collective-permute-start(bf16[128,2176]{1,0:T(8,128)(2,1)S(1)} %add.19), channel_id=1, source_target_pairs={{0,8},{1,9},{2,10},{3,11},{12,4},{13,5},{14,6},{15,7},{16,24},{17,... | collective-permute-start | bytes 1671176 | tf_op jit(solution)/shard_map/ppermute | solution.py:450
  161.6 22.6 %collective-permute-start.38 = (bf16[128,2176]{1,0:T(8,128)(2,1)S(1)}, bf16[128,2176]{1,0:T(8,128)(2,1)S(1)}, u32[]{:S(2)}, u32[]{:S(2)}) collective-permute-start(bf16[128,2176]{1,0:T(8,128)(2,1)S(1)} %add.19), channel_id=1, source_target_pairs={{4,8},{5,9},{6,10},{7,11},{8,4},{9,5},{10,6},{11,7},{20,24},{21,25... | collective-permute-start | bytes 1671176 | tf_op jit(solution)/shard_map/ppermute | solution.py:450
  171.9 13.9 %collective-permute-start.36 = (bf16[128,2176]{1,0:T(8,128)(2,1)S(1)}, bf16[128,2176]{1,0:T(8,128)(2,1)S(1)}, u32[]{:S(2)}, u32[]{:S(2)}) collective-permute-start(bf16[128,2176]{1,0:T(8,128)(2,1)S(1)} %add.18.refs_0_), channel_id=1, source_target_pairs={{0,4},{1,5},{2,6},{3,7},{12,8},{13,9},{14,10},{15,11},{16,20},{17,... | collective-permute-start | bytes 1671176 | tf_op jit(solution)/shard_map/ppermute | solution.py:450
  176.8 23.8 %collective-permute-start.42 = (bf16[128,2176]{1,0:T(8,128)(2,1)S(1)}, bf16[128,2176]{1,0:T(8,128)(2,1)S(1)}, u32[]{:S(2)}, u32[]{:S(2)}) collective-permute-start(bf16[128,2176]{1,0:T(8,128)(2,1)S(1)} %add.13), channel_id=1, source_target_pairs={{0,2},{1,3},{2,0},{3,1},{4,6},{5,7},{6,4},{7,5},{8,10},{9,11},{10,... | collective-permute-start | bytes 1671176 | tf_op jit(solution)/shard_map/ppermute | solution.py:450
  186.0 17.0 %collective-permute-start.41 = (bf16[128,2176]{1,0:T(8,128)(2,1)S(1)}, bf16[128,2176]{1,0:T(8,128)(2,1)S(1)}, u32[]{:S(2)}, u32[]{:S(2)}) collective-permute-start(bf16[128,2176]{1,0:T(8,128)(2,1)S(1)} %add.20), channel_id=1, source_target_pairs={{4,12},{5,13},{6,14},{7,15},{8,0},{9,1},{10,2},{11,3},{20,28},{21,... | collective-permute-start | bytes 1671176 | tf_op jit(solution)/shard_map/ppermute | solution.py:450
  (27 other events, 230.6 us)

commit v7 on v6

--- a/solution.py
+++ b/solution.py
@@ -391,7 +391,7 @@
 def outer(lefts, rights):
     units, width = lefts[0].shape[1], rights[0].shape[1]
     rows = sum(left.shape[0] for left in lefts)
-    tile = 512
+    tile = 1024
     return pl.pallas_call(
         functools.partial(outer_kernel, len(lefts)),
         grid=(width // tile,),
@@ -537,7 +537,7 @@
     rc = across(sumc1)
     rc, sum1 = meet(rc, sum1)
     sumc = add(sumc0, rc)
-    c_edge = outer_z(sumc, part=(0, 3))
+    c_edge = outer_z(sumc)
     r0 = across(sum1)
     y0, _ = meet(y0, sumc)
     ((keep0, send0),), done = backward((state0,), part0, y0)

time: 205 us -> 205 us (level)
  waiting for transfers between devices: 86.8 us -> 89.3 us
    ppermute x36, waiting for transfers between devices: 78.5 us -> 80.9 us  [swap(): return lax.ppermute(value, 'expert', pairs)]
where the time goes in v7:
time: 205 us
  waiting for transfers between devices  89.3 us (44%)
  Pallas kernels  65.2 us (32%)
  starting transfers between devices  41.5 us (20%)
  local copies, waits for them, and re-layouts  6.96 us (3%)
    ppermute x36, waiting for transfers between devices, swap(): return lax.ppermute(value, 'expert', pairs)  80.9 us
    pallas_call x26, Pallas kernels, kernel_call(): pl.pallas_call(body, in_specs=[pl.BlockSpec(memory_space=pltpu.VMEM)] * l...  42.8 us
    ppermute x36, starting transfers between devices, swap(): return lax.ppermute(value, 'expert', pairs)  31.9 us
    pallas_call x3, Pallas kernels, outer(): pl.pallas_call(functools.partial(outer_kernel, len(lefts)), grid=(width /...  19.5 us
    ppermute x7, starting transfers between devices, exchange(): return lax.ppermute(part, 'dp', [(0, 1), (1, 0)])  9.59 us
    ppermute x7, waiting for transfers between devices, exchange(): return lax.ppermute(part, 'dp', [(0, 1), (1, 0)])  8.33 us
    unnamed x16, local copies, waits for them, and re-layouts  6.92 us
  transfers between devices with their start and end apart: 43, of which 18 were waited for; matrix products, arithmetic and copies ran while one was open for 0% of the time, Pallas kernels for 29%

profile of v7, /device:TPU:0, one launch (start us, length us, event | category | flops | bytes accessed | tf_op | source)
XLA Modules:
  0.0 204.6 jit_solution(2981968215235086377)
XLA Ops:
  0.6 2.9 %pack.1.refs_0_ = bf16[128,4224]{1,0:T(8,128)(2,1)} custom-call(bf16[128,2048]{1,0:T(8,128)(2,1)} %tokens.1, bf16[128,2048]{1,0:T(8,128)(2,1)} %cotangent.1, bf16[8,128]{1,0:T(8,128)(2,1)} %bitcast.43, s32[8,128]{1,0:T(8,128)} %bitcast.42), custom_call_target="tpu_custom_call" | custom-call | flops 1000 | bytes 1000 | tf_op jit(solution)/shard_map/pack/pallas_call | solution.py:191
  4.1 2.6 %collective-permute-start = (bf16[128,4224]{1,0:T(8,128)(2,1)}, bf16[128,4224]{1,0:T(8,128)(2,1)S(1)}, u32[]{:S(2)}, u32[]{:S(2)}) collective-permute-start(bf16[128,4224]{1,0:T(8,128)(2,1)} %pack.1.refs_0_), channel_id=1, source_target_pairs={{0,2},{1,3},{2,0},{3,1},{4,6},{5,7},{6,4},{7,5},{8,10},{9,11},{10,... | collective-permute-start | bytes 3244040 | tf_op jit(solution)/shard_map/ppermute | solution.py:450
  15.9 4.3 %front.5 = (bf16[144,2048]{1,0:T(8,128)(2,1)S(1)}, bf16[144,2048]{1,0:T(8,128)(2,1)S(1)}, bf16[256,144]{1,0:T(8,128)(2,1)S(1)}, f32[144,128]{1,0:T(8,128)S(1)}, bf16[136,2304]{1,0:T(8,128)(2,1)S(1)}) custom-call(bf16[128,4224]{1,0:T(8,128)(2,1)S(1)} %copy-done.6, bf16[128,4224]{1,0:T(8,128)(2,1)S(1)} %collective-permute-done.3.refs_1_, ...), custom_call_target="tpu_custom_call" | custom-call | flops 1000 | bytes 1000 | tf_op jit(solution)/shard_map/front/pallas_call | solution.py:117
  20.1 11.2 %collective-permute-done.refs_0_ = bf16[128,4224]{1,0:T(8,128)(2,1)S(1)} collective-permute-done((bf16[128,4224]{1,0:T(8,128)(2,1)}, bf16[128,4224]{1,0:T(8,128)(2,1)S(1)}, u32[]{:S(2)}, u32[]{:S(2)}) %collective-permute-start) | collective-permute-done | bytes 1081376 | tf_op jit(solution)/shard_map/ppermute | solution.py:450
  33.3 4.6 %collective-permute-start.5 = (bf16[128,4224]{1,0:T(8,128)(2,1)S(1)}, bf16[128,4224]{1,0:T(8,128)(2,1)S(1)}, u32[]{:S(2)}, u32[]{:S(2)}) collective-permute-start(bf16[128,4224]{1,0:T(8,128)(2,1)S(1)} %collective-permute-done.2.second), channel_id=1, source_target_pairs={{0,4},{1,5},{2,6},{3,7},{4,0},{5,1},{6,2},{7,3},{8,12},{9,13},{10,... | collective-permute-start | bytes 3244040 | tf_op jit(solution)/shard_map/ppermute | solution.py:450
  39.2 4.7 %front.6 = (bf16[144,2048]{1,0:T(8,128)(2,1)S(1)}, bf16[144,2048]{1,0:T(8,128)(2,1)S(1)}, bf16[256,144]{1,0:T(8,128)(2,1)S(1)}, f32[144,128]{1,0:T(8,128)S(1)}, ...) custom-call(bf16[128,4224]{1,0:T(8,128)(2,1)S(1)} %collective-permut, ...), custom_call_target="tpu_custom_call" | custom-call | flops 1000 | bytes 1000 | tf_op jit(solution)/shard_map/front/pallas_call | solution.py:117
  45.5 16.4 %collective-permute-done.5.first = bf16[128,4224]{1,0:T(8,128)(2,1)S(1)} collective-permute-done((bf16[128,4224]{1,0:T(8,128)(2,1)S(1)}, bf16[128,4224]{1,0:T(8,128)(2,1)S(1)}, u32[]{:S(2)}, u32[]{:S(2)}) %collective-permute-start.5) | collective-permute-done | bytes 1081376 | tf_op jit(solution)/shard_map/ppermute | solution.py:450
  63.9 2.4 %collective-permute-start.10 = (bf16[128,4224]{1,0:T(8,128)(2,1)S(1)}, bf16[128,4224]{1,0:T(8,128)(2,1)S(1)}, u32[]{:S(2)}, u32[]{:S(2)}) collective-permute-start(bf16[128,4224]{1,0:T(8,128)(2,1)S(1)} %collective-permute-done.6.second), channel_id=1, source_target_pairs={{0,4},{1,5},{2,6},{3,7},{4,0},{5,1},{6,2},{7,3},{8,12},{9,13},{10,... | collective-permute-start | bytes 3244040 | tf_op jit(solution)/shard_map/ppermute | solution.py:450
  67.8 4.7 %front.7 = (bf16[144,2048]{1,0:T(8,128)(2,1)S(1)}, bf16[144,2048]{1,0:T(8,128)(2,1)S(1)}, bf16[256,144]{1,0:T(8,128)(2,1)S(1)}, f32[144,128]{1,0:T(8,128)S(1)}, ...) custom-call(bf16[128,4224]{1,0:T(8,128)(2,1)S(1)} %collective-permut, ...), custom_call_target="tpu_custom_call" | custom-call | flops 1000 | bytes 1000 | tf_op jit(solution)/shard_map/front/pallas_call | solution.py:117
  74.4 3.7 %back.7 = (bf16[288,768]{1,0:T(8,128)(2,1)S(1)}, bf16[288,768]{1,0:T(8,128)(2,1)S(1)}, bf16[288,768]{1,0:T(8,128)(2,1)S(1)}, bf16[128,2176]{1,0:T(8,128)(2,1)S(1...) custom-call(bf16[272,2304]{1,0:T(8,128)(2,1)S(1)} %get-tuple-element.152.own, ...), custom_call_target="tpu_custom_call" | custom-call | flops 1000 | bytes 1000 | tf_op jit(solution)/shard_map/back/pallas_call | solution.py:117
  78.6 11.7 %collective-permute-done.10.first = bf16[128,4224]{1,0:T(8,128)(2,1)S(1)} collective-permute-done((bf16[128,4224]{1,0:T(8,128)(2,1)S(1)}, bf16[128,4224]{1,0:T(8,128)(2,1)S(1)}, u32[]{:S(2)}, u32[]{:S(2)}) %collective-permute-start.10) | collective-permute-done | bytes 1081376 | tf_op jit(solution)/shard_map/ppermute | solution.py:450
  98.2 4.7 %front.8 = (bf16[144,2048]{1,0:T(8,128)(2,1)S(1)}, bf16[144,2048]{1,0:T(8,128)(2,1)S(1)}, bf16[256,144]{1,0:T(8,128)(2,1)S(1)}, f32[144,128]{1,0:T(8,128)S(1)}, ...) custom-call(bf16[128,4224]{1,0:T(8,128)(2,1)S(1)} %collective-permut, ...), custom_call_target="tpu_custom_call" | custom-call | flops 1000 | bytes 1000 | tf_op jit(solution)/shard_map/front/pallas_call | solution.py:117
  102.9 5.6 %collective-permute-done.21.peer = bf16[136,2304]{1,0:T(8,128)(2,1)S(1)} collective-permute-done((bf16[136,2304]{1,0:T(8,128)(2,1)S(1)}, bf16[136,2304]{1,0:T(8,128)(2,1)S(1)}, u32[]{:S(2)}, u32[]{:S(2)}) %collective-permute-start.21) | collective-permute-done | bytes 626720 | tf_op jit(solution)/shard_map/ppermute | solution.py:463
  112.8 6.6 %collective-permute-done.17.refs_0_ = bf16[128,2048]{1,0:T(8,128)(2,1)S(1)} collective-permute-done((bf16[128,2048]{1,0:T(8,128)(2,1)S(1)}, bf16[128,2048]{1,0:T(8,128)(2,1)S(1)}, u32[]{:S(2)}, u32[]{:S(2)}) %collective-permute-start.17) | collective-permute-done | bytes 524320 | tf_op jit(solution)/shard_map/ppermute | solution.py:450
  121.4 2.4 %collective-permute-done.23.peer = bf16[136,2304]{1,0:T(8,128)(2,1)S(1)} collective-permute-done((bf16[136,2304]{1,0:T(8,128)(2,1)S(1)}, bf16[136,2304]{1,0:T(8,128)(2,1)S(1)}, u32[]{:S(2)}, u32[]{:S(2)}) %collective-permute-start.23) | collective-permute-done | bytes 626720 | tf_op jit(solution)/shard_map/ppermute | solution.py:463
  129.6 4.3 %front.9 = (bf16[144,2048]{1,0:T(8,128)(2,1)S(1)}, bf16[144,2048]{1,0:T(8,128)(2,1)S(1)}, bf16[256,144]{1,0:T(8,128)(2,1)S(1)}, f32[144,128]{1,0:T(8,128)S(1)}, bf16[136,2304]{1,0:T(8,128)(2,1)S(1)}) custom-call(bf16[128,2048]{1,0:T(8,128)(2,1)S(1)} %collective-permute-done.17.refs_0_, bf16[128,2176]{1,0:T(8,128)(2,1)S(1)} %collective-permute-done.18.refs_1_, ...), custom_call_target="tpu_custom_call" | custom-call | flops 1000 | bytes 1000 | tf_op jit(solution)/shard_map/front/pallas_call | solution.py:117
  133.9 4.2 %collective-permute-done.28.refs_2_ = bf16[128,2176]{1,0:T(8,128)(2,1)S(1)} collective-permute-done((bf16[128,2176]{1,0:T(8,128)(2,1)S(1)}, bf16[128,2176]{1,0:T(8,128)(2,1)S(1)}, u32[]{:S(2)}, u32[]{:S(2)}) %collective-permute-start.28) | collective-permute-done | bytes 557088 | tf_op jit(solution)/shard_map/ppermute | solution.py:450
  144.2 7.3 %collective-permute-done.31.refs_1_ = bf16[128,2176]{1,0:T(8,128)(2,1)S(1)} collective-permute-done((bf16[128,2176]{1,0:T(8,128)(2,1)S(1)}, bf16[128,2176]{1,0:T(8,128)(2,1)S(1)}, u32[]{:S(2)}, u32[]{:S(2)}) %collective-permute-start.31) | collective-permute-done | bytes 557088 | tf_op jit(solution)/shard_map/ppermute | solution.py:450
  157.8 3.7 %collective-permute-start.37 = (bf16[128,2176]{1,0:T(8,128)(2,1)S(1)}, bf16[128,2176]{1,0:T(8,128)(2,1)S(1)}, u32[]{:S(2)}, u32[]{:S(2)}) collective-permute-start(bf16[128,2176]{1,0:T(8,128)(2,1)S(1)} %add.19), channel_id=1, source_target_pairs={{0,8},{1,9},{2,10},{3,11},{12,4},{13,5},{14,6},{15,7},{16,24},{17,... | collective-permute-start | bytes 1671176 | tf_op jit(solution)/shard_map/ppermute | solution.py:450
  162.6 9.2 %collective-permute-done.35.refs_1_ = bf16[128,2176]{1,0:T(8,128)(2,1)S(1)} collective-permute-done((bf16[128,2176]{1,0:T(8,128)(2,1)S(1)}, bf16[128,2176]{1,0:T(8,128)(2,1)S(1)}, u32[]{:S(2)}, u32[]{:S(2)}) %collective-permute-start.35) | collective-permute-done | bytes 557088 | tf_op jit(solution)/shard_map/ppermute | solution.py:450
  175.5 6.5 %outer.3 = bf16[768,2048]{1,0:T(8,128)(2,1)} custom-call(bf16[288,768]{1,0:T(8,128)(2,1)S(1)} %get-tuple-element.222.refs_0_, bf16[144,768]{1,0:T(8,128)(2,1)S(1)} %get-tuple-element.223.refs_1_, bf16[144,768]{1,0:T(8,128)(2,1)S(1)} %get-tuple-element.224.refs_2_, bf16[144,768]{1,0:T(8,128)(2,1)S(1)} %get-tuple-element.225.refs_3_, ...), custom_call_target="tpu_custom_call" | custom-call | flops 1000 | bytes 1000 | tf_op jit(solution)/shard_map/outer/pallas_call | solution.py:395
  182.0 3.8 %collective-permute-done.36.refs_1_ = bf16[128,2176]{1,0:T(8,128)(2,1)S(1)} collective-permute-done((bf16[128,2176]{1,0:T(8,128)(2,1)S(1)}, bf16[128,2176]{1,0:T(8,128)(2,1)S(1)}, u32[]{:S(2)}, u32[]{:S(2)}) %collective-permute-start.36) | collective-permute-done | bytes 557088 | tf_op jit(solution)/shard_map/ppermute | solution.py:450
  187.3 6.5 %outer.4 = bf16[768,2048]{1,0:T(8,128)(2,1)} custom-call(bf16[288,768]{1,0:T(8,128)(2,1)S(1)} %get-tuple-element.261.refs_0_, bf16[144,768]{1,0:T(8,128)(2,1)S(1)} %get-tuple-element.262.refs_1_, bf16[144,768]{1,0:T(8,128)(2,1)S(1)} %get-tuple-element.263.refs_2_, bf16[144,768]{1,0:T(8,128)(2,1)S(1)} %get-tuple-element.264.refs_3_, ...), custom_call_target="tpu_custom_call" | custom-call | flops 1000 | bytes 1000 | tf_op jit(solution)/shard_map/outer/pallas_call | solution.py:395
  193.8 6.5 %outer.5 = bf16[768,2048]{1,0:T(8,128)(2,1)} custom-call(bf16[288,768]{1,0:T(8,128)(2,1)S(1)} %get-tuple-element.268.refs_0_, bf16[144,768]{1,0:T(8,128)(2,1)S(1)} %get-tuple-element.269.refs_1_, bf16[144,768]{1,0:T(8,128)(2,1)S(1)} %get-tuple-element.270.refs_2_, bf16[144,768]{1,0:T(8,128)(2,1)S(1)} %get-tuple-element.271.refs_3_, ...), custom_call_target="tpu_custom_call" | custom-call | flops 1000 | bytes 1000 | tf_op jit(solution)/shard_map/outer/pallas_call | solution.py:395
  (110 shorter events, 63.3 us)
Async XLA Ops:
  4.1 27.2 %collective-permute-start = (bf16[128,4224]{1,0:T(8,128)(2,1)}, bf16[128,4224]{1,0:T(8,128)(2,1)S(1)}, u32[]{:S(2)}, u32[]{:S(2)}) collective-permute-start(bf16[128,4224]{1,0:T(8,128)(2,1)} %pack.1.refs_0_), channel_id=1, source_target_pairs={{0,2},{1,3},{2,0},{3,1},{4,6},{5,7},{6,4},{7,5},{8,10},{9,11},{10,... | collective-permute-start | bytes 3244040 | tf_op jit(solution)/shard_map/ppermute | solution.py:450
  6.6 26.1 %collective-permute-start.1 = (bf16[128,4224]{1,0:T(8,128)(2,1)}, bf16[128,4224]{1,0:T(8,128)(2,1)S(1)}, u32[]{:S(2)}, u32[]{:S(2)}) collective-permute-start(bf16[128,4224]{1,0:T(8,128)(2,1)} %pack.1.refs_0_), channel_id=1, source_target_pairs={{0,4},{1,5},{2,6},{3,7},{4,0},{5,1},{6,2},{7,3},{8,12},{9,13},{10,... | collective-permute-start | bytes 3244040 | tf_op jit(solution)/shard_map/ppermute | solution.py:450
  8.2 24.6 %collective-permute-start.2 = (bf16[128,4224]{1,0:T(8,128)(2,1)}, bf16[128,4224]{1,0:T(8,128)(2,1)S(1)}, u32[]{:S(2)}, u32[]{:S(2)}) collective-permute-start(bf16[128,4224]{1,0:T(8,128)(2,1)} %pack.1.refs_0_), channel_id=1, source_target_pairs={{4,8},{5,9},{6,10},{7,11},{8,4},{9,5},{10,6},{11,7},{20,24},{21,25... | collective-permute-start | bytes 3244040 | tf_op jit(solution)/shard_map/ppermute | solution.py:450
  33.3 28.6 %collective-permute-start.5 = (bf16[128,4224]{1,0:T(8,128)(2,1)S(1)}, bf16[128,4224]{1,0:T(8,128)(2,1)S(1)}, u32[]{:S(2)}, u32[]{:S(2)}) collective-permute-start(bf16[128,4224]{1,0:T(8,128)(2,1)S(1)} %collective-permute-done.2.second), channel_id=1, source_target_pairs={{0,4},{1,5},{2,6},{3,7},{4,0},{5,1},{6,2},{7,3},{8,12},{9,13},{10,... | collective-permute-start | bytes 3244040 | tf_op jit(solution)/shard_map/ppermute | solution.py:450
  37.9 25.5 %collective-permute-start.4 = (bf16[128,4224]{1,0:T(8,128)(2,1)S(1)}, bf16[128,4224]{1,0:T(8,128)(2,1)S(1)}, u32[]{:S(2)}, u32[]{:S(2)}) collective-permute-start(bf16[128,4224]{1,0:T(8,128)(2,1)S(1)} %collective-permute-done.1.refs_2_), channel_id=1, source_target_pairs={{0,2},{1,3},{2,0},{3,1},{4,6},{5,7},{6,4},{7,5},{8,10},{9,11},{10,... | collective-permute-start | bytes 3244040 | tf_op jit(solution)/shard_map/ppermute | solution.py:450
  38.4 25.0 %collective-permute-start.6 = (bf16[128,4224]{1,0:T(8,128)(2,1)S(1)}, bf16[128,4224]{1,0:T(8,128)(2,1)S(1)}, u32[]{:S(2)}, u32[]{:S(2)}) collective-permute-start(bf16[128,4224]{1,0:T(8,128)(2,1)S(1)} %collective-permute-done.1.refs_2_), channel_id=1, source_target_pairs={{4,8},{5,9},{6,10},{7,11},{8,4},{9,5},{10,6},{11,7},{20,24},{21,25... | collective-permute-start | bytes 3244040 | tf_op jit(solution)/shard_map/ppermute | solution.py:450
  43.9 29.0 %collective-permute-start.11 = (bf16[272,2304]{1,0:T(8,128)(2,1)S(1)}, bf16[272,2304]{1,0:T(8,128)(2,1)S(1)}, u32[]{:S(2)}, u32[]{:S(2)}) collective-permute-start(bf16[272,2304]{1,0:T(8,128)(2,1)S(1)} %get-tuple-element.152.own), channel_id=1, source_target_pairs={{0,16},{16,0},{1,17},{17,1},{2,18},{18,2},{3,19},{19,3},{4,20},{20... | collective-permute-start | bytes 3760136 | tf_op jit(solution)/shard_map/ppermute | solution.py:463
  63.9 26.4 %collective-permute-start.10 = (bf16[128,4224]{1,0:T(8,128)(2,1)S(1)}, bf16[128,4224]{1,0:T(8,128)(2,1)S(1)}, u32[]{:S(2)}, u32[]{:S(2)}) collective-permute-start(bf16[128,4224]{1,0:T(8,128)(2,1)S(1)} %collective-permute-done.6.second), channel_id=1, source_target_pairs={{0,4},{1,5},{2,6},{3,7},{4,0},{5,1},{6,2},{7,3},{8,12},{9,13},{10,... | collective-permute-start | bytes 3244040 | tf_op jit(solution)/shard_map/ppermute | solution.py:450
  66.3 25.5 %collective-permute-start.9 = (bf16[128,4224]{1,0:T(8,128)(2,1)S(1)}, bf16[128,4224]{1,0:T(8,128)(2,1)S(1)}, u32[]{:S(2)}, u32[]{:S(2)}) collective-permute-start(bf16[128,4224]{1,0:T(8,128)(2,1)S(1)} %choose.2.refs_2_), channel_id=1, source_target_pairs={{0,2},{1,3},{2,0},{3,1},{4,6},{5,7},{6,4},{7,5},{8,10},{9,11},{10,... | collective-permute-start | bytes 3244040 | tf_op jit(solution)/shard_map/ppermute | solution.py:450
  72.9 18.9 %collective-permute-start.14 = (bf16[136,2304]{1,0:T(8,128)(2,1)S(1)}, bf16[136,2304]{1,0:T(8,128)(2,1)S(1)}, u32[]{:S(2)}, u32[]{:S(2)}) collective-permute-start(bf16[136,2304]{1,0:T(8,128)(2,1)S(1)} %get-tuple-element.160.own), channel_id=1, source_target_pairs={{0,16},{16,0},{1,17},{17,1},{2,18},{18,2},{3,19},{19,3},{4,20},{20... | collective-permute-start | bytes 1880072 | tf_op jit(solution)/shard_map/ppermute | solution.py:463
  78.0 13.8 %collective-permute-start.15 = (bf16[128,2176]{1,0:T(8,128)(2,1)S(1)}, bf16[128,2176]{1,0:T(8,128)(2,1)S(1)}, u32[]{:S(2)}, u32[]{:S(2)}) collective-permute-start(bf16[128,2176]{1,0:T(8,128)(2,1)S(1)} %get-tuple-element.167), channel_id=1, source_target_pairs={{0,1},{1,0},{2,3},{3,2},{4,5},{5,4},{6,7},{7,6},{8,9},{9,8},{10,11... | collective-permute-start | bytes 1671176 | tf_op jit(solution)/shard_map/ppermute | solution.py:450
  92.4 16.1 %collective-permute-start.21 = (bf16[136,2304]{1,0:T(8,128)(2,1)S(1)}, bf16[136,2304]{1,0:T(8,128)(2,1)S(1)}, u32[]{:S(2)}, u32[]{:S(2)}) collective-permute-start(bf16[136,2304]{1,0:T(8,128)(2,1)S(1)} %get-tuple-element.174.own), channel_id=1, source_target_pairs={{0,16},{16,0},{1,17},{17,1},{2,18},{18,2},{3,19},{19,3},{4,20},{20... | collective-permute-start | bytes 1880072 | tf_op jit(solution)/shard_map/ppermute | solution.py:463
  93.9 16.1 %collective-permute-start.18 = (bf16[128,2176]{1,0:T(8,128)(2,1)S(1)}, bf16[128,2176]{1,0:T(8,128)(2,1)S(1)}, u32[]{:S(2)}, u32[]{:S(2)}) collective-permute-start(bf16[128,2176]{1,0:T(8,128)(2,1)S(1)} %get-tuple-element.170), channel_id=1, source_target_pairs={{0,2},{1,3},{2,0},{3,1},{4,6},{5,7},{6,4},{7,5},{8,10},{9,11},{10,... | collective-permute-start | bytes 1671176 | tf_op jit(solution)/shard_map/ppermute | solution.py:450
  95.4 24.1 %collective-permute-start.17 = (bf16[128,2048]{1,0:T(8,128)(2,1)S(1)}, bf16[128,2048]{1,0:T(8,128)(2,1)S(1)}, u32[]{:S(2)}, u32[]{:S(2)}) collective-permute-start(bf16[128,2048]{1,0:T(8,128)(2,1)S(1)} %get-tuple-element.169), channel_id=1, source_target_pairs={{0,2},{1,3},{2,0},{3,1},{4,6},{5,7},{6,4},{7,5},{8,10},{9,11},{10,... | collective-permute-start | bytes 1572872 | tf_op jit(solution)/shard_map/ppermute | solution.py:450
  108.5 15.3 %collective-permute-start.23 = (bf16[136,2304]{1,0:T(8,128)(2,1)S(1)}, bf16[136,2304]{1,0:T(8,128)(2,1)S(1)}, u32[]{:S(2)}, u32[]{:S(2)}) collective-permute-start(bf16[136,2304]{1,0:T(8,128)(2,1)S(1)} %get-tuple-element.181.own), channel_id=1, source_target_pairs={{0,16},{16,0},{1,17},{17,1},{2,18},{18,2},{3,19},{19,3},{4,20},{20... | collective-permute-start | bytes 1880072 | tf_op jit(solution)/shard_map/ppermute | solution.py:463
  123.7 14.5 %collective-permute-start.27 = (bf16[136,2304]{1,0:T(8,128)(2,1)S(1)}, bf16[136,2304]{1,0:T(8,128)(2,1)S(1)}, u32[]{:S(2)}, u32[]{:S(2)}) collective-permute-start(bf16[136,2304]{1,0:T(8,128)(2,1)S(1)} %get-tuple-element.189.own), channel_id=1, source_target_pairs={{0,16},{16,0},{1,17},{17,1},{2,18},{18,2},{3,19},{19,3},{4,20},{20... | collective-permute-start | bytes 1880072 | tf_op jit(solution)/shard_map/ppermute | solution.py:463
  138.2 14.4 %collective-permute-start.29 = (bf16[136,2304]{1,0:T(8,128)(2,1)S(1)}, bf16[136,2304]{1,0:T(8,128)(2,1)S(1)}, u32[]{:S(2)}, u32[]{:S(2)}) collective-permute-start(bf16[136,2304]{1,0:T(8,128)(2,1)S(1)} %get-tuple-element.202.own), channel_id=1, source_target_pairs={{0,16},{16,0},{1,17},{17,1},{2,18},{18,2},{3,19},{19,3},{4,20},{20... | collective-permute-start | bytes 1880072 | tf_op jit(solution)/shard_map/ppermute | solution.py:463
  155.0 17.6 %collective-permute-start.39 = (bf16[136,2304]{1,0:T(8,128)(2,1)S(1)}, bf16[136,2304]{1,0:T(8,128)(2,1)S(1)}, u32[]{:S(2)}, u32[]{:S(2)}) collective-permute-start(bf16[136,2304]{1,0:T(8,128)(2,1)S(1)} %get-tuple-element.228.own), channel_id=1, source_target_pairs={{0,16},{16,0},{1,17},{17,1},{2,18},{18,2},{3,19},{19,3},{4,20},{20... | collective-permute-start | bytes 1880072 | tf_op jit(solution)/shard_map/ppermute | solution.py:463
  157.1 14.7 %collective-permute-start.35 = (bf16[128,2176]{1,0:T(8,128)(2,1)S(1)}, bf16[128,2176]{1,0:T(8,128)(2,1)S(1)}, u32[]{:S(2)}, u32[]{:S(2)}) collective-permute-start(bf16[128,2176]{1,0:T(8,128)(2,1)S(1)} %add.17), channel_id=1, source_target_pairs={{0,2},{1,3},{2,0},{3,1},{4,6},{5,7},{6,4},{7,5},{8,10},{9,11},{10,... | collective-permute-start | bytes 1671176 | tf_op jit(solution)/shard_map/ppermute | solution.py:450
  157.8 24.2 %collective-permute-start.37 = (bf16[128,2176]{1,0:T(8,128)(2,1)S(1)}, bf16[128,2176]{1,0:T(8,128)(2,1)S(1)}, u32[]{:S(2)}, u32[]{:S(2)}) collective-permute-start(bf16[128,2176]{1,0:T(8,128)(2,1)S(1)} %add.19), channel_id=1, source_target_pairs={{0,8},{1,9},{2,10},{3,11},{12,4},{13,5},{14,6},{15,7},{16,24},{17,... | collective-permute-start | bytes 1671176 | tf_op jit(solution)/shard_map/ppermute | solution.py:450
  161.6 20.5 %collective-permute-start.38 = (bf16[128,2176]{1,0:T(8,128)(2,1)S(1)}, bf16[128,2176]{1,0:T(8,128)(2,1)S(1)}, u32[]{:S(2)}, u32[]{:S(2)}) collective-permute-start(bf16[128,2176]{1,0:T(8,128)(2,1)S(1)} %add.19), channel_id=1, source_target_pairs={{4,8},{5,9},{6,10},{7,11},{8,4},{9,5},{10,6},{11,7},{20,24},{21,25... | collective-permute-start | bytes 1671176 | tf_op jit(solution)/shard_map/ppermute | solution.py:450
  171.9 13.9 %collective-permute-start.36 = (bf16[128,2176]{1,0:T(8,128)(2,1)S(1)}, bf16[128,2176]{1,0:T(8,128)(2,1)S(1)}, u32[]{:S(2)}, u32[]{:S(2)}) collective-permute-start(bf16[128,2176]{1,0:T(8,128)(2,1)S(1)} %add.18.refs_0_), channel_id=1, source_target_pairs={{0,4},{1,5},{2,6},{3,7},{4,0},{5,1},{6,2},{7,3},{8,12},{9,13},{10,... | collective-permute-start | bytes 1671176 | tf_op jit(solution)/shard_map/ppermute | solution.py:450
  174.9 25.3 %collective-permute-start.42 = (bf16[128,2176]{1,0:T(8,128)(2,1)S(1)}, bf16[128,2176]{1,0:T(8,128)(2,1)S(1)}, u32[]{:S(2)}, u32[]{:S(2)}) collective-permute-start(bf16[128,2176]{1,0:T(8,128)(2,1)S(1)} %add.13), channel_id=1, source_target_pairs={{0,2},{1,3},{2,0},{3,1},{4,6},{5,7},{6,4},{7,5},{8,10},{9,11},{10,... | collective-permute-start | bytes 1671176 | tf_op jit(solution)/shard_map/ppermute | solution.py:450
  186.0 17.0 %collective-permute-start.41 = (bf16[128,2176]{1,0:T(8,128)(2,1)S(1)}, bf16[128,2176]{1,0:T(8,128)(2,1)S(1)}, u32[]{:S(2)}, u32[]{:S(2)}) collective-permute-start(bf16[128,2176]{1,0:T(8,128)(2,1)S(1)} %add.20), channel_id=1, source_target_pairs={{4,12},{5,13},{6,14},{7,15},{8,0},{9,1},{10,2},{11,3},{20,28},{21,... | collective-permute-start | bytes 1671176 | tf_op jit(solution)/shard_map/ppermute | solution.py:450
  (27 other events, 232.9 us)
